TPU v7x, 256 devices: a whole 4x4x8 slice. The times are simulated.
256 devices in a mesh: row: 32 (over x, z), col: 8 (over y, core).
Axes of the slice: x: 4, y: 4, z: 8, core: 2. Of those that a mesh axis runs over, the one named last changes fastest.
Arguments:
- front: float32 [2, 32, 256, 8, 8, 256], P(None, 'row', None, None, 'col'), as said below
- pattern: int32 [2, 32, 8, 8], P(None, 'row', None, 'col'), may hold values from 0 to 1, as said below
Outputs:
- factored: float32 [2, 32, 256, 8, 8, 256], P(None, 'row', None, None, 'col')
Inputs may be any that keep to these rules, and one draw needn't show every extreme that they name: pattern is symmetric in blocks; block pairs at most two apart (the diagonal included) are always 1; for every k < 2, taken in order, block (i, j) with i > k and j > k is 1 wherever blocks (i, k) and (j, k) are both 1. front is symmetric and positive definite.
All inputs are finite; a program needn't handle non-finite values.
Results may differ from a plain program's by a relative error of at most 0.0001.
Values sent between devices are 32-bit elements; how exact they have to be, the bound alone decides.
No kernel may reach another device: no remote copies, remote signals or barrier semaphores. Data moves between devices by JAX's collectives and lax.ppermute only.
A program may use at most 64 MiB of HBM per device.

v0:
```python
import jax
import jax.numpy as jnp
from jax import lax
from jax.sharding import PartitionSpec as P

PANELS = 2


HIGHEST = lax.Precision.HIGHEST


def broadcast(block, axis, owner):
    block = jnp.where(lax.axis_index(axis) == owner, block, jnp.zeros_like(block))
    return lax.psum(block, axis)


def lower_inverse(pivot_block):
    factor = jnp.linalg.cholesky(pivot_block)
    identity = jnp.eye(pivot_block.shape[0], dtype=jnp.float32)
    inverse = jax.scipy.linalg.solve_triangular(factor, identity, lower=True)
    return (factor, inverse)


def solve_rows(blocks, inverse):
    count = blocks.shape[0]
    block_width = blocks.shape[1]
    flattened = blocks.reshape(count * block_width, block_width)
    product = lax.dot_general(
        flattened,
        inverse,
        (((1,), (1,)), ((), ())),
        precision=HIGHEST,
        preferred_element_type=jnp.float32,
    )
    return product.reshape(count, block_width, block_width)


def update_slots(working, panel_block, mirror, allowed_now, first_slot, last_slot):
    row_blocks = panel_block.shape[0]
    block_width = panel_block.shape[1]
    slot_count = last_slot - first_slot
    left_side = panel_block.reshape(row_blocks * block_width, block_width)
    right_side = mirror.reshape(slot_count * block_width, block_width)
    product = lax.dot_general(
        left_side,
        right_side,
        (((1,), (1,)), ((), ())),
        precision=HIGHEST,
        preferred_element_type=jnp.float32,
    )
    product = product.reshape(row_blocks, block_width, slot_count, block_width)
    selected = allowed_now[:, None, :, None]
    return working.at[:, :, first_slot:last_slot, :].add(jnp.where(selected, -product, 0.0))


def on_device(front, pattern):
    row_blocks, _, block_width, col_blocks, _, _ = front.shape
    rows_size = lax.axis_size("row")
    cols_size = lax.axis_size("col")
    fold_count = rows_size // cols_size
    row_place = lax.axis_index("row")
    col_place = lax.axis_index("col")
    present = pattern.reshape(row_blocks, col_blocks) > 0
    working = jnp.where(
        present[:, None, :, None],
        front.reshape(row_blocks, block_width, col_blocks, block_width),
        0.0,
    )
    global_rows = jnp.arange(row_blocks, dtype=jnp.int32) * rows_size + row_place
    global_cols = jnp.arange(col_blocks, dtype=jnp.int32) * cols_size + col_place
    for column in range(PANELS):
        owner_row = column % rows_size
        slot_row = column // rows_size
        owner_col = column % cols_size
        slot_col = column // cols_size
        column_blocks = working[:, :, slot_col, :]
        factor_factor, factor_inverse = lower_inverse(column_blocks[slot_row])
        paired = broadcast(jnp.stack((factor_factor, factor_inverse)), "row", owner_row)
        finish_panel_block = solve_rows(column_blocks, paired[1])
        finish_panel_block = jnp.where(
            (global_rows == column)[:, None, None], paired[0][None], finish_panel_block
        )
        factor_panel_block = jnp.where(
            (global_rows < column)[:, None, None], 0.0, finish_panel_block
        )
        factor_panel_block = broadcast(factor_panel_block, "col", owner_col)
        pieces = [
            broadcast(factor_panel_block, "row", turn_index * cols_size + col_place)
            for turn_index in range(fold_count)
        ]
        factor_mirror = jnp.stack(pieces, 1).reshape(col_blocks, block_width, block_width)
        place_working = working
        column_select = (global_cols == column)[None, None, :, None] & (global_rows >= column)[
            :, None, None, None
        ]
        place_working = jnp.where(column_select, factor_panel_block[:, :, None, :], place_working)
        row_select = (global_rows == column)[:, None, None, None] & (global_cols > column)[
            None, None, :, None
        ]
        working = jnp.where(
            row_select, jnp.transpose(factor_mirror, (2, 0, 1))[None], place_working
        )
        working = update_slots(
            working,
            factor_panel_block,
            factor_mirror,
            present & (global_rows > column)[:, None] & (global_cols > column)[None, :],
            0,
            col_blocks,
        )
    return working.reshape(row_blocks, 1, block_width, col_blocks, 1, block_width)


def solution(mesh):
    placed = (P(None, "row", None, None, "col", None), P(None, "row", None, "col"))
    return jax.shard_map(
        on_device,
        mesh=mesh,
        in_specs=placed,
        out_specs=P(None, "row", None, None, "col", None),
        check_vma=False,
    )
```

profile of v0, /device:TPU:1, one launch (start us, length us, event | category | flops | bytes accessed | tf_op | source)
XLA Modules:
  0.0 934.0 jit_solution(5836452525593861651)
XLA Ops:
  6.6 10.9 %copy.15 = f32[2,1,256,8,1,256]{2,5,3,0,4,1:T(8,128)} copy(f32[2,1,256,8,1,256]{5,4,3,2,1,0:T(1,128)} %param.13) | data formatting | bytes 8388608 | tf_op args[0]
  17.5 0.7 and_and_fusion
  18.2 2.8 bitcast_select_fusion
  21.0 1.9 copy-done.1
  23.1 1.0 fusion.10
  24.1 11.7 %cholesky.130 = f32[128,128]{1,0:T(8,128)S(1)} custom-call(f32[128,128]{1,0:T(8,128)S(1)} %cholesky.194), custom_call_target="Cholesky" | custom-call | tf_op jit(solution)/shard_map/jit(cholesky)/cholesky | solution.py:18
  35.9 9.8 %custom-call.13 = f32[1,128,128]{1,2,0:T(8,128)S(1)} custom-call(f32[1,128,128]{2,1,0:T(8,128)S(1)} %get-tuple-element.110), custom_call_target="InvertDiagBlocksLowerTriangular" | custom-call | tf_op jit(solution)/shard_map/jit(cholesky)/cholesky | solution.py:18
  45.7 0.2 constant_dynamic-update-slice_fusion.3
  45.9 0.3 convolution_subtract_fusion.3
  46.2 11.7 %cholesky.147 = f32[128,128]{1,0:T(8,128)S(1)} custom-call(f32[128,128]{1,0:T(8,128)S(1)} %convolution_subtract_fusion.3), custom_call_target="Cholesky" | custom-call | tf_op jit(solution)/shard_map/jit(cholesky)/cholesky | solution.py:18
  57.9 0.6 compare_reduce_fusion.3
  58.6 0.6 compare_reduce_fusion.2
  60.6 3.8 while.8
  60.6 0.6 fusion.49
  61.2 1.3 bitcast_dynamic-update-slice_fusion.4
  62.5 0.6 fusion.49
  63.1 1.3 bitcast_dynamic-update-slice_fusion.4
  64.4 19.9 %custom-call.14 = f32[2,128,128]{1,2,0:T(8,128)S(1)} custom-call(f32[2,128,128]{2,1,0:T(8,128)S(1)} %get-tuple-element.61), custom_call_target="InvertDiagBlocksLowerTriangular" | custom-call | tf_op jit(solution)/shard_map/jit(_solve_triangular)/triangular_solve | solution.py:20
  84.3 0.3 fusion.19
  84.6 0.3 convolution_subtract_fusion.1
  84.9 0.3 fusion.26
  85.2 0.8 maximum_select_fusion
  86.1 146.7 %all-reduce.10.cloned.1.call-done = f32[2,256,256]{2,1,0:T(8,128)} async-done(((f32[2,256,256]{2,1,0:T(8,128)}), f32[2,256,256]{2,1,0:T(8,128)}) %all-reduce.10.cloned.1.call-update) | async-done | bytes 524304 | tf_op jit(solution)/shard_map/psum | solution.py:14
  232.8 1.0 slice_bitcast_fusion.9
  233.8 2.9 fusion.5
  236.8 65.4 %all-reduce.12.cloned.1.call-done = f32[2,256,256]{2,1,0:T(8,128)} async-done(((f32[2,256,256]{2,1,0:T(8,128)}), f32[2,256,256]{2,1,0:T(8,128)}) %all-reduce.12.cloned.1.call-update) | async-done | bytes 524304 | tf_op jit(solution)/shard_map/psum | solution.py:14
  302.3 2.5 select_bitcast_fusion.7
  305.1 0.2 copy.19
  305.3 152.5 %all-reduce.20.cloned.1.call-done = (f32[2,1,256,256]{3,2,0,1:T(8,128)}, f32[2,1,256,256]{3,2,0,1:T(8,128)}, f32[2,1,256,256]{3,2,0,1:T(8,128)}, f32[2,1,256,256]{3,2,0,1:T(8,128)}) async-done(((f32[2,1,256,256]{3,2,0,1:T(8,128)}, f32[2,1,256,256]{3,2,0,1:T(8,128)}, f32[2,1,256,256]{3,2,0,1:T(8,128)}, f32[2,1,256,256]{3,2,0,1:T(8,128)}), (f32[2,1,256,256]{3,2,0,1:T(8,128)}, f32[2,1,256,256]{3,2,0,1:T(8,128)}, ...) | async-done | bytes 2097168 | tf_op jit(solution)/shard_map/psum | solution.py:14
  457.7 1.8 pad_maximum_fusion
  459.7 0.9 copy-done.2
  460.6 5.9 select_add_fusion
  466.4 2.0 copy-done.4
  468.5 1.0 fusion.9
  469.6 11.7 %cholesky.164 = f32[128,128]{1,0:T(8,128)S(1)} custom-call(f32[128,128]{1,0:T(8,128)S(1)} %cholesky.197), custom_call_target="Cholesky" | custom-call | tf_op jit(solution)/shard_map/jit(cholesky)/cholesky | solution.py:18
  481.3 9.8 %custom-call.15 = f32[1,128,128]{1,2,0:T(8,128)S(1)} custom-call(f32[1,128,128]{2,1,0:T(8,128)S(1)} %get-tuple-element.106), custom_call_target="InvertDiagBlocksLowerTriangular" | custom-call | tf_op jit(solution)/shard_map/jit(cholesky)/cholesky | solution.py:18
  491.1 1.0 constant_dynamic-update-slice_fusion.1
  492.2 1.1 convolution_subtract_fusion.2
  493.3 11.7 %cholesky.181 = f32[128,128]{1,0:T(8,128)S(1)} custom-call(f32[128,128]{1,0:T(8,128)S(1)} %convolution_subtract_fusion.2), custom_call_target="Cholesky" | custom-call | tf_op jit(solution)/shard_map/jit(cholesky)/cholesky | solution.py:18
  505.0 0.6 compare_reduce_fusion.1
  505.7 0.6 compare_reduce_fusion
  507.5 0.8 fusion.16
  508.3 4.1 while.9
  508.3 0.6 fusion.50
  508.9 1.4 bitcast_dynamic-update-slice_fusion.5
  510.4 0.6 fusion.50
  511.0 1.4 bitcast_dynamic-update-slice_fusion.5
  512.4 19.9 %custom-call.16 = f32[2,128,128]{1,2,0:T(8,128)S(1)} custom-call(f32[2,128,128]{2,1,0:T(8,128)S(1)} %get-tuple-element.62), custom_call_target="InvertDiagBlocksLowerTriangular" | custom-call | tf_op jit(solution)/shard_map/jit(_solve_triangular)/triangular_solve | solution.py:20
  532.3 0.3 fusion.17
  532.7 0.3 convolution_subtract_fusion
  532.9 0.3 fusion.22
  533.3 1.8 maximum_select_fusion.1
  535.2 144.5 %all-reduce.14.cloned.1.call-done = f32[2,256,256]{2,1,0:T(8,128)} async-done(((f32[2,256,256]{2,1,0:T(8,128)}), f32[2,256,256]{2,1,0:T(8,128)}) %all-reduce.14.cloned.1.call-update) | async-done | bytes 524304 | tf_op jit(solution)/shard_map/psum | solution.py:14
  679.7 1.0 slice_bitcast_fusion.6
  680.7 3.0 fusion.3
  683.7 65.4 %all-reduce.16.cloned.1.call-done = f32[2,256,256]{2,1,0:T(8,128)} async-done(((f32[2,256,256]{2,1,0:T(8,128)}), f32[2,256,256]{2,1,0:T(8,128)}) %all-reduce.16.cloned.1.call-update) | async-done | bytes 524304 | tf_op jit(solution)/shard_map/psum | solution.py:14
  749.2 2.5 select_bitcast_fusion.3
  751.9 1.0 copy.24
  752.9 152.1 %all-reduce.18.cloned.1.call-done = (f32[2,1,256,256]{3,2,0,1:T(8,128)}, f32[2,1,256,256]{3,2,0,1:T(8,128)}, f32[2,1,256,256]{3,2,0,1:T(8,128)}, f32[2,1,256,256]{3,2,0,1:T(8,128)}) async-done(((f32[2,1,256,256]{3,2,0,1:T(8,128)}, f32[2,1,256,256]{3,2,0,1:T(8,128)}, f32[2,1,256,256]{3,2,0,1:T(8,128)}, f32[2,1,256,256]{3,2,0,1:T(8,128)}), (f32[2,1,256,256]{3,2,0,1:T(8,128)}, f32[2,1,256,256]{3,2,0,1:T(8,128)}, ...) | async-done | bytes 2097168 | tf_op jit(solution)/shard_map/psum | solution.py:14
  905.1 1.8 pad_maximum_fusion.1
  907.0 0.9 copy-done
  907.9 1.3 copy-done.3
  909.1 7.1 bitcast_add_fusion
  916.3 10.9 %copy.28 = f32[2,1,256,8,1,256]{5,4,3,2,1,0:T(1,128)} copy(f32[2,1,256,8,1,256]{2,5,3,0,4,1:T(8,128)} %bitcast_add_fusion) | data formatting | bytes 8388608 | tf_op jit(solution)/shard_map/add | solution.py:53
  (72 shorter events, 1.7 us)
Async XLA Ops:
  6.5 226.3 %all-reduce.10.cloned.1.call-start = ((), (), s32[]{:S(2)}) async-start(), calls=%async_computation | async-start | bytes 1048576 | tf_op jit(solution)/shard_map/psum | solution.py:14
  6.6 10.9 %copy-start.8 = (s32[2,1,8,1]{2,3,1,0:T(1,128)S(1)}, s32[2,1,8,1]{2,3,1,0:T(1,128)}, u32[]{:S(2)}) copy-start(s32[2,1,8,1]{2,3,1,0:T(1,128)} %param.14) | copy-start | bytes 196
  17.5 3.5 copy-start.10
  21.0 2.0 copy-start.1
  86.1 216.2 %all-reduce.12.cloned.1.call-start = ((), (), s32[]{:S(2)}) async-start(), calls=%async_computation.1 | async-start | bytes 1048576 | tf_op jit(solution)/shard_map/psum | solution.py:14
  236.7 221.0 %all-reduce.20.cloned.1.call-start = ((), (), s32[]{:S(2)}) async-start(), calls=%async_computation.5 | async-start | bytes 4194304 | tf_op jit(solution)/shard_map/psum | solution.py:14
  302.2 2.8 copy-start.5
  304.8 374.9 %all-reduce.14.cloned.1.call-start = ((), (), s32[]{:S(2)}) async-start(), calls=%async_computation.2 | async-start | bytes 1048576 | tf_op jit(solution)/shard_map/psum | solution.py:14
  457.7 2.8 copy-start.2
  466.4 2.0 copy-start.4
  469.5 11.7 %copy-start.7 = (f32[256,256]{1,0:T(8,128)}, f32[256,256]{1,0:T(8,128)S(1)}, u32[]{:S(2)}) copy-start(f32[256,256]{1,0:T(8,128)S(1)} %fusion.9) | copy-start | bytes 786436
  535.1 216.7 %copy-start.9 = (pred[2,1,8,1]{2,3,1,0:T(4,128)(4,1)S(1)}, pred[2,1,8,1]{2,3,1,0:T(4,128)(4,1)}, u32[]{:S(2)}) copy-start(pred[2,1,8,1]{2,3,1,0:T(4,128)(4,1)} %get-tuple-element.111) | copy-start | bytes 52
  535.1 216.7 %copy-start.11 = (pred[8]{0:T(512)(128)(4,1)S(1)}, pred[8]{0:T(512)(128)(4,1)}, u32[]{:S(2)}) copy-start(pred[8]{0:T(512)(128)(4,1)} %copy-done.10) | copy-start | bytes 28
  535.1 214.1 %all-reduce.16.cloned.1.call-start = ((), (), s32[]{:S(2)}) async-start(), calls=%async_computation.3 | async-start | bytes 1048576 | tf_op jit(solution)/shard_map/psum | solution.py:14
  683.7 221.4 %all-reduce.18.cloned.1.call-start = ((), (), s32[]{:S(2)}) async-start(), calls=%async_computation.4 | async-start | bytes 4194304 | tf_op jit(solution)/shard_map/psum | solution.py:14
  749.2 2.8 copy-start.6
  905.1 2.8 copy-start
  905.1 4.1 copy-start.3
Sparse Core Ops, SparseCore 0:
  86.2 146.6 all-reduce.9
  236.9 65.3 all-reduce.11
  306.2 151.5 all-reduce.19
  535.2 144.4 all-reduce.13
  683.8 65.3 all-reduce.15
  753.5 151.5 all-reduce.17
where the time goes:
time: 938 us; the launch traced here: 934 us
  waiting for transfers between devices  727 us (78%)
  other arithmetic  127 us (14%)
  local copies, waits for them, and re-layouts  40.4 us (4%)
  matrix products  23.2 us (2%)
  between operations  16.3 us (2%)
    psum x6, waiting for transfers between devices, broadcast(): return lax.psum(block, axis)  727 us
    another operation x14, other arithmetic, lower_inverse(): factor = jnp.linalg.cholesky(pivot_block)  69.1 us
    another operation x3, other arithmetic, lower_inverse(): inverse = jax.scipy.linalg.solve_triangular(factor, identity, lower=True)  39.8 us
  transfers between devices with their start and end apart: 6, of which 6 were waited for; matrix products, arithmetic and copies ran while one was open for 0% of the time, Pallas kernels for 0%

commit v1 on v0

v1 whole, which is shorter than its diff:
```python
import jax
import jax.numpy as jnp
from jax import lax
from jax.experimental import pallas as pl
from jax.experimental.pallas import tpu as pltpu
from jax.sharding import PartitionSpec as P

W = 256
NB = 32
HIGHEST = lax.Precision.HIGHEST
F32 = jnp.float32
BF16 = jnp.bfloat16


def dot_nn(a, b):
    return lax.dot_general(a, b, (((1,), (0,)), ((), ())), precision=HIGHEST, preferred_element_type=F32)


def dot_nt(a, b):
    return lax.dot_general(a, b, (((1,), (1,)), ((), ())), precision=HIGHEST, preferred_element_type=F32)


def dot_tn(a, b):
    return lax.dot_general(a, b, (((0,), (0,)), ((), ())), precision=HIGHEST, preferred_element_type=F32)


def split3(x):
    hi = x.astype(BF16)
    rest = x - hi.astype(F32)
    mid = rest.astype(BF16)
    low = (rest - mid.astype(F32)).astype(BF16)
    return hi, mid, low


def eliminate(rows):
    sub = lax.broadcasted_iota(jnp.int32, (8, 384), 0)
    for t in range(4):
        x = rows[t]
        head = x[:, 0:128]
        cols = [jnp.broadcast_to(head[:, 8 * t + k : 8 * t + k + 1], (8, 128)) for k in range(8)]
        below = {
            g: [
                jnp.broadcast_to(rows[g][:, 8 * t + k : 8 * t + k + 1], (8, 128))
                for k in range(8)
            ]
            for g in range(t + 1, 4)
        }
        a = {
            (i, k): jnp.broadcast_to(cols[k][i : i + 1, :], (8, 128))
            for k in range(8)
            for i in range(k, 8)
        }
        r = [jnp.broadcast_to(x[k : k + 1, :], (8, 384)) for k in range(8)]
        for k in range(8):
            scale = lax.rsqrt(a[k, k])
            wide = jnp.concatenate([scale] * 3, axis=1)
            r[k] = r[k] * wide
            for g in below:
                below[g][k] = below[g][k] * scale
            l = {i: a[i, k] * scale for i in range(k + 1, 8)}
            for i in range(k + 1, 8):
                for j in range(k + 1, i + 1):
                    a[i, j] = a[i, j] - l[i] * l[j]
                r[i] = r[i] - jnp.concatenate([l[i]] * 3, axis=1) * r[k]
                for g in below:
                    below[g][i] = below[g][i] - l[i] * below[g][k]
        out = r[0]
        for k in range(1, 8):
            out = jnp.where(sub == k, r[k], out)
        rows[t] = out
        for g in below:
            acc = rows[g]
            for k in range(8):
                acc = acc - jnp.concatenate([below[g][k]] * 3, axis=1) * r[k]
            rows[g] = acc
    return rows


def factor_block(g_ref, u_ref, v_ref):
    lane = lax.broadcasted_iota(jnp.int32, (NB, W), 1)
    row = lax.broadcasted_iota(jnp.int32, (NB, W), 0)
    eye = (
        lax.broadcasted_iota(jnp.int32, (NB, 128), 0)
        == lax.broadcasted_iota(jnp.int32, (NB, 128), 1)
    ).astype(F32)
    tail = lax.broadcasted_iota(jnp.int32, (W - NB, W), 1)

    def panel(p, carry):
        x = jnp.concatenate([g_ref[0:NB, :], eye], axis=1)
        rows = eliminate([x[8 * t : 8 * t + 8] for t in range(4)])
        r = jnp.concatenate(rows, axis=0)
        shifted = pltpu.roll(r, 384 - NB, 1)[:, 0:W]
        at = pl.multiple_of(p * NB, NB)
        u_ref[pl.ds(at, NB), :] = jnp.where(
            lane >= row + at, pltpu.roll(r[:, 0:W], at, 1), 0.0
        )
        v_ref[pl.ds(at, NB), :] = jnp.where(
            lane <= row + at, pltpu.roll(shifted, at + NB, 1), 0.0
        )
        hi, mid, low = split3(shifted)
        left = jnp.concatenate([hi, hi, mid, mid, hi, low], axis=0)
        right = jnp.concatenate([hi, mid, hi, mid, low, hi], axis=0)
        prod = lax.dot_general(
            left, right, (((0,), (0,)), ((), ())), preferred_element_type=F32
        )
        old = pltpu.roll(g_ref[NB:W, :], W - NB, 1)
        g_ref[0 : W - NB, :] = jnp.where(tail < W - NB, old, 0.0) - prod[0 : W - NB, :]
        return carry

    lax.fori_loop(0, W // NB, panel, 0)


def factor_kernel(t_ref, a01_ref, u0_ref, v0_ref, pt_ref, u1_ref, v1_ref, g_ref):
    lower = lax.broadcasted_iota(jnp.int32, (W, W), 0)
    upper = lax.broadcasted_iota(jnp.int32, (W, W), 1)
    t = t_ref[0:W, :]
    flipped = jnp.transpose(t)
    g_ref[...] = jnp.where(lower >= upper, t, flipped)
    factor_block(g_ref, u0_ref, v0_ref)
    pt = dot_nn(v0_ref[...], a01_ref[0:W, :])
    pt_ref[...] = pt
    own = jnp.where(lower < upper, t, flipped)
    own = jnp.where(lower == upper, t_ref[W : W + 1, :], own)
    g_ref[...] = own - dot_tn(pt, pt)
    factor_block(g_ref, u1_ref, v1_ref)


def factor_pair(packed, a01):
    block = jax.ShapeDtypeStruct((W, W), F32)
    return pl.pallas_call(
        factor_kernel,
        out_shape=[block] * 5,
        scratch_shapes=[pltpu.VMEM((W, W), F32)],
        compiler_params=pltpu.CompilerParams(vmem_limit_bytes=32 * 1024 * 1024),
        name="factor_pair",
    )(packed, a01)


def extract_kernel(info_ref, front_ref, slab_ref, block_ref, *piece_refs):
    odd = info_ref[2]
    for m in range(2):
        keep = info_ref[m] > 0
        for h in range(2):
            part = front_ref[pl.ds(m * 4096 + h, W, stride=16), :]
            part = jnp.where(keep, part, 0.0)
            slab_ref[2 * m + h] = part
            if m == 0:
                block_ref[0:W, 128 * h : 128 * h + 128] = part
            for half in range(2):
                place = 2 * h + half
                mine = part[128 * half : 128 * half + 128]

                @pl.when(odd == 0)
                def _(place=place, mine=mine, m=m):
                    piece_refs[4 * m + place][...] = mine

                @pl.when(odd != 0)
                def _(place=place, mine=mine, m=m):
                    piece_refs[4 * (1 - m) + place][...] = mine

    block_ref[W : W + 8, :] = jnp.zeros((8, W), F32)


def extract(info, view):
    return pl.pallas_call(
        extract_kernel,
        in_specs=[
            pl.BlockSpec(memory_space=pltpu.SMEM),
            pl.BlockSpec(memory_space=pltpu.VMEM),
        ],
        out_specs=[pl.BlockSpec(memory_space=pltpu.VMEM)] * 10,
        out_shape=[
            jax.ShapeDtypeStruct((4, W, 128), F32),
            jax.ShapeDtypeStruct((W + 8, W), F32),
        ]
        + [jax.ShapeDtypeStruct((128, 128), F32)] * 8,
        compiler_params=pltpu.CompilerParams(vmem_limit_bytes=32 * 1024 * 1024),
        name="extract",
    )(info, view)


def split2(x):
    hi = x.astype(BF16)
    return hi, (x - hi.astype(F32)).astype(BF16)


def dot_bf(a, b):
    return lax.dot_general(a, b, (((1,), (1,)), ((), ())), preferred_element_type=F32)


def update_kernel(
    info_ref, mask_ref, front_ref, q_ref, p_ref, u0_ref, v0_ref, pt_ref, u1_ref, v1_ref,
    out_ref, qh_ref, ql_ref, ph_ref, pl_ref,
):
    step = pl.program_id(0)
    r, c, x = info_ref[0], info_ref[1], info_ref[2]
    lane = lax.broadcasted_iota(jnp.int32, (W, 2 * W), 1)
    row = lax.broadcasted_iota(jnp.int32, (W, 2 * W), 0)

    def solve(raw0, raw1, place):
        first = dot_nt(raw0, v0_ref[...])
        second = dot_nt(raw1 - dot_nn(first, pt_ref[...]), v1_ref[...])
        both = jnp.concatenate([first, second], axis=1)
        unit = jnp.where(lane == row + place * W, -1.0, 0.0)
        return split2(jnp.where(place < 2, unit, both))

    @pl.when(step == 0)
    def _():
        for m in range(2):
            raw = [
                jnp.concatenate([p_ref[s, 2 * m], p_ref[s, 2 * m + 1]], axis=1)
                for s in range(2)
            ]
            place = r if m == 0 else r + 32
            ph_ref[m], pl_ref[m] = solve(raw[0], raw[1], place)
        for n in range(8):
            m = n // 4
            near = lax.rem(n % 4 - x + 4, 4)
            raw = []
            for s in range(2):
                tall = []
                for h in range(2):
                    parts = [
                        q_ref[lax.rem(4 * m + 2 * h + half + c, 8), near, s]
                        for half in range(2)
                    ]
                    tall.append(jnp.concatenate(parts, axis=0))
                raw.append(jnp.concatenate(tall, axis=1))
            qh_ref[n], ql_ref[n] = solve(raw[0], raw[1], c + 8 * n)

    ph = ph_ref[step]
    pl_ = pl_ref[step]
    for n in range(8):
        qh = qh_ref[n]
        prod = dot_bf(ph, qh) + (dot_bf(ph, ql_ref[n]) + dot_bf(pl_, qh))
        keep = mask_ref[step, n] > 0
        for h in range(2):
            here = pl.ds(2 * n + h, W, stride=16)
            old = jnp.where(keep, front_ref[here, :], 0.0)
            out_ref[here, :] = old - prod[:, 128 * h : 128 * h + 128]

    def place_block(block):
        for h in range(2):
            out_ref[pl.ds(h, W, stride=16), :] = block[:, 128 * h : 128 * h + 128]

    corner = jnp.logical_and(step == 0, jnp.logical_and(r < 2, c < 2))

    @pl.when(jnp.logical_and(corner, r + c == 0))
    def _():
        place_block(jnp.transpose(u0_ref[...]))

    @pl.when(jnp.logical_and(corner, r < c))
    def _():
        place_block(pt_ref[...])

    @pl.when(jnp.logical_and(corner, r > c))
    def _():
        place_block(jnp.transpose(pt_ref[...]))

    @pl.when(jnp.logical_and(corner, r + c == 2))
    def _():
        place_block(jnp.transpose(u1_ref[...]))


def update(info, mask, view, gathered, rows, factors):
    whole = pl.BlockSpec(memory_space=pltpu.VMEM)
    return pl.pallas_call(
        update_kernel,
        grid=(2,),
        in_specs=[
            pl.BlockSpec(memory_space=pltpu.SMEM),
            pl.BlockSpec(memory_space=pltpu.SMEM),
            pl.BlockSpec((4096, 128), lambda i: (i, 0)),
        ]
        + [whole] * 7,
        out_specs=pl.BlockSpec((4096, 128), lambda i: (i, 0)),
        out_shape=jax.ShapeDtypeStruct((8192, 128), F32),
        scratch_shapes=[
            pltpu.VMEM((8, W, 2 * W), BF16),
            pltpu.VMEM((8, W, 2 * W), BF16),
            pltpu.VMEM((2, W, 2 * W), BF16),
            pltpu.VMEM((2, W, 2 * W), BF16),
        ],
        compiler_params=pltpu.CompilerParams(vmem_limit_bytes=48 * 1024 * 1024),
        name="update",
    )(info, mask, view, gathered, rows, *factors)


BOTH = ("row", "col")


def device(x, z, c):
    return (x * 8 + z) * 8 + c


def fan(value, axis, moves):
    total = value
    for pairs in moves:
        total = total + lax.ppermute(value, axis, pairs)
    return total


def on_device(front, pattern):
    row_place = lax.axis_index("row")
    col_place = lax.axis_index("col")
    x_place = row_place // 8
    view = front.reshape(8192, 128)
    present = pattern.reshape(2, 8)
    parity = col_place % 2
    zero = jnp.zeros((), jnp.int32)

    info = jnp.stack([present[0, 0], present[1, 0], parity])
    slab, block, *pieces = extract(info, view)

    far = lax.ppermute(block, BOTH, [(device(0, 1, 1), device(0, 0, 0))])
    below = lax.broadcasted_iota(jnp.int32, (W, W), 0)
    right = lax.broadcasted_iota(jnp.int32, (W, W), 1)
    packed = jnp.where(below >= right, block[:W], far[:W])
    extra = jnp.sum(jnp.where(below == right, far[:W], 0.0), axis=0, keepdims=True)
    packed = jnp.concatenate([packed, jnp.broadcast_to(extra, (8, W))], axis=0)
    mine = (row_place == 0) & (col_place < 2)
    diag = jnp.where(mine, jnp.where(col_place == 0, packed, block), 0.0)
    diag = fan(diag, BOTH, [
        [(device(0, 0, s), device(0, 3, s)) for s in range(2)],
        [(device(0, 0, s), device(0, 6, s)) for s in range(2)],
    ])
    diag = fan(diag, BOTH, [
        [(device(0, z, s), device(0, z + 1, s)) for z in (0, 3, 6) for s in range(2)],
        [(device(0, z, s), device(0, z - 1, s)) for z in (3, 6) for s in range(2)],
    ])
    diag = fan(diag, BOTH, [
        [(device(0, z, s), device(x, z, s)) for z in range(8) for s in range(2)]
        for x in (1, 3, 2)
    ])
    diag = fan(diag, "col", [[(s, s + y) for s in range(2)] for y in (2, 6, 4)])
    swap = [(c, c ^ 1) for c in range(8)]
    other = lax.ppermute(diag, "col", swap)
    first = jnp.where(parity == 0, diag, other)
    second = jnp.where(parity == 0, other, diag)
    factors = factor_pair(first, second)

    near = jnp.zeros((128, 128), F32)
    cross = jnp.zeros((128, 128), F32)
    offset = (row_place - col_place) % 8
    for k in range(8):
        pairs = [
            (device(x, z, s), device(x, (z + k + 4 * s) % 8, z))
            for x in range(4)
            for z in range(8)
            for s in range(2)
        ]
        got = lax.ppermute(pieces[k], BOTH, pairs)
        near = jnp.where(offset == k, got, near)
        cross = jnp.where(offset == (k + 4) % 8, got, cross)
    share = jnp.stack([near, cross])
    around = [share]
    for d in range(1, 4):
        pairs = [
            (((x + d) % 4) * 8 + z, x * 8 + z) for x in range(4) for z in range(8)
        ]
        around.append(lax.ppermute(share, "row", pairs))
    around = jnp.stack(around)
    groups = [[x * 8 + z for z in range(8)] for x in range(4)]
    gathered = lax.all_gather(around, "row", axis_index_groups=groups)

    slab = jnp.where(col_place < 2, slab, 0.0)
    slab = fan(slab, "col", [[(s, s + y) for s in range(2)] for y in (2, 6, 4)])
    twin = lax.ppermute(slab, "col", swap)
    rows = jnp.where(parity == 0, jnp.stack([slab, twin]), jnp.stack([twin, slab]))

    global_rows = jnp.arange(2, dtype=jnp.int32) * 32 + row_place
    global_cols = jnp.arange(8, dtype=jnp.int32) * 8 + col_place
    mask = jnp.where(
        (global_rows > 1)[:, None] & (global_cols > 1)[None, :], present, 0
    )
    place = jnp.stack([row_place, col_place, x_place, zero])
    out = update(place, mask, view, gathered, rows, factors)
    return out.reshape(2, 1, 256, 8, 1, 256)


def solution(mesh):
    placed = (P(None, "row", None, None, "col", None), P(None, "row", None, "col"))
    return jax.shard_map(
        on_device,
        mesh=mesh,
        in_specs=placed,
        out_specs=P(None, "row", None, None, "col", None),
        check_vma=False,
    )
```

time: 938 us -> 164 us (0.17)
  waiting for transfers between devices: 727 us -> 30.5 us
  other arithmetic: 127 us -> 3.05 us
  starting transfers between devices: 0.21 us -> 72.6 us
  Pallas kernels: 0 us -> 39.5 us
  local copies, waits for them, and re-layouts: 40.4 us -> 3.49 us
  matrix products: 23.2 us -> 0 us
    psum x6 -> x0, waiting for transfers between devices: 727 us -> none  [broadcast(): return lax.psum(block, axis)]
    another operation x25 -> x5, other arithmetic: 118 us -> 2.32 us  [the longest x1 1.36 us: on_device(): info = jnp.stack([present[0, 0], present[1, 0], parity])]
    ppermute x0 -> x27, starting transfers between devices: none -> 72.6 us  [the longest x8 24.1 us: on_device(): got = lax.ppermute(pieces[k], BOTH, pairs)]
    pallas_call x0 -> x3, Pallas kernels: none -> 39.5 us  [the longest x1 19.7 us: update(): pl.pallas_call(update_kernel, grid=(2,), in_specs=[pl.BlockSpec(memory_sp...]
    ppermute x0 -> x27, waiting for transfers between devices: none -> 30.5 us  [the longest x13 23.2 us: fan(): total = total + lax.ppermute(value, axis, pairs)]
    dot_general x4 -> x0, matrix products: 18.9 us -> none  [the longest x2 13 us: update_slots(): lax.dot_general(left_side, right_side, (((1,), (1,)), ((), ())), precisio...]
    unnamed x28 -> x4, local copies, waits for them, and re-layouts: 17.9 us -> 2.2 us
    add x1 -> x0, local copies, waits for them, and re-layouts: 10.9 us -> none  [update_slots(): working.at[:, :, first_slot:last_slot, :]]
  transfers between devices with their start and end apart: 6 -> 28, of which waited for: 6 -> 10; matrix products, arithmetic and copies ran while one was open for 0% -> 1% of each run, Pallas kernels for 0% -> 12%
where the time goes in v1:
time: 164 us; the launch traced here: 163 us
  starting transfers between devices  72.6 us (44%)
  Pallas kernels  39.5 us (24%)
  waiting for transfers between devices  30.5 us (19%)
  between operations  13.8 us (8%)
  local copies, waits for them, and re-layouts  3.49 us (2%)
  other arithmetic  3.05 us (2%)
    ppermute x8, starting transfers between devices, on_device(): got = lax.ppermute(pieces[k], BOTH, pairs)  24.1 us
    ppermute x13, waiting for transfers between devices, fan(): total = total + lax.ppermute(value, axis, pairs)  23.2 us
    ppermute x13, starting transfers between devices, fan(): total = total + lax.ppermute(value, axis, pairs)  21.7 us
    pallas_call x1, Pallas kernels, update(): pl.pallas_call(update_kernel, grid=(2,), in_specs=[pl.BlockSpec(memory_sp...  19.7 us
    pallas_call x1, Pallas kernels, factor_pair(): pl.pallas_call(factor_kernel, out_shape=[block] * 5, scratch_shapes=[pltp...  18.9 us
    ppermute x1, starting transfers between devices, on_device(): twin = lax.ppermute(slab, 'col', swap)  16.1 us
    ppermute x1, starting transfers between devices, on_device(): other = lax.ppermute(diag, 'col', swap)  5.67 us
    ppermute x3, waiting for transfers between devices, on_device(): around.append(lax.ppermute(share, 'row', pairs))  4.68 us
  transfers between devices with their start and end apart: 28, of which 10 were waited for; matrix products, arithmetic and copies ran while one was open for 1% of the time, Pallas kernels for 12%

profile of v1, /device:TPU:1, one launch (start us, length us, event | category | flops | bytes accessed | tf_op | source)
XLA Modules:
  0.0 162.9 jit_solution(8216734703911817710)
XLA Ops:
  6.5 1.3 fusion.2
  7.8 1.4 pad_add_fusion.1.info_ref
  9.2 2.2 %copy-done = f32[2,1,256,8,1,256]{5,4,3,2,1,0:T(1,128)S(1)} copy-done((f32[2,1,256,8,1,256]{5,4,3,2,1,0:T(1,128)S(1)}, f32[2,1,256,8,1,256]{5,4,3,2,1,0:T(1,128)}, u32[]{:S(2)}) %copy-start) | copy-done | bytes 4194328
  11.4 0.9 extract.1
  12.3 7.6 %collective-permute-start = (f32[128,128]{1,0:T(8,128)S(1)}, f32[128,128]{1,0:T(8,128)S(1)}, u32[]{:S(2)}, u32[]{:S(2)}) collective-permute-start(f32[128,128]{1,0:T(8,128)S(1)} %get-tuple-element.20), channel_id=1, source_target_pairs={{0,56},{1,24},{8,1},{9,33},{16,10},{17,42},{24,19},{25,51},{32,28}... | collective-permute-start | bytes 196616 | tf_op jit(solution)/shard_map/ppermute | solution.py:352
  19.9 1.7 %collective-permute-start.1 = (f32[128,128]{1,0:T(8,128)S(1)}, f32[128,128]{1,0:T(8,128)S(1)}, u32[]{:S(2)}, u32[]{:S(2)}) collective-permute-start(f32[128,128]{1,0:T(8,128)S(1)} %get-tuple-element.21), channel_id=1, source_target_pairs={{0,48},{1,16},{8,57},{9,25},{16,2},{17,34},{24,11},{25,43},{32,20}... | collective-permute-start | bytes 196616 | tf_op jit(solution)/shard_map/ppermute | solution.py:352
  21.6 6.5 %collective-permute-start.2 = (f32[128,128]{1,0:T(8,128)S(1)}, f32[128,128]{1,0:T(8,128)S(1)}, u32[]{:S(2)}, u32[]{:S(2)}) collective-permute-start(f32[128,128]{1,0:T(8,128)S(1)} %get-tuple-element.22), channel_id=1, source_target_pairs={{0,40},{1,8},{8,49},{9,17},{16,58},{17,26},{24,3},{25,35},{32,12},... | collective-permute-start | bytes 196616 | tf_op jit(solution)/shard_map/ppermute | solution.py:352
  28.1 2.5 %collective-permute-start.3 = (f32[128,128]{1,0:T(8,128)S(1)}, f32[128,128]{1,0:T(8,128)S(1)}, u32[]{:S(2)}, u32[]{:S(2)}) collective-permute-start(f32[128,128]{1,0:T(8,128)S(1)} %get-tuple-element.23), channel_id=1, source_target_pairs={{0,32},{1,0},{8,41},{9,9},{16,50},{17,18},{24,59},{25,27},{32,4},{... | collective-permute-start | bytes 196616 | tf_op jit(solution)/shard_map/ppermute | solution.py:352
  30.6 1.9 %collective-permute-start.4 = (f32[128,128]{1,0:T(8,128)S(1)}, f32[128,128]{1,0:T(8,128)S(1)}, u32[]{:S(2)}, u32[]{:S(2)}) collective-permute-start(f32[128,128]{1,0:T(8,128)S(1)} %get-tuple-element.24), channel_id=1, source_target_pairs={{0,24},{1,56},{8,33},{9,1},{16,42},{17,10},{24,51},{25,19},{32,60}... | collective-permute-start | bytes 196616 | tf_op jit(solution)/shard_map/ppermute | solution.py:352
  32.6 0.0 collective-permute-done
  32.6 1.3 collective-permute-start.5
  33.9 0.0 collective-permute-done.1
  33.9 1.3 collective-permute-start.6
  35.2 0.0 collective-permute-done.2
  35.2 1.3 collective-permute-start.7
  36.5 0.5 collective-permute-done.4
  37.0 0.0 collective-permute-done.5
  37.0 1.2 collective-permute-done.6
  38.3 2.8 %collective-permute-start.9 = (f32[2,128,128]{2,1,0:T(8,128)S(1)}, f32[2,128,128]{2,1,0:T(8,128)S(1)}, u32[]{:S(2)}, u32[]{:S(2)}) collective-permute-start(f32[2,128,128]{2,1,0:T(8,128)S(1)} %get-tuple-element.42), channel_id=1, source_target_pairs={{128,0},{136,8},{144,16},{152,24},{160,32},{168,40},{176,48},{184,... | collective-permute-start | bytes 393224 | tf_op jit(solution)/shard_map/ppermute | solution.py:361
  41.1 0.9 collective-permute-start.8
  42.0 0.6 collective-permute-start.10
  42.6 1.8 %collective-permute-done.9 = f32[2,128,128]{2,1,0:T(8,128)S(1)} collective-permute-done((f32[2,128,128]{2,1,0:T(8,128)S(1)}, f32[2,128,128]{2,1,0:T(8,128)S(1)}, u32[]{:S(2)}, u32[]{:S(2)}) %collective-permute-start.9) | collective-permute-done | bytes 131104 | tf_op jit(solution)/shard_map/ppermute | solution.py:361
  44.4 2.9 %collective-permute-done.8 = f32[2,128,128]{2,1,0:T(8,128)S(1)} collective-permute-done((f32[2,128,128]{2,1,0:T(8,128)S(1)}, f32[2,128,128]{2,1,0:T(8,128)S(1)}, u32[]{:S(2)}, u32[]{:S(2)}) %collective-permute-start.8) | collective-permute-done | bytes 131104 | tf_op jit(solution)/shard_map/ppermute | solution.py:361
  47.3 0.0 collective-permute-done.10
  47.3 0.8 pad_maximum_fusion
  48.1 0.0 all-gather.3.cloned.1.call-update
  48.1 0.7 collective-permute-start.15
  48.8 0.0 collective-permute-done.15
  48.8 0.1 slice_select_fusion
  48.9 0.0 copy-start.1
  48.9 6.6 %collective-permute-start.17 = (f32[264,256]{1,0:T(8,128)S(1)}, f32[264,256]{1,0:T(8,128)S(1)}, u32[]{:S(2)}, u32[]{:S(2)}) collective-permute-start(f32[264,256]{1,0:T(8,128)S(1)} %fusion), channel_id=1, source_target_pairs={{0,48},{1,49}} | collective-permute-start | bytes 811016 | tf_op jit(solution)/shard_map/ppermute | solution.py:299
  55.6 1.3 collective-permute-start.16
  56.9 2.1 %collective-permute-done.17 = f32[264,256]{1,0:T(8,128)S(1)} collective-permute-done((f32[264,256]{1,0:T(8,128)S(1)}, f32[264,256]{1,0:T(8,128)S(1)}, u32[]{:S(2)}, u32[]{:S(2)}) %collective-permute-start.17) | collective-permute-done | bytes 270368 | tf_op jit(solution)/shard_map/ppermute | solution.py:299
  58.9 2.2 %collective-permute-done.16 = f32[264,256]{1,0:T(8,128)S(1)} collective-permute-done((f32[264,256]{1,0:T(8,128)S(1)}, f32[264,256]{1,0:T(8,128)S(1)}, u32[]{:S(2)}, u32[]{:S(2)}) %collective-permute-start.16) | collective-permute-done | bytes 270368 | tf_op jit(solution)/shard_map/ppermute | solution.py:299
  61.2 0.1 add_add_fusion.4
  61.2 0.7 collective-permute-start.19
  61.9 1.3 collective-permute-start.18
  63.2 0.0 collective-permute-done.19
  63.2 11.2 %collective-permute-done.18 = f32[264,256]{1,0:T(8,128)S(1)} collective-permute-done((f32[264,256]{1,0:T(8,128)S(1)}, f32[264,256]{1,0:T(8,128)S(1)}, u32[]{:S(2)}, u32[]{:S(2)}) %collective-permute-start.18) | collective-permute-done | bytes 270368 | tf_op jit(solution)/shard_map/ppermute | solution.py:299
  74.4 0.1 add_add_fusion.3
  74.5 1.3 collective-permute-start.22
  75.8 1.3 collective-permute-start.21
  77.1 1.3 collective-permute-start.20
  78.5 1.3 collective-permute-start.12
  79.8 1.3 collective-permute-start.13
  81.1 1.3 collective-permute-start.11
  82.5 0.1 add_add_fusion.2
  82.6 1.3 collective-permute-start.25
  83.9 1.3 collective-permute-start.24
  85.2 0.6 collective-permute-done.12
  85.9 1.3 collective-permute-start.23
  87.2 0.0 collective-permute-done.13
  87.2 7.0 %collective-permute-done.11 = f32[4,256,128]{2,1,0:T(8,128)S(1)} collective-permute-done((f32[4,256,128]{2,1,0:T(8,128)S(1)}, f32[4,256,128]{2,1,0:T(8,128)S(1)}, u32[]{:S(2)}, u32[]{:S(2)}) %collective-permute-start.11) | collective-permute-done | bytes 524320 | tf_op jit(solution)/shard_map/ppermute | solution.py:299
  94.2 0.1 add_add_fusion
  94.3 16.1 %collective-permute-start.14 = (f32[4,256,128]{2,1,0:T(8,128)S(1)}, f32[4,256,128]{2,1,0:T(8,128)S(1)}, u32[]{:S(2)}, u32[]{:S(2)}) collective-permute-start(f32[4,256,128]{2,1,0:T(8,128)S(1)} %add_add_fusion), channel_id=1, source_target_pairs={{0,1},{1,0},{2,3},{3,2},{4,5},{5,4},{6,7},{7,6},{8,9},{9,8},{10,11... | collective-permute-start | bytes 1572872 | tf_op jit(solution)/shard_map/ppermute | solution.py:368
  110.4 0.1 add_add_fusion.1
  110.5 5.7 %collective-permute-start.26 = (f32[264,256]{1,0:T(8,128)S(1)}, f32[264,256]{1,0:T(8,128)S(1)}, u32[]{:S(2)}, u32[]{:S(2)}) collective-permute-start(f32[264,256]{1,0:T(8,128)S(1)} %add_add_fusion.1), channel_id=1, source_target_pairs={{0,1},{1,0},{2,3},{3,2},{4,5},{5,4},{6,7},{7,6},{8,9},{9,8},{10,11... | collective-permute-start | bytes 811016 | tf_op jit(solution)/shard_map/ppermute | solution.py:337
  116.2 0.1 and_select_fusion.mask_ref
  116.3 0.1 pad_add_fusion.info_ref
  116.4 0.1 maximum_select_fusion.p_ref
  116.4 0.9 collective-permute-done.26
  117.4 18.9 %factor_pair.1 = (f32[256,256]{1,0:T(8,128)S(1)}, f32[256,256]{1,0:T(8,128)S(1)}, f32[256,256]{1,0:T(8,128)S(1)}, f32[256,256]{1,0:T(8,128)S(1)}, f32[256,256]{1,0:T(8,128)S(1)}) custom-call(f32[264,256]{1,0:T(8,128)S(1)} %get-tuple-element.36.t_ref, f32[264,256]{1,0:T(8,128)S(1)} %get-tuple-element.35.a01_ref), custom_call_target="tpu_custom_call" | custom-call | tf_op jit(solution)/shard_map/factor_pair/pallas_call | solution.py:130
  136.3 0.0 all-gather.3.cloned.1.call-done
  136.4 19.7 %update.1 = f32[8192,128]{1,0:T(8,128)} custom-call(s32[4]{0:T(128)S(1)} %pad_add_fusion.info_ref, s32[2,8]{1,0:T(2,128)S(1)} %and_select_fusion.mask_ref, f32[8192,128]{1,0:T(8,128)} %bitcast.21, f32[8,4,2,128,128]{4,3,2,1,0:T(8,128)} %bitcast.23, f32[2,4,256,128]{3,2,1,0:T(8,128)S(1)} %maximum_select_fusion.p_ref, ...), custom_call_target="tpu_custom_call" | custom-call | tf_op jit(solution)/shard_map/update/pallas_call | solution.py:267
  (20 shorter events, 0.2 us)
Async XLA Ops:
  6.5 129.8 %all-gather.3.cloned.1.call-start = ((), (), s32[]{:S(2)}) async-start(), calls=%async_computation | async-start | bytes 4718592 | tf_op jit(solution)/shard_map/all_gather | solution.py:364
  9.2 2.2 %copy-start = (f32[2,1,256,8,1,256]{5,4,3,2,1,0:T(1,128)S(1)}, f32[2,1,256,8,1,256]{5,4,3,2,1,0:T(1,128)}, u32[]{:S(2)}) copy-start(f32[2,1,256,8,1,256]{5,4,3,2,1,0:T(1,128)} %param.2) | copy-start | bytes 12582916
  12.3 20.3 %collective-permute-start = (f32[128,128]{1,0:T(8,128)S(1)}, f32[128,128]{1,0:T(8,128)S(1)}, u32[]{:S(2)}, u32[]{:S(2)}) collective-permute-start(f32[128,128]{1,0:T(8,128)S(1)} %get-tuple-element.20), channel_id=1, source_target_pairs={{0,56},{1,24},{8,1},{9,33},{16,10},{17,42},{24,19},{25,51},{32,28}... | collective-permute-start | bytes 196616 | tf_op jit(solution)/shard_map/ppermute | solution.py:352
  19.9 14.0 %collective-permute-start.1 = (f32[128,128]{1,0:T(8,128)S(1)}, f32[128,128]{1,0:T(8,128)S(1)}, u32[]{:S(2)}, u32[]{:S(2)}) collective-permute-start(f32[128,128]{1,0:T(8,128)S(1)} %get-tuple-element.21), channel_id=1, source_target_pairs={{0,48},{1,16},{8,57},{9,25},{16,2},{17,34},{24,11},{25,43},{32,20}... | collective-permute-start | bytes 196616 | tf_op jit(solution)/shard_map/ppermute | solution.py:352
  21.6 13.6 %collective-permute-start.2 = (f32[128,128]{1,0:T(8,128)S(1)}, f32[128,128]{1,0:T(8,128)S(1)}, u32[]{:S(2)}, u32[]{:S(2)}) collective-permute-start(f32[128,128]{1,0:T(8,128)S(1)} %get-tuple-element.22), channel_id=1, source_target_pairs={{0,40},{1,8},{8,49},{9,17},{16,58},{17,26},{24,3},{25,35},{32,12},... | collective-permute-start | bytes 196616 | tf_op jit(solution)/shard_map/ppermute | solution.py:352
  28.1 8.4 %collective-permute-start.3 = (f32[128,128]{1,0:T(8,128)S(1)}, f32[128,128]{1,0:T(8,128)S(1)}, u32[]{:S(2)}, u32[]{:S(2)}) collective-permute-start(f32[128,128]{1,0:T(8,128)S(1)} %get-tuple-element.23), channel_id=1, source_target_pairs={{0,32},{1,0},{8,41},{9,9},{16,50},{17,18},{24,59},{25,27},{32,4},{... | collective-permute-start | bytes 196616 | tf_op jit(solution)/shard_map/ppermute | solution.py:352
  30.6 6.4 %collective-permute-start.4 = (f32[128,128]{1,0:T(8,128)S(1)}, f32[128,128]{1,0:T(8,128)S(1)}, u32[]{:S(2)}, u32[]{:S(2)}) collective-permute-start(f32[128,128]{1,0:T(8,128)S(1)} %get-tuple-element.24), channel_id=1, source_target_pairs={{0,24},{1,56},{8,33},{9,1},{16,42},{17,10},{24,51},{25,19},{32,60}... | collective-permute-start | bytes 196616 | tf_op jit(solution)/shard_map/ppermute | solution.py:352
  32.6 4.5 %collective-permute-start.5 = (f32[128,128]{1,0:T(8,128)S(1)}, f32[128,128]{1,0:T(8,128)S(1)}, u32[]{:S(2)}, u32[]{:S(2)}) collective-permute-start(f32[128,128]{1,0:T(8,128)S(1)} %get-tuple-element.25), channel_id=1, source_target_pairs={{0,16},{1,48},{8,25},{9,57},{16,34},{17,2},{24,43},{25,11},{32,52}... | collective-permute-start | bytes 196616 | tf_op jit(solution)/shard_map/ppermute | solution.py:352
  33.9 4.3 %collective-permute-start.6 = (f32[128,128]{1,0:T(8,128)S(1)}, f32[128,128]{1,0:T(8,128)S(1)}, u32[]{:S(2)}, u32[]{:S(2)}) collective-permute-start(f32[128,128]{1,0:T(8,128)S(1)} %get-tuple-element.26), channel_id=1, source_target_pairs={{0,8},{1,40},{8,17},{9,49},{16,26},{17,58},{24,35},{25,3},{32,44},... | collective-permute-start | bytes 196616 | tf_op jit(solution)/shard_map/ppermute | solution.py:352
  35.2 3.0 %collective-permute-start.7 = (f32[128,128]{1,0:T(8,128)S(1)}, f32[128,128]{1,0:T(8,128)S(1)}, u32[]{:S(2)}, u32[]{:S(2)}) collective-permute-start(f32[128,128]{1,0:T(8,128)S(1)} %get-tuple-element.27), channel_id=1, source_target_pairs={{0,0},{1,32},{8,9},{9,41},{16,18},{17,50},{24,27},{25,59},{32,36},... | collective-permute-start | bytes 196616 | tf_op jit(solution)/shard_map/ppermute | solution.py:352
  38.3 6.1 %collective-permute-start.9 = (f32[2,128,128]{2,1,0:T(8,128)S(1)}, f32[2,128,128]{2,1,0:T(8,128)S(1)}, u32[]{:S(2)}, u32[]{:S(2)}) collective-permute-start(f32[2,128,128]{2,1,0:T(8,128)S(1)} %get-tuple-element.42), channel_id=1, source_target_pairs={{128,0},{136,8},{144,16},{152,24},{160,32},{168,40},{176,48},{184,... | collective-permute-start | bytes 393224 | tf_op jit(solution)/shard_map/ppermute | solution.py:361
  41.1 6.1 %collective-permute-start.8 = (f32[2,128,128]{2,1,0:T(8,128)S(1)}, f32[2,128,128]{2,1,0:T(8,128)S(1)}, u32[]{:S(2)}, u32[]{:S(2)}) collective-permute-start(f32[2,128,128]{2,1,0:T(8,128)S(1)} %get-tuple-element.42), channel_id=1, source_target_pairs={{64,0},{72,8},{80,16},{88,24},{96,32},{104,40},{112,48},{120,56},{... | collective-permute-start | bytes 393224 | tf_op jit(solution)/shard_map/ppermute | solution.py:361
  42.0 5.3 %collective-permute-start.10 = (f32[2,128,128]{2,1,0:T(8,128)S(1)}, f32[2,128,128]{2,1,0:T(8,128)S(1)}, u32[]{:S(2)}, u32[]{:S(2)}) collective-permute-start(f32[2,128,128]{2,1,0:T(8,128)S(1)} %get-tuple-element.42), channel_id=1, source_target_pairs={{192,0},{200,8},{208,16},{216,24},{224,32},{232,40},{240,48},{248,... | collective-permute-start | bytes 393224 | tf_op jit(solution)/shard_map/ppermute | solution.py:361
  48.1 0.7 collective-permute-start.15
  48.9 67.3 %copy-start.1 = (s32[2,1,8,1]{2,3,1,0:T(1,128)S(1)}, s32[2,1,8,1]{2,3,1,0:T(1,128)}, u32[]{:S(2)}) copy-start(s32[2,1,8,1]{2,3,1,0:T(1,128)} %param.3) | copy-start | bytes 196
  48.9 10.0 %collective-permute-start.17 = (f32[264,256]{1,0:T(8,128)S(1)}, f32[264,256]{1,0:T(8,128)S(1)}, u32[]{:S(2)}, u32[]{:S(2)}) collective-permute-start(f32[264,256]{1,0:T(8,128)S(1)} %fusion), channel_id=1, source_target_pairs={{0,48},{1,49}} | collective-permute-start | bytes 811016 | tf_op jit(solution)/shard_map/ppermute | solution.py:299
  55.6 5.6 %collective-permute-start.16 = (f32[264,256]{1,0:T(8,128)S(1)}, f32[264,256]{1,0:T(8,128)S(1)}, u32[]{:S(2)}, u32[]{:S(2)}) collective-permute-start(f32[264,256]{1,0:T(8,128)S(1)} %fusion), channel_id=1, source_target_pairs={{0,24},{1,25}} | collective-permute-start | bytes 811016 | tf_op jit(solution)/shard_map/ppermute | solution.py:299
  61.2 2.0 %collective-permute-start.19 = (f32[264,256]{1,0:T(8,128)S(1)}, f32[264,256]{1,0:T(8,128)S(1)}, u32[]{:S(2)}, u32[]{:S(2)}) collective-permute-start(f32[264,256]{1,0:T(8,128)S(1)} %add_add_fusion.4), channel_id=1, source_target_pairs={{24,16},{25,17},{48,40},{49,41}} | collective-permute-start | bytes 811016 | tf_op jit(solution)/shard_map/ppermute | solution.py:299
  61.9 12.5 %collective-permute-start.18 = (f32[264,256]{1,0:T(8,128)S(1)}, f32[264,256]{1,0:T(8,128)S(1)}, u32[]{:S(2)}, u32[]{:S(2)}) collective-permute-start(f32[264,256]{1,0:T(8,128)S(1)} %add_add_fusion.4), channel_id=1, source_target_pairs={{0,8},{1,9},{24,32},{25,33},{48,56},{49,57}} | collective-permute-start | bytes 811016 | tf_op jit(solution)/shard_map/ppermute | solution.py:299
  74.5 6.7 %collective-permute-start.22 = (f32[264,256]{1,0:T(8,128)S(1)}, f32[264,256]{1,0:T(8,128)S(1)}, u32[]{:S(2)}, u32[]{:S(2)}) collective-permute-start(f32[264,256]{1,0:T(8,128)S(1)} %add_add_fusion.3), channel_id=1, source_target_pairs={{0,128},{1,129},{8,136},{9,137},{16,144},{17,145},{24,152},{25,153... | collective-permute-start | bytes 811016 | tf_op jit(solution)/shard_map/ppermute | solution.py:299
  75.8 6.7 %collective-permute-start.21 = (f32[264,256]{1,0:T(8,128)S(1)}, f32[264,256]{1,0:T(8,128)S(1)}, u32[]{:S(2)}, u32[]{:S(2)}) collective-permute-start(f32[264,256]{1,0:T(8,128)S(1)} %add_add_fusion.3), channel_id=1, source_target_pairs={{0,192},{1,193},{8,200},{9,201},{16,208},{17,209},{24,216},{25,217... | collective-permute-start | bytes 811016 | tf_op jit(solution)/shard_map/ppermute | solution.py:299
  77.1 5.4 %collective-permute-start.20 = (f32[264,256]{1,0:T(8,128)S(1)}, f32[264,256]{1,0:T(8,128)S(1)}, u32[]{:S(2)}, u32[]{:S(2)}) collective-permute-start(f32[264,256]{1,0:T(8,128)S(1)} %add_add_fusion.3), channel_id=1, source_target_pairs={{0,64},{1,65},{8,72},{9,73},{16,80},{17,81},{24,88},{25,89},{32,96... | collective-permute-start | bytes 811016 | tf_op jit(solution)/shard_map/ppermute | solution.py:299
  78.5 7.4 %collective-permute-start.12 = (f32[4,256,128]{2,1,0:T(8,128)S(1)}, f32[4,256,128]{2,1,0:T(8,128)S(1)}, u32[]{:S(2)}, u32[]{:S(2)}) collective-permute-start(f32[4,256,128]{2,1,0:T(8,128)S(1)} %broadcast_select_fusion), channel_id=1, source_target_pairs={{0,6},{1,7},{8,14},{9,15},{16,22},{17,23},{24,30},{25,31},{32,38},... | collective-permute-start | bytes 1572872 | tf_op jit(solution)/shard_map/ppermute | solution.py:299
  79.8 7.4 %collective-permute-start.13 = (f32[4,256,128]{2,1,0:T(8,128)S(1)}, f32[4,256,128]{2,1,0:T(8,128)S(1)}, u32[]{:S(2)}, u32[]{:S(2)}) collective-permute-start(f32[4,256,128]{2,1,0:T(8,128)S(1)} %broadcast_select_fusion), channel_id=1, source_target_pairs={{0,4},{1,5},{8,12},{9,13},{16,20},{17,21},{24,28},{25,29},{32,36},... | collective-permute-start | bytes 1572872 | tf_op jit(solution)/shard_map/ppermute | solution.py:299
  81.1 13.1 %collective-permute-start.11 = (f32[4,256,128]{2,1,0:T(8,128)S(1)}, f32[4,256,128]{2,1,0:T(8,128)S(1)}, u32[]{:S(2)}, u32[]{:S(2)}) collective-permute-start(f32[4,256,128]{2,1,0:T(8,128)S(1)} %broadcast_select_fusion), channel_id=1, source_target_pairs={{0,2},{1,3},{8,10},{9,11},{16,18},{17,19},{24,26},{25,27},{32,34},... | collective-permute-start | bytes 1572872 | tf_op jit(solution)/shard_map/ppermute | solution.py:299
  82.6 27.8 %collective-permute-start.25 = (f32[264,256]{1,0:T(8,128)S(1)}, f32[264,256]{1,0:T(8,128)S(1)}, u32[]{:S(2)}, u32[]{:S(2)}) collective-permute-start(f32[264,256]{1,0:T(8,128)S(1)} %add_add_fusion.2), channel_id=1, source_target_pairs={{0,4},{1,5},{8,12},{9,13},{16,20},{17,21},{24,28},{25,29},{32,36},... | collective-permute-start | bytes 811016 | tf_op jit(solution)/shard_map/ppermute | solution.py:299
  83.9 26.5 %collective-permute-start.24 = (f32[264,256]{1,0:T(8,128)S(1)}, f32[264,256]{1,0:T(8,128)S(1)}, u32[]{:S(2)}, u32[]{:S(2)}) collective-permute-start(f32[264,256]{1,0:T(8,128)S(1)} %add_add_fusion.2), channel_id=1, source_target_pairs={{0,6},{1,7},{8,14},{9,15},{16,22},{17,23},{24,30},{25,31},{32,38},... | collective-permute-start | bytes 811016 | tf_op jit(solution)/shard_map/ppermute | solution.py:299
  85.9 24.6 %collective-permute-start.23 = (f32[264,256]{1,0:T(8,128)S(1)}, f32[264,256]{1,0:T(8,128)S(1)}, u32[]{:S(2)}, u32[]{:S(2)}) collective-permute-start(f32[264,256]{1,0:T(8,128)S(1)} %add_add_fusion.2), channel_id=1, source_target_pairs={{0,2},{1,3},{8,10},{9,11},{16,18},{17,19},{24,26},{25,27},{32,34},... | collective-permute-start | bytes 811016 | tf_op jit(solution)/shard_map/ppermute | solution.py:299
  94.3 22.0 %collective-permute-start.14 = (f32[4,256,128]{2,1,0:T(8,128)S(1)}, f32[4,256,128]{2,1,0:T(8,128)S(1)}, u32[]{:S(2)}, u32[]{:S(2)}) collective-permute-start(f32[4,256,128]{2,1,0:T(8,128)S(1)} %add_add_fusion), channel_id=1, source_target_pairs={{0,1},{1,0},{2,3},{3,2},{4,5},{5,4},{6,7},{7,6},{8,9},{9,8},{10,11... | collective-permute-start | bytes 1572872 | tf_op jit(solution)/shard_map/ppermute | solution.py:368
  110.5 6.8 %collective-permute-start.26 = (f32[264,256]{1,0:T(8,128)S(1)}, f32[264,256]{1,0:T(8,128)S(1)}, u32[]{:S(2)}, u32[]{:S(2)}) collective-permute-start(f32[264,256]{1,0:T(8,128)S(1)} %add_add_fusion.1), channel_id=1, source_target_pairs={{0,1},{1,0},{2,3},{3,2},{4,5},{5,4},{6,7},{7,6},{8,9},{9,8},{10,11... | collective-permute-start | bytes 811016 | tf_op jit(solution)/shard_map/ppermute | solution.py:337
Sparse Core Ops, SparseCore 0:
  48.2 59.7 all-gather.2

commit v2 on v1

v2 whole, which is shorter than its diff:
```python
import jax
import jax.numpy as jnp
from jax import lax
from jax.experimental import pallas as pl
from jax.experimental.pallas import tpu as pltpu
from jax.sharding import PartitionSpec as P

W = 256
NB = 32
HIGHEST = lax.Precision.HIGHEST
F32 = jnp.float32
BF16 = jnp.bfloat16


def dot_nn(a, b):
    return lax.dot_general(a, b, (((1,), (0,)), ((), ())), precision=HIGHEST, preferred_element_type=F32)


def dot_nt(a, b):
    return lax.dot_general(a, b, (((1,), (1,)), ((), ())), precision=HIGHEST, preferred_element_type=F32)


def dot_tn(a, b):
    return lax.dot_general(a, b, (((0,), (0,)), ((), ())), precision=HIGHEST, preferred_element_type=F32)


def split3(x):
    hi = x.astype(BF16)
    rest = x - hi.astype(F32)
    mid = rest.astype(BF16)
    low = (rest - mid.astype(F32)).astype(BF16)
    return hi, mid, low


def eliminate(rows):
    sub = lax.broadcasted_iota(jnp.int32, (8, 384), 0)
    for t in range(4):
        x = rows[t]
        head = x[:, 0:128]
        cols = [jnp.broadcast_to(head[:, 8 * t + k : 8 * t + k + 1], (8, 128)) for k in range(8)]
        below = {
            g: [
                jnp.broadcast_to(rows[g][:, 8 * t + k : 8 * t + k + 1], (8, 128))
                for k in range(8)
            ]
            for g in range(t + 1, 4)
        }
        a = {
            (i, k): jnp.broadcast_to(cols[k][i : i + 1, :], (8, 128))
            for k in range(8)
            for i in range(k, 8)
        }
        r = [jnp.broadcast_to(x[k : k + 1, :], (8, 384)) for k in range(8)]
        for k in range(8):
            scale = lax.rsqrt(a[k, k])
            wide = jnp.concatenate([scale] * 3, axis=1)
            r[k] = r[k] * wide
            for g in below:
                below[g][k] = below[g][k] * scale
            l = {i: a[i, k] * scale for i in range(k + 1, 8)}
            for i in range(k + 1, 8):
                for j in range(k + 1, i + 1):
                    a[i, j] = a[i, j] - l[i] * l[j]
                r[i] = r[i] - jnp.concatenate([l[i]] * 3, axis=1) * r[k]
                for g in below:
                    below[g][i] = below[g][i] - l[i] * below[g][k]
        out = r[0]
        for k in range(1, 8):
            out = jnp.where(sub == k, r[k], out)
        rows[t] = out
        for g in below:
            acc = rows[g]
            for k in range(8):
                acc = acc - jnp.concatenate([below[g][k]] * 3, axis=1) * r[k]
            rows[g] = acc
    return rows


def factor_block(g_ref, u_ref, v_ref):
    lane = lax.broadcasted_iota(jnp.int32, (NB, W), 1)
    row = lax.broadcasted_iota(jnp.int32, (NB, W), 0)
    eye = (
        lax.broadcasted_iota(jnp.int32, (NB, 128), 0)
        == lax.broadcasted_iota(jnp.int32, (NB, 128), 1)
    ).astype(F32)
    tail = lax.broadcasted_iota(jnp.int32, (W - NB, W), 1)

    def panel(p, carry):
        x = jnp.concatenate([g_ref[0:NB, :], eye], axis=1)
        rows = eliminate([x[8 * t : 8 * t + 8] for t in range(4)])
        r = jnp.concatenate(rows, axis=0)
        shifted = pltpu.roll(r, 384 - NB, 1)[:, 0:W]
        at = pl.multiple_of(p * NB, NB)
        u_ref[pl.ds(at, NB), :] = jnp.where(
            lane >= row + at, pltpu.roll(r[:, 0:W], at, 1), 0.0
        )
        v_ref[pl.ds(at, NB), :] = jnp.where(
            lane <= row + at, pltpu.roll(shifted, at + NB, 1), 0.0
        )
        hi, mid, low = split3(shifted)
        left = jnp.concatenate([hi, hi, mid, mid, hi, low], axis=0)
        right = jnp.concatenate([hi, mid, hi, mid, low, hi], axis=0)
        prod = lax.dot_general(
            left, right, (((0,), (0,)), ((), ())), preferred_element_type=F32
        )
        old = pltpu.roll(g_ref[NB:W, :], W - NB, 1)
        g_ref[0 : W - NB, :] = jnp.where(tail < W - NB, old, 0.0) - prod[0 : W - NB, :]
        return carry

    lax.fori_loop(0, W // NB, panel, 0)


H = W // 2


def half_masks():
    return (
        lax.broadcasted_iota(jnp.int32, (H, H), 0),
        lax.broadcasted_iota(jnp.int32, (H, H), 1),
    )


def unpack(packed):
    below, right = half_masks()
    mixed = packed[0:H, 0:H]
    flipped = jnp.transpose(mixed)
    first = jnp.where(below >= right, mixed, flipped)
    second = jnp.where(below < right, mixed, flipped)
    second = jnp.where(below == right, packed[H : H + 1, 0:H], second)
    corner = packed[0:H, H:W]
    top = jnp.concatenate([first, jnp.transpose(corner)], axis=1)
    return jnp.concatenate([top, jnp.concatenate([corner, second], axis=1)], axis=0)


def factor_kernel(
    mine_ref, other_ref, slab_ref, twin_ref, panel_ref, row_ref, g_ref, u_ref, v0_ref, v1_ref
):
    r, c = lax.axis_index("row"), lax.axis_index("col")
    even = lax.rem(c, 2) == 0
    left = [jnp.where(even, mine_ref[i], other_ref[i]) for i in range(2)]
    right = [jnp.where(even, other_ref[i], mine_ref[i]) for i in range(2)]
    g_ref[...] = unpack(left[0])
    factor_block(g_ref, u_ref, v0_ref)
    low = jnp.concatenate(
        [jnp.transpose(left[1][0:H, 0:H]), jnp.transpose(left[1][0:H, H:W])], axis=1
    )
    a01 = jnp.concatenate([right[0][0:H], low], axis=0)
    v0 = v0_ref[...]
    pt = dot_nn(v0, a01)
    p10 = jnp.transpose(pt)
    g_ref[...] = unpack(right[1]) - dot_tn(pt, pt)
    first_u = jnp.transpose(u_ref[...])
    factor_block(g_ref, u_ref, v1_ref)
    v1 = v1_ref[...]

    raws = []
    for s in range(2):
        parts = [
            jnp.where(even == (s == 0), slab_ref[i], twin_ref[i]) for i in range(4)
        ]
        raws.append(
            jnp.concatenate(
                [jnp.concatenate(parts[2 * m : 2 * m + 2], axis=1) for m in range(2)], axis=0
            )
        )
    first = dot_nt(raws[0], v0)
    second = dot_nt(raws[1] - dot_nn(first, pt), v1)
    panel_ref[...] = jnp.where(c == 0, first, second)
    back1 = dot_nn(second, v1)
    row_ref[:, 0:W] = dot_nn(first - dot_nn(back1, p10), v0)
    row_ref[:, W : 2 * W] = back1

    @pl.when(r == 0)
    def _():
        row_ref[0:W, 0:W] = -v0
        row_ref[0:W, W : 2 * W] = jnp.zeros((W, W), F32)
        panel_ref[0:W, :] = jnp.where(c == 0, first_u, pt)

    @pl.when(r == 1)
    def _():
        row_ref[0:W, 0:W] = dot_nn(dot_nn(v1, p10), v0)
        row_ref[0:W, W : 2 * W] = -v1
        panel_ref[0:W, :] = jnp.where(c == 0, p10, jnp.transpose(u_ref[...]))


def factor_pair(mine, other, slab, twin):
    return pl.pallas_call(
        factor_kernel,
        out_shape=[
            jax.ShapeDtypeStruct((2 * W, W), F32),
            jax.ShapeDtypeStruct((2 * W, 2 * W), F32),
        ],
        scratch_shapes=[pltpu.VMEM((W, W), F32)] * 4,
        compiler_params=pltpu.CompilerParams(vmem_limit_bytes=24 * 1024 * 1024),
        name="factor_pair",
    )(mine, other, slab, twin)


def extract_kernel(pattern_ref, front_ref, slab_ref, packed_ref, *piece_refs):
    r, c = lax.axis_index("row"), lax.axis_index("col")
    parts = []
    for m in range(2):
        keep = pattern_ref[m, 0] > 0
        for h in range(2):
            part = jnp.where(keep, front_ref[m * W : m * W + W, h, :], 0.0)
            slab_ref[2 * m + h] = part
            piece_refs[2 * m + h][...] = part
            parts.append(part)
    below, right = half_masks()
    packed_ref[...] = jnp.zeros((H + 8, W), F32)

    @pl.when(r == c)
    def _():
        second = parts[1][H:W]
        diagonal = jnp.sum(jnp.where(below == right, second, 0.0), axis=0, keepdims=True)
        packed_ref[0:H, 0:H] = jnp.where(below >= right, parts[0][0:H], second)
        packed_ref[0:H, H:W] = parts[0][H:W]
        packed_ref[H : H + 8, 0:H] = jnp.broadcast_to(diagonal, (8, H))

    @pl.when(r < c)
    def _():
        packed_ref[0:H, 0:H] = parts[0][0:H]
        packed_ref[0:H, H:W] = parts[1][0:H]

    @pl.when(r > c)
    def _():
        packed_ref[0:H, 0:H] = parts[1][0:H]
        packed_ref[0:H, H:W] = parts[1][H:W]


def extract(pattern, view):
    return pl.pallas_call(
        extract_kernel,
        grid=(1,),
        in_specs=[
            pl.BlockSpec(memory_space=pltpu.SMEM),
            pl.BlockSpec((2 * W, 8, 128), lambda i: (0, 0, 0)),
        ],
        out_specs=[pl.BlockSpec(memory_space=pltpu.VMEM)] * 6,
        out_shape=[
            jax.ShapeDtypeStruct((4, W, 128), F32),
            jax.ShapeDtypeStruct((H + 8, W), F32),
        ]
        + [jax.ShapeDtypeStruct((W, 128), F32)] * 4,
        compiler_params=pltpu.CompilerParams(vmem_limit_bytes=56 * 1024 * 1024),
        name="extract",
    )(pattern, view)


FAR = ((0, 1, 7, 2), (4, 3, 5, 6))


def update_kernel(
    pattern_ref, front_hbm, q_hbm, panel_hbm, row_hbm, out_hbm,
    front_ref, q_ref, panel_ref, row_ref, out_ref, front_sem, q_sem, row_sem, out_sem,
):
    r, c = lax.axis_index("row"), lax.axis_index("col")
    x = r // 8
    q_copies, front_copies, out_copies = [], [], []

    def begin(source, target, sem):
        copy = pltpu.make_async_copy(source, target, sem)
        copy.start()
        return copy

    row_copy = begin(row_hbm, row_ref, row_sem.at[0])
    for m in range(2):
        for h in range(2):
            for s in range(2):
                i = 4 * m + 2 * h + s
                at = lax.rem(c + FAR[s][2 * m + h], 8)
                q_copies.append(begin(q_hbm.at[at], q_ref.at[i], q_sem.at[i]))
    panel_copy = begin(panel_hbm, panel_ref, row_sem.at[1])
    for m in range(2):
        half = pl.ds(m * 4096, 4096)
        front_copies.append(begin(front_hbm.at[half], front_ref.at[half], front_sem.at[m]))
        out_copies.append(
            pltpu.make_async_copy(out_ref.at[half], out_hbm.at[half], out_sem.at[m])
        )
    row_copy.wait()
    for m in range(2):
        place = r + 32 * m
        row = row_ref[m * W : m * W + W, :]
        scale, parts = [], []
        for n in range(8):
            if m == 0 and n % 4 == 0:
                for copy in q_copies[n : n + 4]:
                    copy.wait()
            j = 4 * (n // 4)
            near = lax.rem(n % 4 - x + 4, 4)
            raw = jnp.concatenate([q_ref[j + i, near] for i in (0, 2, 1, 3)], axis=1)
            prod = dot_nt(row, raw)
            keep = jnp.logical_and(
                pattern_ref[m, n] > 0, jnp.logical_and(place > 1, c + 8 * n > 1)
            )
            parts += [prod[:, 0:128], prod[:, 128:256]]
            scale.append(jnp.broadcast_to(jnp.where(keep, 1.0, 0.0), (2, 128)))
        scale = jnp.concatenate(scale, axis=0)[None]
        moved = jnp.swapaxes(jnp.stack(parts), 0, 1)
        half = pl.ds(4096 * m, 4096)
        front_copies[m].wait()
        old = front_ref[half, :].reshape(W, 16, 128)
        out_ref[half, :] = (old * scale - moved).reshape(4096, 128)
        if m == 0:
            panel_copy.wait()

        @pl.when(c < 2)
        def _():
            for h in range(2):
                out_ref[pl.ds(4096 * m + h, W, stride=16), :] = panel_ref[
                    m * W : m * W + W, 128 * h : 128 * h + 128
                ]

        out_copies[m].start()
    for copy in out_copies:
        copy.wait()


def update(pattern, view, gathered, panel, row):
    hbm = pl.BlockSpec(memory_space=pl.ANY)
    return pl.pallas_call(
        update_kernel,
        in_specs=[pl.BlockSpec(memory_space=pltpu.SMEM)] + [hbm] * 4,
        out_specs=hbm,
        out_shape=jax.ShapeDtypeStruct((8192, 128), F32),
        scratch_shapes=[
            pltpu.VMEM((8192, 128), F32),
            pltpu.VMEM((8, 4, W, 128), F32),
            pltpu.VMEM((2 * W, W), F32),
            pltpu.VMEM((2 * W, 2 * W), F32),
            pltpu.VMEM((8192, 128), F32),
            pltpu.SemaphoreType.DMA((2,)),
            pltpu.SemaphoreType.DMA((8,)),
            pltpu.SemaphoreType.DMA((2,)),
            pltpu.SemaphoreType.DMA((2,)),
        ],
        compiler_params=pltpu.CompilerParams(vmem_limit_bytes=52 * 1024 * 1024),
        name="update",
    )(pattern, view, gathered, panel, row)


BOTH = ("row", "col")


def device(x, z, c):
    return (x * 8 + z) * 8 + c


def around(value, axis, moves):
    return [lax.ppermute(value, axis, pairs) for pairs in moves]


def on_device(front, pattern):
    row_place = lax.axis_index("row")
    col_place = lax.axis_index("col")
    z_place = row_place % 8
    view = front.reshape(8192, 128)
    present = pattern.reshape(2, 8)
    slab, packed, *pieces = extract(present, front.reshape(512, 16, 128))

    at_first = (z_place == 0) | (z_place == 3) | (z_place == 6)
    at_second = (z_place == 1) | (z_place == 4) | (z_place == 7)
    steps = around(packed, BOTH, [
        [(device(0, z, s), device(0, (z + d) % 8, s)) for z in range(2) for s in range(2)]
        for d in (3, 6)
    ])
    source = (row_place < 2) & (col_place < 2)
    held = jnp.where(source, packed, 0.0) + steps[0] + steps[1]
    pieces, held = lax.optimization_barrier((pieces, held))
    plus, minus = around(held, BOTH, [
        [(device(0, z, s), device(0, (z + 1) % 8, s)) for z in (0, 3, 6, 1, 4, 7) for s in range(2)],
        [(device(0, z, s), device(0, z - 1, s)) for z in (3, 6, 4, 7) for s in range(2)],
    ])
    either = plus + minus
    diag = jnp.stack([
        jnp.where(at_first, held, jnp.where(at_second, plus, minus)),
        jnp.where(at_first, either, jnp.where(at_second, held, plus)),
    ])
    diag = jnp.where((row_place < 8) & (col_place < 2), diag, 0.0)
    share = 0.0
    for k in range(4):
        pairs = [
            (device(x, z, s), device(x, (z + FAR[s][k]) % 8, z))
            for x in range(4)
            for z in range(8)
            for s in range(2)
        ]
        share = share + lax.ppermute(pieces[k], BOTH, pairs)
    line = [share]
    for d in range(1, 4):
        pairs = [
            (((x + d) % 4) * 8 + z, x * 8 + z) for x in range(4) for z in range(8)
        ]
        line.append(lax.ppermute(share, "row", pairs))
    line = jnp.stack(line)
    line, diag = lax.optimization_barrier((line, diag))
    groups = [[x * 8 + z for z in range(8)] for x in range(4)]
    gathered = lax.all_gather(line, "row", axis_index_groups=groups)

    steps = around(diag, BOTH, [
        [(device(0, z, s), device(x, z, s)) for z in range(8) for s in range(2)]
        for x in (1, 3, 2)
    ])
    diag = diag + steps[0] + steps[1] + steps[2]
    fan_y = [[(s, s + y) for s in range(2)] for y in (2, 6, 4)]
    steps = around(slab, "col", fan_y)
    slab = jnp.where(col_place < 2, slab, steps[0] + steps[1] + steps[2])
    slab, diag = lax.optimization_barrier((slab, diag))
    steps = around(diag, "col", fan_y)
    diag = diag + steps[0] + steps[1] + steps[2]
    swap = [(c, c ^ 1) for c in range(8)]
    other = lax.ppermute(diag, "col", swap)

    twin = lax.ppermute(slab, "col", swap)

    panel, row = factor_pair(diag, other, slab, twin)
    out = update(present, view, gathered, panel, row)
    return out.reshape(2, 1, 256, 8, 1, 256)


def solution(mesh):
    placed = (P(None, "row", None, None, "col", None), P(None, "row", None, "col"))
    return jax.shard_map(
        on_device,
        mesh=mesh,
        in_specs=placed,
        out_specs=P(None, "row", None, None, "col", None),
        check_vma=False,
    )
```

time: 164 us -> 135 us (0.82)
  starting transfers between devices: 72.6 us -> 49.8 us
  local copies, waits for them, and re-layouts: 3.49 us -> 0.01 us
    ppermute x1, starting transfers between devices: 16.1 us -> 2.47 us  [on_device(): twin = lax.ppermute(slab, 'col', swap)]
    ppermute x25 -> x20, starting transfers between devices: 50.8 us -> 45.1 us  [the longest x13 29 us: around(): return [lax.ppermute(value, axis, pairs) for pairs in moves]]
    ppermute x1, starting transfers between devices: 5.67 us -> 2.2 us  [on_device(): other = lax.ppermute(diag, 'col', swap)]
    unnamed x4, local copies, waits for them, and re-layouts: 2.2 us -> 0.01 us
    ppermute x25 -> x20, waiting for transfers between devices: 29.5 us -> 28 us  [the longest x13 22.2 us: around(): return [lax.ppermute(value, axis, pairs) for pairs in moves]]
  transfers between devices with their start and end apart: 28 -> 23, of which waited for: 10 -> 8; matrix products, arithmetic and copies ran while one was open for 1% -> 0% of each run, Pallas kernels for 12% -> 18%
where the time goes in v2:
time: 135 us; the launch traced here: 134 us
  starting transfers between devices  49.8 us (37%)
  Pallas kernels  39 us (29%)
  waiting for transfers between devices  29.2 us (22%)
  between operations  13.7 us (10%)
  other arithmetic  2.12 us (2%)
    ppermute x13, starting transfers between devices, around(): return [lax.ppermute(value, axis, pairs) for pairs in moves]  29 us
    pallas_call x1, Pallas kernels, factor_pair(): pl.pallas_call(factor_kernel, out_shape=[jax.ShapeDtypeStruct((2 * W, W),...  24.2 us
    ppermute x13, waiting for transfers between devices, around(): return [lax.ppermute(value, axis, pairs) for pairs in moves]  22.2 us
    ppermute x4, starting transfers between devices, on_device(): share = share + lax.ppermute(pieces[k], BOTH, pairs)  13.3 us
    pallas_call x1, Pallas kernels, update(): pl.pallas_call(update_kernel, in_specs=[pl.BlockSpec(memory_space=pltpu.S...  11.8 us
    ppermute x3, waiting for transfers between devices, on_device(): line.append(lax.ppermute(share, 'row', pairs))  4.88 us
    pallas_call x1, Pallas kernels, extract(): pl.pallas_call(extract_kernel, grid=(1,), in_specs=[pl.BlockSpec(memory_s...  3.04 us
    ppermute x3, starting transfers between devices, on_device(): line.append(lax.ppermute(share, 'row', pairs))  2.74 us
  transfers between devices with their start and end apart: 23, of which 8 were waited for; matrix products, arithmetic and copies ran while one was open for 0% of the time, Pallas kernels for 18%

profile of v2, /device:TPU:1, one launch (start us, length us, event | category | flops | bytes accessed | tf_op | source)
XLA Modules:
  0.0 133.8 jit_solution(7131209852136102381)
XLA Ops:
  6.5 0.0 all-gather.3.cloned.1.call-start
  6.5 3.0 %extract.1 = (f32[4,256,128]{2,1,0:T(8,128)}, f32[136,256]{1,0:T(8,128)}, f32[256,128]{1,0:T(8,128)}, f32[256,128]{1,0:T(8,128)}, f32[256,128]{1,0:T(8,128)}, /*index=5*/f32[256,128]{1,0:T(8,128)}) custom-call(s32[2,8]{1,0:T(2,128)} %bitcast.13, f32[512,16,128]{2,1,0:T(8,128)} %bitcast.15), custom_call_target="tpu_custom_call" | custom-call | tf_op jit(solution)/shard_map/extract/pallas_call | solution.py:232
  9.6 0.0 copy-start.1
  9.6 8.9 %collective-permute-start.1 = (f32[136,256]{1,0:T(8,128)}, f32[136,256]{1,0:T(8,128)S(1)}, u32[]{:S(2)}, u32[]{:S(2)}) collective-permute-start(f32[136,256]{1,0:T(8,128)} %get-tuple-element.26), channel_id=1, source_target_pairs={{0,48},{1,49},{8,56},{9,57}} | collective-permute-start | bytes 417800 | tf_op jit(solution)/shard_map/ppermute | solution.py:350
  18.5 1.3 collective-permute-start
  19.8 4.9 %collective-permute-done.1 = f32[136,256]{1,0:T(8,128)S(1)} collective-permute-done((f32[136,256]{1,0:T(8,128)}, f32[136,256]{1,0:T(8,128)S(1)}, u32[]{:S(2)}, u32[]{:S(2)}) %collective-permute-start.1) | collective-permute-done | bytes 139296 | tf_op jit(solution)/shard_map/ppermute | solution.py:350
  24.7 0.0 collective-permute-done
  24.7 0.9 add_add_fusion.2
  25.6 8.8 %collective-permute-start.2 = (f32[256,128]{1,0:T(8,128)}, f32[256,128]{1,0:T(8,128)S(1)}, u32[]{:S(2)}, u32[]{:S(2)}) collective-permute-start(f32[256,128]{1,0:T(8,128)} %get-tuple-element.27), channel_id=1, source_target_pairs={{0,0},{1,32},{8,9},{9,41},{16,18},{17,50},{24,27},{25,59},{32,36},... | collective-permute-start | bytes 393224 | tf_op jit(solution)/shard_map/ppermute | solution.py:388
  34.4 1.3 collective-permute-start.3
  35.7 1.9 %collective-permute-start.4 = (f32[256,128]{1,0:T(8,128)}, f32[256,128]{1,0:T(8,128)S(1)}, u32[]{:S(2)}, u32[]{:S(2)}) collective-permute-start(f32[256,128]{1,0:T(8,128)} %get-tuple-element.29), channel_id=1, source_target_pairs={{0,56},{1,40},{8,1},{9,49},{16,10},{17,58},{24,19},{25,3},{32,28},... | collective-permute-start | bytes 393224 | tf_op jit(solution)/shard_map/ppermute | solution.py:388
  37.7 1.3 collective-permute-start.5
  39.0 0.7 collective-permute-start.10
  39.7 0.0 collective-permute-done.2
  39.7 1.9 %collective-permute-start.9 = (f32[136,256]{1,0:T(8,128)S(1)}, f32[136,256]{1,0:T(8,128)S(1)}, u32[]{:S(2)}, u32[]{:S(2)}) collective-permute-start(f32[136,256]{1,0:T(8,128)S(1)} %add_add_fusion.2), channel_id=1, source_target_pairs={{0,8},{1,9},{24,32},{25,33},{48,56},{49,57},{8,16},{9,17},{32,40},... | collective-permute-start | bytes 417800 | tf_op jit(solution)/shard_map/ppermute | solution.py:350
  41.6 0.0 collective-permute-done.3
  41.6 0.9 collective-permute-done.4
  42.5 0.0 collective-permute-done.5
  42.6 0.1 collective-permute-start.8
  42.7 0.1 collective-permute-start.7
  42.8 2.6 %collective-permute-start.6 = (f32[256,128]{1,0:T(8,128)S(1)}, f32[256,128]{1,0:T(8,128)S(1)}, u32[]{:S(2)}, u32[]{:S(2)}) collective-permute-start(f32[256,128]{1,0:T(8,128)S(1)} %add_add_fusion.3), channel_id=1, source_target_pairs={{64,0},{72,8},{80,16},{88,24},{96,32},{104,40},{112,48},{120,56},{... | collective-permute-start | bytes 393224 | tf_op jit(solution)/shard_map/ppermute | solution.py:394
  45.4 0.0 collective-permute-done.10
  45.4 1.3 %collective-permute-done.9 = f32[136,256]{1,0:T(8,128)S(1)} collective-permute-done((f32[136,256]{1,0:T(8,128)S(1)}, f32[136,256]{1,0:T(8,128)S(1)}, u32[]{:S(2)}, u32[]{:S(2)}) %collective-permute-start.9) | collective-permute-done | bytes 139296 | tf_op jit(solution)/shard_map/ppermute | solution.py:350
  46.8 4.9 %collective-permute-done.8 = f32[256,128]{1,0:T(8,128)S(1)} collective-permute-done((f32[256,128]{1,0:T(8,128)S(1)}, f32[256,128]{1,0:T(8,128)S(1)}, u32[]{:S(2)}, u32[]{:S(2)}) %collective-permute-start.8) | collective-permute-done | bytes 131104 | tf_op jit(solution)/shard_map/ppermute | solution.py:394
  51.7 0.0 collective-permute-done.7
  51.7 0.0 collective-permute-done.6
  51.7 0.0 copy-start
  51.7 0.8 pad_maximum_fusion
  52.5 0.0 all-gather.3.cloned.1.call-update
  52.5 1.3 collective-permute-start.13
  53.9 1.3 collective-permute-start.12
  55.2 1.3 collective-permute-start.11
  56.5 1.9 %collective-permute-start.16 = (f32[2,136,256]{2,1,0:T(8,128)S(1)}, f32[2,136,256]{2,1,0:T(8,128)S(1)}, u32[]{:S(2)}, u32[]{:S(2)}) collective-permute-start(f32[2,136,256]{2,1,0:T(8,128)S(1)} %maximum_select_fusion), channel_id=1, source_target_pairs={{0,128},{1,129},{8,136},{9,137},{16,144},{17,145},{24,152},{25,153... | collective-permute-start | bytes 835592 | tf_op jit(solution)/shard_map/ppermute | solution.py:350
  58.4 3.3 %collective-permute-start.15 = (f32[2,136,256]{2,1,0:T(8,128)S(1)}, f32[2,136,256]{2,1,0:T(8,128)S(1)}, u32[]{:S(2)}, u32[]{:S(2)}) collective-permute-start(f32[2,136,256]{2,1,0:T(8,128)S(1)} %maximum_select_fusion), channel_id=1, source_target_pairs={{0,192},{1,193},{8,200},{9,201},{16,208},{17,209},{24,216},{25,217... | collective-permute-start | bytes 835592 | tf_op jit(solution)/shard_map/ppermute | solution.py:350
  61.7 2.3 %collective-permute-done.13 = f32[4,256,128]{2,1,0:T(8,128)S(1)} collective-permute-done((f32[4,256,128]{2,1,0:T(8,128)}, f32[4,256,128]{2,1,0:T(8,128)S(1)}, u32[]{:S(2)}, u32[]{:S(2)}) %collective-permute-start.13) | collective-permute-done | bytes 524320 | tf_op jit(solution)/shard_map/ppermute | solution.py:350
  64.1 1.6 %collective-permute-start.14 = (f32[2,136,256]{2,1,0:T(8,128)S(1)}, f32[2,136,256]{2,1,0:T(8,128)S(1)}, u32[]{:S(2)}, u32[]{:S(2)}) collective-permute-start(f32[2,136,256]{2,1,0:T(8,128)S(1)} %maximum_select_fusion), channel_id=1, source_target_pairs={{0,64},{1,65},{8,72},{9,73},{16,80},{17,81},{24,88},{25,89},{32,96... | collective-permute-start | bytes 835592 | tf_op jit(solution)/shard_map/ppermute | solution.py:350
  65.7 0.0 collective-permute-done.12
  65.7 9.6 %collective-permute-done.11 = f32[4,256,128]{2,1,0:T(8,128)S(1)} collective-permute-done((f32[4,256,128]{2,1,0:T(8,128)}, f32[4,256,128]{2,1,0:T(8,128)S(1)}, u32[]{:S(2)}, u32[]{:S(2)}) %collective-permute-start.11) | collective-permute-done | bytes 524320 | tf_op jit(solution)/shard_map/ppermute | solution.py:350
  75.3 0.0 copy-done.1
  75.3 0.1 add_select_fusion.slab_ref
  75.4 0.0 collective-permute-done.16
  75.4 0.0 collective-permute-done.15
  75.4 0.0 collective-permute-done.14
  75.4 0.1 add_add_fusion.1
  75.5 1.3 collective-permute-start.19
  76.8 1.3 collective-permute-start.18
  78.1 2.9 %collective-permute-start.17 = (f32[2,136,256]{2,1,0:T(8,128)S(1)}, f32[2,136,256]{2,1,0:T(8,128)S(1)}, u32[]{:S(2)}, u32[]{:S(2)}) collective-permute-start(f32[2,136,256]{2,1,0:T(8,128)S(1)} %add_add_fusion.1), channel_id=1, source_target_pairs={{0,2},{1,3},{8,10},{9,11},{16,18},{17,19},{24,26},{25,27},{32,34},... | collective-permute-start | bytes 835592 | tf_op jit(solution)/shard_map/ppermute | solution.py:350
  81.0 2.5 %collective-permute-start.21 = (f32[4,256,128]{2,1,0:T(8,128)S(1)}, f32[4,256,128]{2,1,0:T(8,128)S(1)}, u32[]{:S(2)}, u32[]{:S(2)}) collective-permute-start(f32[4,256,128]{2,1,0:T(8,128)S(1)} %add_select_fusion.slab_ref), channel_id=1, source_target_pairs={{0,1},{1,0},{2,3},{3,2},{4,5},{5,4},{6,7},{7,6},{8,9},{9,8},{10,11... | collective-permute-start | bytes 1572872 | tf_op jit(solution)/shard_map/ppermute | solution.py:414
  83.5 0.0 collective-permute-done.19
  83.5 0.0 collective-permute-done.18
  83.5 4.0 %collective-permute-done.17 = f32[2,136,256]{2,1,0:T(8,128)S(1)} collective-permute-done((f32[2,136,256]{2,1,0:T(8,128)S(1)}, f32[2,136,256]{2,1,0:T(8,128)S(1)}, u32[]{:S(2)}, u32[]{:S(2)}) %collective-permute-start.17) | collective-permute-done | bytes 278560 | tf_op jit(solution)/shard_map/ppermute | solution.py:350
  87.5 0.1 add_add_fusion.mine_ref
  87.6 2.2 %collective-permute-start.20 = (f32[2,136,256]{2,1,0:T(8,128)S(1)}, f32[2,136,256]{2,1,0:T(8,128)S(1)}, u32[]{:S(2)}, u32[]{:S(2)}) collective-permute-start(f32[2,136,256]{2,1,0:T(8,128)S(1)} %add_add_fusion.mine_ref), channel_id=1, source_target_pairs={{0,1},{1,0},{2,3},{3,2},{4,5},{5,4},{6,7},{7,6},{8,9},{9,8},{10,11... | collective-permute-start | bytes 835592 | tf_op jit(solution)/shard_map/ppermute | solution.py:412
  89.8 0.0 collective-permute-done.21.twin_ref
  89.8 1.2 collective-permute-done.20.other_ref
  91.0 24.2 %factor_pair.1 = (f32[512,256]{1,0:T(8,128)S(1)}, f32[512,512]{1,0:T(8,128)S(1)}) custom-call(f32[2,136,256]{2,1,0:T(8,128)S(1)} %add_add_fusion.mine_ref, f32[2,136,256]{2,1,0:T(8,128)S(1)} %collective-permute-done.20.other_ref, f32[4,256,128]{2,1,0:T(8,128)S(1)} %add_select_fusion.slab_ref, f32[4,256,128]{2,1,0:T(8,128)S(1)} %collective-permute-done.21.twin_ref), custom_call_target="tpu_custom_call" | custom-call | tf_op jit(solution)/shard_map/factor_pair/pallas_call | solution.py:187
  115.2 0.0 all-gather.3.cloned.1.call-done
  115.2 0.0 copy-done
  115.2 11.8 %update.1 = f32[8192,128]{1,0:T(8,128)} custom-call(s32[2,8]{1,0:T(2,128)S(1)} %bitcast.14, f32[8192,128]{1,0:T(8,128)} %bitcast.16, f32[8,4,256,128]{3,2,1,0:T(8,128)} %bitcast.17, f32[512,256]{1,0:T(8,128)S(1)} %get-tuple-element.37.panel_hbm, f32[512,512]{1,0:T(8,128)S(1)} %get-tuple-element.38.row_hbm), custom_call_target="tpu_custom_call" | custom-call | tf_op jit(solution)/shard_map/update/pallas_call | solution.py:321
  (3 shorter events, 0.1 us)
Async XLA Ops:
  6.5 108.6 %all-gather.3.cloned.1.call-start = ((), (), s32[]{:S(2)}) async-start(), calls=%async_computation | async-start | bytes 4718592 | tf_op jit(solution)/shard_map/all_gather | solution.py:398
  9.6 65.7 %copy-start.1 = (f32[4,256,128]{2,1,0:T(8,128)S(1)}, f32[4,256,128]{2,1,0:T(8,128)}, u32[]{:S(2)}) copy-start(f32[4,256,128]{2,1,0:T(8,128)} %get-tuple-element.33) | copy-start | bytes 1572868
  9.6 15.1 %collective-permute-start.1 = (f32[136,256]{1,0:T(8,128)}, f32[136,256]{1,0:T(8,128)S(1)}, u32[]{:S(2)}, u32[]{:S(2)}) collective-permute-start(f32[136,256]{1,0:T(8,128)} %get-tuple-element.26), channel_id=1, source_target_pairs={{0,48},{1,49},{8,56},{9,57}} | collective-permute-start | bytes 417800 | tf_op jit(solution)/shard_map/ppermute | solution.py:350
  18.5 6.2 %collective-permute-start = (f32[136,256]{1,0:T(8,128)}, f32[136,256]{1,0:T(8,128)S(1)}, u32[]{:S(2)}, u32[]{:S(2)}) collective-permute-start(f32[136,256]{1,0:T(8,128)} %get-tuple-element.26), channel_id=1, source_target_pairs={{0,24},{1,25},{8,32},{9,33}} | collective-permute-start | bytes 417800 | tf_op jit(solution)/shard_map/ppermute | solution.py:350
  25.6 14.1 %collective-permute-start.2 = (f32[256,128]{1,0:T(8,128)}, f32[256,128]{1,0:T(8,128)S(1)}, u32[]{:S(2)}, u32[]{:S(2)}) collective-permute-start(f32[256,128]{1,0:T(8,128)} %get-tuple-element.27), channel_id=1, source_target_pairs={{0,0},{1,32},{8,9},{9,41},{16,18},{17,50},{24,27},{25,59},{32,36},... | collective-permute-start | bytes 393224 | tf_op jit(solution)/shard_map/ppermute | solution.py:388
  34.4 7.2 %collective-permute-start.3 = (f32[256,128]{1,0:T(8,128)}, f32[256,128]{1,0:T(8,128)S(1)}, u32[]{:S(2)}, u32[]{:S(2)}) collective-permute-start(f32[256,128]{1,0:T(8,128)} %get-tuple-element.28), channel_id=1, source_target_pairs={{0,8},{1,24},{8,17},{9,33},{16,26},{17,42},{24,35},{25,51},{32,44}... | collective-permute-start | bytes 393224 | tf_op jit(solution)/shard_map/ppermute | solution.py:388
  35.7 6.8 %collective-permute-start.4 = (f32[256,128]{1,0:T(8,128)}, f32[256,128]{1,0:T(8,128)S(1)}, u32[]{:S(2)}, u32[]{:S(2)}) collective-permute-start(f32[256,128]{1,0:T(8,128)} %get-tuple-element.29), channel_id=1, source_target_pairs={{0,56},{1,40},{8,1},{9,49},{16,10},{17,58},{24,19},{25,3},{32,28},... | collective-permute-start | bytes 393224 | tf_op jit(solution)/shard_map/ppermute | solution.py:388
  37.7 4.9 %collective-permute-start.5 = (f32[256,128]{1,0:T(8,128)}, f32[256,128]{1,0:T(8,128)S(1)}, u32[]{:S(2)}, u32[]{:S(2)}) collective-permute-start(f32[256,128]{1,0:T(8,128)} %get-tuple-element.30), channel_id=1, source_target_pairs={{0,16},{1,48},{8,25},{9,57},{16,34},{17,2},{24,43},{25,11},{32,52}... | collective-permute-start | bytes 393224 | tf_op jit(solution)/shard_map/ppermute | solution.py:388
  39.0 6.4 %collective-permute-start.10 = (f32[136,256]{1,0:T(8,128)S(1)}, f32[136,256]{1,0:T(8,128)S(1)}, u32[]{:S(2)}, u32[]{:S(2)}) collective-permute-start(f32[136,256]{1,0:T(8,128)S(1)} %add_add_fusion.2), channel_id=1, source_target_pairs={{24,16},{25,17},{48,40},{49,41},{32,24},{33,25},{56,48},{57,49}} | collective-permute-start | bytes 417800 | tf_op jit(solution)/shard_map/ppermute | solution.py:350
  39.7 7.0 %collective-permute-start.9 = (f32[136,256]{1,0:T(8,128)S(1)}, f32[136,256]{1,0:T(8,128)S(1)}, u32[]{:S(2)}, u32[]{:S(2)}) collective-permute-start(f32[136,256]{1,0:T(8,128)S(1)} %add_add_fusion.2), channel_id=1, source_target_pairs={{0,8},{1,9},{24,32},{25,33},{48,56},{49,57},{8,16},{9,17},{32,40},... | collective-permute-start | bytes 417800 | tf_op jit(solution)/shard_map/ppermute | solution.py:350
  42.6 9.1 %collective-permute-start.8 = (f32[256,128]{1,0:T(8,128)S(1)}, f32[256,128]{1,0:T(8,128)S(1)}, u32[]{:S(2)}, u32[]{:S(2)}) collective-permute-start(f32[256,128]{1,0:T(8,128)S(1)} %add_add_fusion.3), channel_id=1, source_target_pairs={{192,0},{200,8},{208,16},{216,24},{224,32},{232,40},{240,48},{248,... | collective-permute-start | bytes 393224 | tf_op jit(solution)/shard_map/ppermute | solution.py:394
  42.7 9.0 %collective-permute-start.7 = (f32[256,128]{1,0:T(8,128)S(1)}, f32[256,128]{1,0:T(8,128)S(1)}, u32[]{:S(2)}, u32[]{:S(2)}) collective-permute-start(f32[256,128]{1,0:T(8,128)S(1)} %add_add_fusion.3), channel_id=1, source_target_pairs={{128,0},{136,8},{144,16},{152,24},{160,32},{168,40},{176,48},{184,... | collective-permute-start | bytes 393224 | tf_op jit(solution)/shard_map/ppermute | solution.py:394
  42.8 8.9 %collective-permute-start.6 = (f32[256,128]{1,0:T(8,128)S(1)}, f32[256,128]{1,0:T(8,128)S(1)}, u32[]{:S(2)}, u32[]{:S(2)}) collective-permute-start(f32[256,128]{1,0:T(8,128)S(1)} %add_add_fusion.3), channel_id=1, source_target_pairs={{64,0},{72,8},{80,16},{88,24},{96,32},{104,40},{112,48},{120,56},{... | collective-permute-start | bytes 393224 | tf_op jit(solution)/shard_map/ppermute | solution.py:394
  51.7 63.5 %copy-start = (s32[2,1,8,1]{2,3,1,0:T(1,128)S(1)}, s32[2,1,8,1]{2,3,1,0:T(1,128)}, u32[]{:S(2)}) copy-start(s32[2,1,8,1]{2,3,1,0:T(1,128)} %param.3) | copy-start | bytes 196
  52.5 11.5 %collective-permute-start.13 = (f32[4,256,128]{2,1,0:T(8,128)}, f32[4,256,128]{2,1,0:T(8,128)S(1)}, u32[]{:S(2)}, u32[]{:S(2)}) collective-permute-start(f32[4,256,128]{2,1,0:T(8,128)} %get-tuple-element.33), channel_id=1, source_target_pairs={{0,4},{1,5},{8,12},{9,13},{16,20},{17,21},{24,28},{25,29},{32,36},... | collective-permute-start | bytes 1572872 | tf_op jit(solution)/shard_map/ppermute | solution.py:350
  53.9 11.8 %collective-permute-start.12 = (f32[4,256,128]{2,1,0:T(8,128)}, f32[4,256,128]{2,1,0:T(8,128)S(1)}, u32[]{:S(2)}, u32[]{:S(2)}) collective-permute-start(f32[4,256,128]{2,1,0:T(8,128)} %get-tuple-element.33), channel_id=1, source_target_pairs={{0,6},{1,7},{8,14},{9,15},{16,22},{17,23},{24,30},{25,31},{32,38},... | collective-permute-start | bytes 1572872 | tf_op jit(solution)/shard_map/ppermute | solution.py:350
  55.2 20.1 %collective-permute-start.11 = (f32[4,256,128]{2,1,0:T(8,128)}, f32[4,256,128]{2,1,0:T(8,128)S(1)}, u32[]{:S(2)}, u32[]{:S(2)}) collective-permute-start(f32[4,256,128]{2,1,0:T(8,128)} %get-tuple-element.33), channel_id=1, source_target_pairs={{0,2},{1,3},{8,10},{9,11},{16,18},{17,19},{24,26},{25,27},{32,34},... | collective-permute-start | bytes 1572872 | tf_op jit(solution)/shard_map/ppermute | solution.py:350
  56.5 18.9 %collective-permute-start.16 = (f32[2,136,256]{2,1,0:T(8,128)S(1)}, f32[2,136,256]{2,1,0:T(8,128)S(1)}, u32[]{:S(2)}, u32[]{:S(2)}) collective-permute-start(f32[2,136,256]{2,1,0:T(8,128)S(1)} %maximum_select_fusion), channel_id=1, source_target_pairs={{0,128},{1,129},{8,136},{9,137},{16,144},{17,145},{24,152},{25,153... | collective-permute-start | bytes 835592 | tf_op jit(solution)/shard_map/ppermute | solution.py:350
  58.4 17.0 %collective-permute-start.15 = (f32[2,136,256]{2,1,0:T(8,128)S(1)}, f32[2,136,256]{2,1,0:T(8,128)S(1)}, u32[]{:S(2)}, u32[]{:S(2)}) collective-permute-start(f32[2,136,256]{2,1,0:T(8,128)S(1)} %maximum_select_fusion), channel_id=1, source_target_pairs={{0,192},{1,193},{8,200},{9,201},{16,208},{17,209},{24,216},{25,217... | collective-permute-start | bytes 835592 | tf_op jit(solution)/shard_map/ppermute | solution.py:350
  64.1 11.4 %collective-permute-start.14 = (f32[2,136,256]{2,1,0:T(8,128)S(1)}, f32[2,136,256]{2,1,0:T(8,128)S(1)}, u32[]{:S(2)}, u32[]{:S(2)}) collective-permute-start(f32[2,136,256]{2,1,0:T(8,128)S(1)} %maximum_select_fusion), channel_id=1, source_target_pairs={{0,64},{1,65},{8,72},{9,73},{16,80},{17,81},{24,88},{25,89},{32,96... | collective-permute-start | bytes 835592 | tf_op jit(solution)/shard_map/ppermute | solution.py:350
  75.5 8.0 %collective-permute-start.19 = (f32[2,136,256]{2,1,0:T(8,128)S(1)}, f32[2,136,256]{2,1,0:T(8,128)S(1)}, u32[]{:S(2)}, u32[]{:S(2)}) collective-permute-start(f32[2,136,256]{2,1,0:T(8,128)S(1)} %add_add_fusion.1), channel_id=1, source_target_pairs={{0,4},{1,5},{8,12},{9,13},{16,20},{17,21},{24,28},{25,29},{32,36},... | collective-permute-start | bytes 835592 | tf_op jit(solution)/shard_map/ppermute | solution.py:350
  76.8 6.7 %collective-permute-start.18 = (f32[2,136,256]{2,1,0:T(8,128)S(1)}, f32[2,136,256]{2,1,0:T(8,128)S(1)}, u32[]{:S(2)}, u32[]{:S(2)}) collective-permute-start(f32[2,136,256]{2,1,0:T(8,128)S(1)} %add_add_fusion.1), channel_id=1, source_target_pairs={{0,6},{1,7},{8,14},{9,15},{16,22},{17,23},{24,30},{25,31},{32,38},... | collective-permute-start | bytes 835592 | tf_op jit(solution)/shard_map/ppermute | solution.py:350
  78.1 9.4 %collective-permute-start.17 = (f32[2,136,256]{2,1,0:T(8,128)S(1)}, f32[2,136,256]{2,1,0:T(8,128)S(1)}, u32[]{:S(2)}, u32[]{:S(2)}) collective-permute-start(f32[2,136,256]{2,1,0:T(8,128)S(1)} %add_add_fusion.1), channel_id=1, source_target_pairs={{0,2},{1,3},{8,10},{9,11},{16,18},{17,19},{24,26},{25,27},{32,34},... | collective-permute-start | bytes 835592 | tf_op jit(solution)/shard_map/ppermute | solution.py:350
  81.0 8.8 %collective-permute-start.21 = (f32[4,256,128]{2,1,0:T(8,128)S(1)}, f32[4,256,128]{2,1,0:T(8,128)S(1)}, u32[]{:S(2)}, u32[]{:S(2)}) collective-permute-start(f32[4,256,128]{2,1,0:T(8,128)S(1)} %add_select_fusion.slab_ref), channel_id=1, source_target_pairs={{0,1},{1,0},{2,3},{3,2},{4,5},{5,4},{6,7},{7,6},{8,9},{9,8},{10,11... | collective-permute-start | bytes 1572872 | tf_op jit(solution)/shard_map/ppermute | solution.py:414
  87.6 3.4 %collective-permute-start.20 = (f32[2,136,256]{2,1,0:T(8,128)S(1)}, f32[2,136,256]{2,1,0:T(8,128)S(1)}, u32[]{:S(2)}, u32[]{:S(2)}) collective-permute-start(f32[2,136,256]{2,1,0:T(8,128)S(1)} %add_add_fusion.mine_ref), channel_id=1, source_target_pairs={{0,1},{1,0},{2,3},{3,2},{4,5},{5,4},{6,7},{7,6},{8,9},{9,8},{10,11... | collective-permute-start | bytes 835592 | tf_op jit(solution)/shard_map/ppermute | solution.py:412
Sparse Core Ops, SparseCore 0:
  52.7 53.0 all-gather.2

commit v3 on v2

--- a/solution.py
+++ b/solution.py
@@ -76,7 +76,7 @@
     return rows
 
 
-def factor_block(g_ref, u_ref, v_ref):
+def factor_block(g_ref, u_ref, v_ref, beside=None):
     lane = lax.broadcasted_iota(jnp.int32, (NB, W), 1)
     row = lax.broadcasted_iota(jnp.int32, (NB, W), 0)
     eye = (
@@ -86,6 +86,8 @@
     tail = lax.broadcasted_iota(jnp.int32, (W - NB, W), 1)
 
     def panel(p, carry):
+        if beside is not None:
+            beside(p)
         x = jnp.concatenate([g_ref[0:NB, :], eye], axis=1)
         rows = eliminate([x[8 * t : 8 * t + 8] for t in range(4)])
         r = jnp.concatenate(rows, axis=0)
@@ -111,6 +113,8 @@
 
 
 H = W // 2
+PACKED = H + 16
+PIECE = PACKED // 2
 
 
 def half_masks():
@@ -133,42 +137,59 @@
 
 
 def factor_kernel(
-    mine_ref, other_ref, slab_ref, twin_ref, panel_ref, row_ref, g_ref, u_ref, v0_ref, v1_ref
+    mine_ref, other_ref, slab_ref, twin_ref,
+    panel_ref, row_ref, g_ref, u_ref, v0_ref, v1_ref, r0_ref, r1_ref,
 ):
     r, c = lax.axis_index("row"), lax.axis_index("col")
     even = lax.rem(c, 2) == 0
-    left = [jnp.where(even, mine_ref[i], other_ref[i]) for i in range(2)]
-    right = [jnp.where(even, other_ref[i], mine_ref[i]) for i in range(2)]
-    g_ref[...] = unpack(left[0])
+
+    def joined(t, side):
+        spots = [lax.rem(x - r // 8 + 4, 4) for x in range(4)]
+        tall = [
+            jnp.where(even == side, mine_ref[spot, t], other_ref[spot, t]) for spot in spots
+        ]
+        return jnp.concatenate(
+            [jnp.concatenate(tall[2 * h : 2 * h + 2], axis=0) for h in range(2)], axis=1
+        )
+
+    g_ref[...] = unpack(joined(0, True))
     factor_block(g_ref, u_ref, v0_ref)
+    upper, lower = joined(0, False), joined(1, True)
     low = jnp.concatenate(
-        [jnp.transpose(left[1][0:H, 0:H]), jnp.transpose(left[1][0:H, H:W])], axis=1
+        [jnp.transpose(lower[0:H, 0:H]), jnp.transpose(lower[0:H, H:W])], axis=1
     )
-    a01 = jnp.concatenate([right[0][0:H], low], axis=0)
+    a01 = jnp.concatenate([upper[0:H], low], axis=0)
     v0 = v0_ref[...]
     pt = dot_nn(v0, a01)
     p10 = jnp.transpose(pt)
-    g_ref[...] = unpack(right[1]) - dot_tn(pt, pt)
+    g_ref[...] = unpack(joined(1, False)) - dot_tn(pt, pt)
     first_u = jnp.transpose(u_ref[...])
-    factor_block(g_ref, u_ref, v1_ref)
+    for s, ref in enumerate((r0_ref, r1_ref)):
+        for m in range(2):
+            for h in range(2):
+                i = 2 * m + h
+                ref[m * W : m * W + W, h * H : h * H + H] = jnp.where(
+                    even == (s == 0), slab_ref[i], twin_ref[i]
+                )
+
+    def beside(p):
+        span = pl.ds(pl.multiple_of(p * 64, 64), 64)
+        first = dot_nt(r0_ref[span, :], v0_ref[...])
+        panel_ref[span, :] = first
+        r1_ref[span, :] = r1_ref[span, :] - dot_nn(first, pt)
+        r0_ref[span, :] = dot_nn(first, v0_ref[...])
+
+    factor_block(g_ref, u_ref, v1_ref, beside)
     v1 = v1_ref[...]
-
-    raws = []
-    for s in range(2):
-        parts = [
-            jnp.where(even == (s == 0), slab_ref[i], twin_ref[i]) for i in range(4)
-        ]
-        raws.append(
-            jnp.concatenate(
-                [jnp.concatenate(parts[2 * m : 2 * m + 2], axis=1) for m in range(2)], axis=0
-            )
-        )
-    first = dot_nt(raws[0], v0)
-    second = dot_nt(raws[1] - dot_nn(first, pt), v1)
-    panel_ref[...] = jnp.where(c == 0, first, second)
+    p10v0 = dot_nn(p10, v0)
+    second = dot_nt(r1_ref[...], v1)
     back1 = dot_nn(second, v1)
-    row_ref[:, 0:W] = dot_nn(first - dot_nn(back1, p10), v0)
+    row_ref[:, 0:W] = r0_ref[...] - dot_nn(back1, p10v0)
     row_ref[:, W : 2 * W] = back1
+
+    @pl.when(c != 0)
+    def _():
+        panel_ref[...] = second
 
     @pl.when(r == 0)
     def _():
@@ -178,7 +199,7 @@
 
     @pl.when(r == 1)
     def _():
-        row_ref[0:W, 0:W] = dot_nn(dot_nn(v1, p10), v0)
+        row_ref[0:W, 0:W] = dot_nn(v1, p10v0)
         row_ref[0:W, W : 2 * W] = -v1
         panel_ref[0:W, :] = jnp.where(c == 0, p10, jnp.transpose(u_ref[...]))
 
@@ -190,7 +211,8 @@
             jax.ShapeDtypeStruct((2 * W, W), F32),
             jax.ShapeDtypeStruct((2 * W, 2 * W), F32),
         ],
-        scratch_shapes=[pltpu.VMEM((W, W), F32)] * 4,
+        scratch_shapes=[pltpu.VMEM((W, W), F32)] * 4
+        + [pltpu.VMEM((2 * W, W), F32)] * 2,
         compiler_params=pltpu.CompilerParams(vmem_limit_bytes=24 * 1024 * 1024),
         name="factor_pair",
     )(mine, other, slab, twin)
@@ -207,25 +229,28 @@
             piece_refs[2 * m + h][...] = part
             parts.append(part)
     below, right = half_masks()
-    packed_ref[...] = jnp.zeros((H + 8, W), F32)
+
+    def put(first, second, extra):
+        packed_ref[...] = jnp.concatenate(
+            [first, jnp.broadcast_to(extra, (PACKED - H, H)), second, jnp.zeros((PACKED - H, H), F32)],
+            axis=0,
+        )
 
     @pl.when(r == c)
     def _():
         second = parts[1][H:W]
         diagonal = jnp.sum(jnp.where(below == right, second, 0.0), axis=0, keepdims=True)
-        packed_ref[0:H, 0:H] = jnp.where(below >= right, parts[0][0:H], second)
-        packed_ref[0:H, H:W] = parts[0][H:W]
-        packed_ref[H : H + 8, 0:H] = jnp.broadcast_to(diagonal, (8, H))
+        put(jnp.where(below >= right, parts[0][0:H], second), parts[0][H:W], diagonal)
+
+    zero = jnp.zeros((1, H), F32)
 
     @pl.when(r < c)
     def _():
-        packed_ref[0:H, 0:H] = parts[0][0:H]
-        packed_ref[0:H, H:W] = parts[1][0:H]
+        put(parts[0][0:H], parts[1][0:H], zero)
 
     @pl.when(r > c)
     def _():
-        packed_ref[0:H, 0:H] = parts[1][0:H]
-        packed_ref[0:H, H:W] = parts[1][H:W]
+        put(parts[1][0:H], parts[1][H:W], zero)
 
 
 def extract(pattern, view):
@@ -239,7 +264,7 @@
         out_specs=[pl.BlockSpec(memory_space=pltpu.VMEM)] * 6,
         out_shape=[
             jax.ShapeDtypeStruct((4, W, 128), F32),
-            jax.ShapeDtypeStruct((H + 8, W), F32),
+            jax.ShapeDtypeStruct((2 * PACKED, H), F32),
         ]
         + [jax.ShapeDtypeStruct((W, 128), F32)] * 4,
         compiler_params=pltpu.CompilerParams(vmem_limit_bytes=56 * 1024 * 1024),
@@ -251,8 +276,8 @@
 
 
 def update_kernel(
-    pattern_ref, front_hbm, q_hbm, panel_hbm, row_hbm, out_hbm,
-    front_ref, q_ref, panel_ref, row_ref, out_ref, front_sem, q_sem, row_sem, out_sem,
+    pattern_ref, front_hbm, q_hbm, panel_ref, row_ref, out_hbm,
+    front_ref, q_ref, out_ref, front_sem, q_sem, out_sem,
 ):
     r, c = lax.axis_index("row"), lax.axis_index("col")
     x = r // 8
@@ -263,21 +288,18 @@
         copy.start()
         return copy
 
-    row_copy = begin(row_hbm, row_ref, row_sem.at[0])
     for m in range(2):
         for h in range(2):
             for s in range(2):
                 i = 4 * m + 2 * h + s
                 at = lax.rem(c + FAR[s][2 * m + h], 8)
                 q_copies.append(begin(q_hbm.at[at], q_ref.at[i], q_sem.at[i]))
-    panel_copy = begin(panel_hbm, panel_ref, row_sem.at[1])
     for m in range(2):
         half = pl.ds(m * 4096, 4096)
         front_copies.append(begin(front_hbm.at[half], front_ref.at[half], front_sem.at[m]))
         out_copies.append(
             pltpu.make_async_copy(out_ref.at[half], out_hbm.at[half], out_sem.at[m])
         )
-    row_copy.wait()
     for m in range(2):
         place = r + 32 * m
         row = row_ref[m * W : m * W + W, :]
@@ -301,8 +323,6 @@
         front_copies[m].wait()
         old = front_ref[half, :].reshape(W, 16, 128)
         out_ref[half, :] = (old * scale - moved).reshape(4096, 128)
-        if m == 0:
-            panel_copy.wait()
 
         @pl.when(c < 2)
         def _():
@@ -318,20 +338,18 @@
 
 def update(pattern, view, gathered, panel, row):
     hbm = pl.BlockSpec(memory_space=pl.ANY)
+    vmem = pl.BlockSpec(memory_space=pltpu.VMEM)
     return pl.pallas_call(
         update_kernel,
-        in_specs=[pl.BlockSpec(memory_space=pltpu.SMEM)] + [hbm] * 4,
+        in_specs=[pl.BlockSpec(memory_space=pltpu.SMEM), hbm, hbm, vmem, vmem],
         out_specs=hbm,
         out_shape=jax.ShapeDtypeStruct((8192, 128), F32),
         scratch_shapes=[
             pltpu.VMEM((8192, 128), F32),
             pltpu.VMEM((8, 4, W, 128), F32),
-            pltpu.VMEM((2 * W, W), F32),
-            pltpu.VMEM((2 * W, 2 * W), F32),
             pltpu.VMEM((8192, 128), F32),
             pltpu.SemaphoreType.DMA((2,)),
             pltpu.SemaphoreType.DMA((8,)),
-            pltpu.SemaphoreType.DMA((2,)),
             pltpu.SemaphoreType.DMA((2,)),
         ],
         compiler_params=pltpu.CompilerParams(vmem_limit_bytes=52 * 1024 * 1024),
@@ -353,30 +371,21 @@
 def on_device(front, pattern):
     row_place = lax.axis_index("row")
     col_place = lax.axis_index("col")
-    z_place = row_place % 8
     view = front.reshape(8192, 128)
     present = pattern.reshape(2, 8)
     slab, packed, *pieces = extract(present, front.reshape(512, 16, 128))
 
-    at_first = (z_place == 0) | (z_place == 3) | (z_place == 6)
-    at_second = (z_place == 1) | (z_place == 4) | (z_place == 7)
-    steps = around(packed, BOTH, [
-        [(device(0, z, s), device(0, (z + d) % 8, s)) for z in range(2) for s in range(2)]
-        for d in (3, 6)
-    ])
-    source = (row_place < 2) & (col_place < 2)
-    held = jnp.where(source, packed, 0.0) + steps[0] + steps[1]
-    pieces, held = lax.optimization_barrier((pieces, held))
-    plus, minus = around(held, BOTH, [
-        [(device(0, z, s), device(0, (z + 1) % 8, s)) for z in (0, 3, 6, 1, 4, 7) for s in range(2)],
-        [(device(0, z, s), device(0, z - 1, s)) for z in (3, 6, 4, 7) for s in range(2)],
-    ])
-    either = plus + minus
-    diag = jnp.stack([
-        jnp.where(at_first, held, jnp.where(at_second, plus, minus)),
-        jnp.where(at_first, either, jnp.where(at_second, held, plus)),
-    ])
-    diag = jnp.where((row_place < 8) & (col_place < 2), diag, 0.0)
+    x_moves = [
+        [(((x + d) % 4) * 8 + z, x * 8 + z) for x in range(4) for z in range(8)]
+        for d in (1, 2, 3)
+    ]
+    swap = [(c, c ^ 1) for c in range(8)]
+    groups = [[x * 8 + z for z in range(8)] for x in range(4)]
+    z_place = row_place % 8
+
+    across = lax.all_gather(packed, "col")
+    held = jnp.where(col_place % 2 == 0, across[0], across[1])
+
     share = 0.0
     for k in range(4):
         pairs = [
@@ -386,34 +395,40 @@
             for s in range(2)
         ]
         share = share + lax.ppermute(pieces[k], BOTH, pairs)
-    line = [share]
-    for d in range(1, 4):
-        pairs = [
-            (((x + d) % 4) * 8 + z, x * 8 + z) for x in range(4) for z in range(8)
-        ]
-        line.append(lax.ppermute(share, "row", pairs))
-    line = jnp.stack(line)
-    line, diag = lax.optimization_barrier((line, diag))
-    groups = [[x * 8 + z for z in range(8)] for x in range(4)]
+    line = jnp.stack([share] + around(share, "row", x_moves))
+    slab = jnp.where(col_place < 2, slab, lax.ppermute(slab, "col", [(0, 4), (1, 5)]))
+    line, held, slab = lax.optimization_barrier((line, held, slab))
     gathered = lax.all_gather(line, "row", axis_index_groups=groups)
 
-    steps = around(diag, BOTH, [
-        [(device(0, z, s), device(x, z, s)) for z in range(8) for s in range(2)]
-        for x in (1, 3, 2)
+    quarters = [held[PIECE * x : PIECE * x + PIECE] for x in range(4)]
+    held = jnp.where(row_place < 2, quarters[0], 0.0)
+    for x in (1, 3, 2):
+        held = held + lax.ppermute(quarters[x], "row", [(z, x * 8 + z) for z in range(2)])
+    moved = lax.ppermute(slab, "col", [(0, 2), (1, 3), (4, 6), (5, 7)])
+
+    at_first = (z_place == 0) | (z_place == 3) | (z_place == 6)
+    at_second = (z_place == 1) | (z_place == 4) | (z_place == 7)
+    steps = around(held, "row", [
+        [(x * 8 + z, x * 8 + (z + d) % 8) for x in range(4) for z in range(2)]
+        for d in (3, 6)
     ])
-    diag = diag + steps[0] + steps[1] + steps[2]
-    fan_y = [[(s, s + y) for s in range(2)] for y in (2, 6, 4)]
-    steps = around(slab, "col", fan_y)
-    slab = jnp.where(col_place < 2, slab, steps[0] + steps[1] + steps[2])
-    slab, diag = lax.optimization_barrier((slab, diag))
-    steps = around(diag, "col", fan_y)
-    diag = diag + steps[0] + steps[1] + steps[2]
-    swap = [(c, c ^ 1) for c in range(8)]
-    other = lax.ppermute(diag, "col", swap)
-
+    held = held + steps[0] + steps[1]
+    plus, minus = around(held, "row", [
+        [(x * 8 + z, x * 8 + (z + 1) % 8) for x in range(4) for z in (0, 3, 6, 1, 4, 7)],
+        [(x * 8 + z, x * 8 + z - 1) for x in range(4) for z in (3, 6, 4, 7)],
+    ])
+    either = plus + minus
+    diag = jnp.stack([
+        jnp.where(at_first, held, jnp.where(at_second, plus, minus)),
+        jnp.where(at_first, either, jnp.where(at_second, held, plus)),
+    ])
+    slab = jnp.where(col_place % 4 < 2, slab, moved)
+    diag, slab = lax.optimization_barrier((diag, slab))
     twin = lax.ppermute(slab, "col", swap)
-
-    panel, row = factor_pair(diag, other, slab, twin)
+    mine = jnp.stack([diag] + around(diag, "row", x_moves))
+    other = lax.ppermute(mine, "col", swap)
+
+    panel, row = factor_pair(mine, other, slab, twin)
     out = update(present, view, gathered, panel, row)
     return out.reshape(2, 1, 256, 8, 1, 256)
 

time: 135 us -> 125 us (0.926)
  waiting for transfers between devices: 29.2 us -> 24.2 us
  starting transfers between devices: 49.8 us -> 45.3 us
  Pallas kernels: 39 us -> 37.4 us
    ppermute x13 -> x10, starting transfers between devices: 29 us -> 15.9 us  [around(): return [lax.ppermute(value, axis, pairs) for pairs in moves]]
    ppermute x13 -> x10, waiting for transfers between devices: 22.2 us -> 12.3 us  [around(): return [lax.ppermute(value, axis, pairs) for pairs in moves]]
    ppermute x4 -> x6, starting transfers between devices: 4.94 us -> 10.6 us  [the longest x3 6.68 us: on_device(): lax.ppermute(quarters[x], 'row', [(z, x * 8 + z) for z in range(2)])]
    ppermute x4, waiting for transfers between devices: 0.94 us -> 6.36 us  [on_device(): share = share + lax.ppermute(pieces[k], BOTH, pairs)]
    ppermute x4, starting transfers between devices: 13.3 us -> 16.9 us  [on_device(): share = share + lax.ppermute(pieces[k], BOTH, pairs)]
    select_n x2 -> x3, other arithmetic: 0.12 us -> 2.2 us  [the longest x1 1.14 us: on_device(): jnp.where(col_place < 2, slab, lax.ppermute(slab, 'col', [(0, 4), (1, 5)]))]
    pallas_call x1, Pallas kernels: 24.2 us -> 22.4 us  [factor_pair(): pl.pallas_call(factor_kernel, out_shape=[jax.ShapeDtypeStruct((2 * W, W),...]
    ppermute x4 -> x6, waiting for transfers between devices: 6.06 us -> 5.45 us  [the longest x1 1.82 us: on_device(): lax.ppermute(slab, 'col', [(0, 4), (1, 5)])]
  transfers between devices with their start and end apart: 23 -> 23, of which waited for: 8 -> 11; matrix products, arithmetic and copies ran while one was open for 0% -> 2% of each run, Pallas kernels for 18% -> 18%
where the time goes in v3:
time: 125 us; the launch traced here: 124 us
  starting transfers between devices  45.3 us (36%)
  Pallas kernels  37.4 us (30%)
  waiting for transfers between devices  24.2 us (19%)
  between operations  13.7 us (11%)
  other arithmetic  3.15 us (3%)
    pallas_call x1, Pallas kernels, factor_pair(): pl.pallas_call(factor_kernel, out_shape=[jax.ShapeDtypeStruct((2 * W, W),...  22.4 us
    ppermute x4, starting transfers between devices, on_device(): share = share + lax.ppermute(pieces[k], BOTH, pairs)  16.9 us
    ppermute x10, starting transfers between devices, around(): return [lax.ppermute(value, axis, pairs) for pairs in moves]  15.9 us
    ppermute x10, waiting for transfers between devices, around(): return [lax.ppermute(value, axis, pairs) for pairs in moves]  12.3 us
    pallas_call x1, Pallas kernels, update(): pl.pallas_call(update_kernel, in_specs=[pl.BlockSpec(memory_space=pltpu.S...  12 us
    ppermute x3, starting transfers between devices, on_device(): lax.ppermute(quarters[x], 'row', [(z, x * 8 + z) for z in range(2)])  6.68 us
    ppermute x4, waiting for transfers between devices, on_device(): share = share + lax.ppermute(pieces[k], BOTH, pairs)  6.36 us
    pallas_call x1, Pallas kernels, extract(): pl.pallas_call(extract_kernel, grid=(1,), in_specs=[pl.BlockSpec(memory_s...  3.04 us
  transfers between devices with their start and end apart: 23, of which 11 were waited for; matrix products, arithmetic and copies ran while one was open for 2% of the time, Pallas kernels for 18%

profile of v3, /device:TPU:1, one launch (start us, length us, event | category | flops | bytes accessed | tf_op | source)
XLA Modules:
  0.0 123.9 jit_solution(1241816900703174220)
XLA Ops:
  6.5 0.0 all-gather.5.cloned.1.call-start
  6.5 3.0 %extract.1 = (f32[4,256,128]{2,1,0:T(8,128)}, f32[288,128]{1,0:T(8,128)}, f32[256,128]{1,0:T(8,128)}, f32[256,128]{1,0:T(8,128)}, f32[256,128]{1,0:T(8,128)}, /*index=5*/f32[256,128]{1,0:T(8,128)}) custom-call(s32[2,8]{1,0:T(2,128)} %bitcast.17, f32[512,16,128]{2,1,0:T(8,128)} %bitcast.19), custom_call_target="tpu_custom_call" | custom-call | tf_op jit(solution)/shard_map/extract/pallas_call | solution.py:257
  9.6 0.0 all-gather.5.cloned.1.call-update
  9.6 0.0 all-gather.7.cloned.1.call-start
  9.6 10.2 %collective-permute-start = (f32[256,128]{1,0:T(8,128)}, f32[256,128]{1,0:T(8,128)S(1)}, u32[]{:S(2)}, u32[]{:S(2)}) collective-permute-start(f32[256,128]{1,0:T(8,128)} %get-tuple-element.18), channel_id=1, source_target_pairs={{0,0},{1,32},{8,9},{9,41},{16,18},{17,50},{24,27},{25,59},{32,36},... | collective-permute-start | bytes 393224 | tf_op jit(solution)/shard_map/ppermute | solution.py:397
  19.9 1.3 %collective-permute-start.1 = (f32[256,128]{1,0:T(8,128)}, f32[256,128]{1,0:T(8,128)S(1)}, u32[]{:S(2)}, u32[]{:S(2)}) collective-permute-start(f32[256,128]{1,0:T(8,128)} %get-tuple-element.19), channel_id=1, source_target_pairs={{0,8},{1,24},{8,17},{9,33},{16,26},{17,42},{24,35},{25,51},{32,44}... | collective-permute-start | bytes 393224 | tf_op jit(solution)/shard_map/ppermute | solution.py:397
  21.2 4.1 %collective-permute-start.2 = (f32[256,128]{1,0:T(8,128)}, f32[256,128]{1,0:T(8,128)S(1)}, u32[]{:S(2)}, u32[]{:S(2)}) collective-permute-start(f32[256,128]{1,0:T(8,128)} %get-tuple-element.20), channel_id=1, source_target_pairs={{0,56},{1,40},{8,1},{9,49},{16,10},{17,58},{24,19},{25,3},{32,28},... | collective-permute-start | bytes 393224 | tf_op jit(solution)/shard_map/ppermute | solution.py:397
  25.3 1.3 %collective-permute-start.3 = (f32[256,128]{1,0:T(8,128)}, f32[256,128]{1,0:T(8,128)S(1)}, u32[]{:S(2)}, u32[]{:S(2)}) collective-permute-start(f32[256,128]{1,0:T(8,128)} %get-tuple-element.21), channel_id=1, source_target_pairs={{0,16},{1,48},{8,25},{9,57},{16,34},{17,2},{24,43},{25,11},{32,52}... | collective-permute-start | bytes 393224 | tf_op jit(solution)/shard_map/ppermute | solution.py:397
  26.6 1.3 %collective-permute-start.7 = (f32[4,256,128]{2,1,0:T(8,128)}, f32[4,256,128]{2,1,0:T(8,128)S(1)}, u32[]{:S(2)}, u32[]{:S(2)}) collective-permute-start(f32[4,256,128]{2,1,0:T(8,128)} %get-tuple-element.23), channel_id=1, source_target_pairs={{0,4},{1,5},{8,12},{9,13},{16,20},{17,21},{24,28},{25,29},{32,36},... | collective-permute-start | bytes 1572872 | tf_op jit(solution)/shard_map/ppermute | solution.py:399
  27.9 0.0 collective-permute-done
  27.9 0.0 collective-permute-done.1
  27.9 6.4 %collective-permute-done.2 = f32[256,128]{1,0:T(8,128)S(1)} collective-permute-done((f32[256,128]{1,0:T(8,128)}, f32[256,128]{1,0:T(8,128)S(1)}, u32[]{:S(2)}, u32[]{:S(2)}) %collective-permute-start.2) | collective-permute-done | bytes 131104 | tf_op jit(solution)/shard_map/ppermute | solution.py:397
  34.3 0.0 collective-permute-done.3
  34.3 1.3 %collective-permute-start.6 = (f32[256,128]{1,0:T(8,128)S(1)}, f32[256,128]{1,0:T(8,128)S(1)}, u32[]{:S(2)}, u32[]{:S(2)}) collective-permute-start(f32[256,128]{1,0:T(8,128)S(1)} %add_add_fusion), channel_id=1, source_target_pairs={{192,0},{200,8},{208,16},{216,24},{224,32},{232,40},{240,48},{248,... | collective-permute-start | bytes 393224 | tf_op jit(solution)/shard_map/ppermute | solution.py:368
  35.6 2.5 %collective-permute-start.5 = (f32[256,128]{1,0:T(8,128)S(1)}, f32[256,128]{1,0:T(8,128)S(1)}, u32[]{:S(2)}, u32[]{:S(2)}) collective-permute-start(f32[256,128]{1,0:T(8,128)S(1)} %add_add_fusion), channel_id=1, source_target_pairs={{128,0},{136,8},{144,16},{152,24},{160,32},{168,40},{176,48},{184,... | collective-permute-start | bytes 393224 | tf_op jit(solution)/shard_map/ppermute | solution.py:368
  38.1 1.2 collective-permute-start.4
  39.2 0.0 copy-start
  39.2 1.4 %collective-permute-done.6 = f32[256,128]{1,0:T(8,128)S(1)} collective-permute-done((f32[256,128]{1,0:T(8,128)S(1)}, f32[256,128]{1,0:T(8,128)S(1)}, u32[]{:S(2)}, u32[]{:S(2)}) %collective-permute-start.6) | collective-permute-done | bytes 131104 | tf_op jit(solution)/shard_map/ppermute | solution.py:368
  40.6 1.4 %collective-permute-done.5 = f32[256,128]{1,0:T(8,128)S(1)} collective-permute-done((f32[256,128]{1,0:T(8,128)S(1)}, f32[256,128]{1,0:T(8,128)S(1)}, u32[]{:S(2)}, u32[]{:S(2)}) %collective-permute-start.5) | collective-permute-done | bytes 131104 | tf_op jit(solution)/shard_map/ppermute | solution.py:368
  42.0 0.6 collective-permute-done.4
  42.6 0.9 pad_maximum_fusion
  43.5 1.8 %collective-permute-done.7 = f32[4,256,128]{2,1,0:T(8,128)S(1)} collective-permute-done((f32[4,256,128]{2,1,0:T(8,128)}, f32[4,256,128]{2,1,0:T(8,128)S(1)}, u32[]{:S(2)}, u32[]{:S(2)}) %collective-permute-start.7) | collective-permute-done | bytes 524320 | tf_op jit(solution)/shard_map/ppermute | solution.py:399
  45.3 1.1 broadcast_select_fusion.1
  46.4 0.0 all-gather.5.cloned.1.call-done
  46.5 1.0 slice_select_fusion
  47.5 0.0 all-gather.7.cloned.1.call-update
  47.5 3.2 %collective-permute-start.8 = (f32[72,128]{1,0:T(8,128)S(1)}, f32[72,128]{1,0:T(8,128)S(1)}, u32[]{:S(2)}, u32[]{:S(2)}) collective-permute-start(f32[72,128]{1,0:T(8,128)S(1)} %get-tuple-element.31), channel_id=1, source_target_pairs={{0,64},{8,72},{1,65},{9,73},{2,66},{10,74},{3,67},{11,75},{4,68},{... | collective-permute-start | bytes 110600 | tf_op jit(solution)/shard_map/ppermute | solution.py:406
  50.7 2.2 %collective-permute-start.10 = (f32[72,128]{1,0:T(8,128)S(1)}, f32[72,128]{1,0:T(8,128)S(1)}, u32[]{:S(2)}, u32[]{:S(2)}) collective-permute-start(f32[72,128]{1,0:T(8,128)S(1)} %get-tuple-element.32), channel_id=1, source_target_pairs={{0,128},{8,136},{1,129},{9,137},{2,130},{10,138},{3,131},{11,139},... | collective-permute-start | bytes 110600 | tf_op jit(solution)/shard_map/ppermute | solution.py:406
  52.9 1.3 %collective-permute-start.9 = (f32[72,128]{1,0:T(8,128)S(1)}, f32[72,128]{1,0:T(8,128)S(1)}, u32[]{:S(2)}, u32[]{:S(2)}) collective-permute-start(f32[72,128]{1,0:T(8,128)S(1)} %get-tuple-element.33), channel_id=1, source_target_pairs={{0,192},{8,200},{1,193},{9,201},{2,194},{10,202},{3,195},{11,203},... | collective-permute-start | bytes 110600 | tf_op jit(solution)/shard_map/ppermute | solution.py:406
  54.2 0.0 collective-permute-done.8
  54.2 0.0 collective-permute-done.10
  54.2 1.0 collective-permute-done.9
  55.3 1.3 %collective-permute-start.12 = (f32[72,128]{1,0:T(8,128)S(1)}, f32[72,128]{1,0:T(8,128)S(1)}, u32[]{:S(2)}, u32[]{:S(2)}) collective-permute-start(f32[72,128]{1,0:T(8,128)S(1)} %add_add_fusion.2), channel_id=1, source_target_pairs={{0,48},{8,56},{64,112},{72,120},{128,176},{136,184},{192,240},{200... | collective-permute-start | bytes 110600 | tf_op jit(solution)/shard_map/ppermute | solution.py:368
  56.6 1.3 %collective-permute-start.11 = (f32[72,128]{1,0:T(8,128)S(1)}, f32[72,128]{1,0:T(8,128)S(1)}, u32[]{:S(2)}, u32[]{:S(2)}) collective-permute-start(f32[72,128]{1,0:T(8,128)S(1)} %add_add_fusion.2), channel_id=1, source_target_pairs={{0,24},{8,32},{64,88},{72,96},{128,152},{136,160},{192,216},{200,2... | collective-permute-start | bytes 110600 | tf_op jit(solution)/shard_map/ppermute | solution.py:368
  57.9 1.3 %collective-permute-start.15 = (f32[4,256,128]{2,1,0:T(8,128)S(1)}, f32[4,256,128]{2,1,0:T(8,128)S(1)}, u32[]{:S(2)}, u32[]{:S(2)}) collective-permute-start(f32[4,256,128]{2,1,0:T(8,128)S(1)} %broadcast_select_fusion.1), channel_id=1, source_target_pairs={{0,2},{1,3},{4,6},{5,7},{8,10},{9,11},{12,14},{13,15},{16,18},{17,... | collective-permute-start | bytes 1572872 | tf_op jit(solution)/shard_map/ppermute | solution.py:407
  59.2 0.0 collective-permute-done.12
  59.2 0.0 collective-permute-done.11
  59.2 0.7 collective-permute-start.14
  59.9 3.1 %collective-permute-start.13 = (f32[72,128]{1,0:T(8,128)S(1)}, f32[72,128]{1,0:T(8,128)S(1)}, u32[]{:S(2)}, u32[]{:S(2)}) collective-permute-start(f32[72,128]{1,0:T(8,128)S(1)} %add_add_fusion.1), channel_id=1, source_target_pairs={{0,8},{24,32},{48,56},{8,16},{32,40},{56,0},{64,72},{88,96},{112,1... | collective-permute-start | bytes 110600 | tf_op jit(solution)/shard_map/ppermute | solution.py:368
  63.1 0.0 collective-permute-done.14
  63.1 5.0 %collective-permute-done.13 = f32[72,128]{1,0:T(8,128)S(1)} collective-permute-done((f32[72,128]{1,0:T(8,128)S(1)}, f32[72,128]{1,0:T(8,128)S(1)}, u32[]{:S(2)}, u32[]{:S(2)}) %collective-permute-start.13) | collective-permute-done | bytes 36896 | tf_op jit(solution)/shard_map/ppermute | solution.py:368
  68.1 1.4 %collective-permute-done.15 = f32[4,256,128]{2,1,0:T(8,128)S(1)} collective-permute-done((f32[4,256,128]{2,1,0:T(8,128)S(1)}, f32[4,256,128]{2,1,0:T(8,128)S(1)}, u32[]{:S(2)}, u32[]{:S(2)}) %collective-permute-start.15) | collective-permute-done | bytes 524320 | tf_op jit(solution)/shard_map/ppermute | solution.py:407
  69.5 0.1 broadcast_select_fusion.slab_ref
  69.6 1.9 %collective-permute-start.20 = (f32[4,256,128]{2,1,0:T(8,128)S(1)}, f32[4,256,128]{2,1,0:T(8,128)S(1)}, u32[]{:S(2)}, u32[]{:S(2)}) collective-permute-start(f32[4,256,128]{2,1,0:T(8,128)S(1)} %broadcast_select_fusion.slab_ref), channel_id=1, source_target_pairs={{0,1},{1,0},{2,3},{3,2},{4,5},{5,4},{6,7},{7,6},{8,9},{9,8},{10,11... | collective-permute-start | bytes 1572872 | tf_op jit(solution)/shard_map/ppermute | solution.py:427
  71.4 0.0 collective-permute-start.18
  71.4 4.6 %collective-permute-start.17 = (f32[2,72,128]{2,1,0:T(8,128)S(1)}, f32[2,72,128]{2,1,0:T(8,128)S(1)}, u32[]{:S(2)}, u32[]{:S(2)}) collective-permute-start(f32[2,72,128]{2,1,0:T(8,128)S(1)} %pad_maximum_fusion.2), channel_id=1, source_target_pairs={{128,0},{136,8},{144,16},{152,24},{160,32},{168,40},{176,48},{184,... | collective-permute-start | bytes 221192 | tf_op jit(solution)/shard_map/ppermute | solution.py:368
  76.1 0.0 collective-permute-start.16
  76.1 1.5 %collective-permute-done.18 = f32[2,72,128]{2,1,0:T(8,128)S(1)} collective-permute-done((f32[2,72,128]{2,1,0:T(8,128)S(1)}, f32[2,72,128]{2,1,0:T(8,128)S(1)}, u32[]{:S(2)}, u32[]{:S(2)}) %collective-permute-start.18) | collective-permute-done | bytes 73760 | tf_op jit(solution)/shard_map/ppermute | solution.py:368
  77.5 2.5 %collective-permute-done.17 = f32[2,72,128]{2,1,0:T(8,128)S(1)} collective-permute-done((f32[2,72,128]{2,1,0:T(8,128)S(1)}, f32[2,72,128]{2,1,0:T(8,128)S(1)}, u32[]{:S(2)}, u32[]{:S(2)}) %collective-permute-start.17) | collective-permute-done | bytes 73760 | tf_op jit(solution)/shard_map/ppermute | solution.py:368
  80.0 0.0 collective-permute-done.16
  80.0 1.3 %collective-permute-start.19 = (f32[4,2,72,128]{3,2,1,0:T(8,128)S(1)}, f32[4,2,72,128]{3,2,1,0:T(8,128)S(1)}, u32[]{:S(2)}, u32[]{:S(2)}) collective-permute-start(f32[4,2,72,128]{3,2,1,0:T(8,128)S(1)} %pad_maximum_fusion.1.mine_ref), channel_id=1, source_target_pairs={{0,1},{1,0},{2,3},{3,2},{4,5},{5,4},{6,7},{7,6},{8,9},{9,8},{10,11... | collective-permute-start | bytes 884744 | tf_op jit(solution)/shard_map/ppermute | solution.py:429
  81.3 1.2 collective-permute-done.19.other_ref
  82.5 0.0 collective-permute-done.20.twin_ref
  82.6 22.4 %factor_pair.1 = (f32[512,256]{1,0:T(8,128)S(1)}, f32[512,512]{1,0:T(8,128)S(1)}) custom-call(f32[4,2,72,128]{3,2,1,0:T(8,128)S(1)} %pad_maximum_fusion.1.mine_ref, f32[4,2,72,128]{3,2,1,0:T(8,128)S(1)} %collective-permute-done.19.other_ref, f32[4,256,128]{2,1,0:T(8,128)S(1)} %broadcast_select_fusion.slab_ref, ...), custom_call_target="tpu_custom_call" | custom-call | tf_op jit(solution)/shard_map/factor_pair/pallas_call | solution.py:208
  104.9 0.0 all-gather.7.cloned.1.call-done
  105.0 0.0 copy-done
  105.0 12.0 %update.1 = f32[8192,128]{1,0:T(8,128)} custom-call(s32[2,8]{1,0:T(2,128)S(1)} %bitcast.18, f32[8192,128]{1,0:T(8,128)} %bitcast.20, f32[8,4,256,128]{3,2,1,0:T(8,128)} %bitcast.21, f32[512,256]{1,0:T(8,128)S(1)} %get-tuple-element.29.panel_ref, f32[512,512]{1,0:T(8,128)S(1)} %get-tuple-element.30.row_ref), custom_call_target="tpu_custom_call" | custom-call | tf_op jit(solution)/shard_map/update/pallas_call | solution.py:342
  (7 shorter events, 0.1 us)
Async XLA Ops:
  6.5 39.9 %all-gather.5.cloned.1.call-start = ((), (), s32[]{:S(2)}) async-start(), calls=%async_computation | async-start | bytes 1327104 | tf_op jit(solution)/shard_map/all_gather | solution.py:386
  9.6 95.3 %all-gather.7.cloned.1.call-start = ((), (), s32[]{:S(2)}) async-start(), calls=%async_computation.1 | async-start | bytes 4718592 | tf_op jit(solution)/shard_map/all_gather | solution.py:401
  9.6 18.3 %collective-permute-start = (f32[256,128]{1,0:T(8,128)}, f32[256,128]{1,0:T(8,128)S(1)}, u32[]{:S(2)}, u32[]{:S(2)}) collective-permute-start(f32[256,128]{1,0:T(8,128)} %get-tuple-element.18), channel_id=1, source_target_pairs={{0,0},{1,32},{8,9},{9,41},{16,18},{17,50},{24,27},{25,59},{32,36},... | collective-permute-start | bytes 393224 | tf_op jit(solution)/shard_map/ppermute | solution.py:397
  19.9 8.1 %collective-permute-start.1 = (f32[256,128]{1,0:T(8,128)}, f32[256,128]{1,0:T(8,128)S(1)}, u32[]{:S(2)}, u32[]{:S(2)}) collective-permute-start(f32[256,128]{1,0:T(8,128)} %get-tuple-element.19), channel_id=1, source_target_pairs={{0,8},{1,24},{8,17},{9,33},{16,26},{17,42},{24,35},{25,51},{32,44}... | collective-permute-start | bytes 393224 | tf_op jit(solution)/shard_map/ppermute | solution.py:397
  21.2 13.1 %collective-permute-start.2 = (f32[256,128]{1,0:T(8,128)}, f32[256,128]{1,0:T(8,128)S(1)}, u32[]{:S(2)}, u32[]{:S(2)}) collective-permute-start(f32[256,128]{1,0:T(8,128)} %get-tuple-element.20), channel_id=1, source_target_pairs={{0,56},{1,40},{8,1},{9,49},{16,10},{17,58},{24,19},{25,3},{32,28},... | collective-permute-start | bytes 393224 | tf_op jit(solution)/shard_map/ppermute | solution.py:397
  25.3 9.0 %collective-permute-start.3 = (f32[256,128]{1,0:T(8,128)}, f32[256,128]{1,0:T(8,128)S(1)}, u32[]{:S(2)}, u32[]{:S(2)}) collective-permute-start(f32[256,128]{1,0:T(8,128)} %get-tuple-element.21), channel_id=1, source_target_pairs={{0,16},{1,48},{8,25},{9,57},{16,34},{17,2},{24,43},{25,11},{32,52}... | collective-permute-start | bytes 393224 | tf_op jit(solution)/shard_map/ppermute | solution.py:397
  26.6 18.7 %collective-permute-start.7 = (f32[4,256,128]{2,1,0:T(8,128)}, f32[4,256,128]{2,1,0:T(8,128)S(1)}, u32[]{:S(2)}, u32[]{:S(2)}) collective-permute-start(f32[4,256,128]{2,1,0:T(8,128)} %get-tuple-element.23), channel_id=1, source_target_pairs={{0,4},{1,5},{8,12},{9,13},{16,20},{17,21},{24,28},{25,29},{32,36},... | collective-permute-start | bytes 1572872 | tf_op jit(solution)/shard_map/ppermute | solution.py:399
  34.3 6.3 %collective-permute-start.6 = (f32[256,128]{1,0:T(8,128)S(1)}, f32[256,128]{1,0:T(8,128)S(1)}, u32[]{:S(2)}, u32[]{:S(2)}) collective-permute-start(f32[256,128]{1,0:T(8,128)S(1)} %add_add_fusion), channel_id=1, source_target_pairs={{192,0},{200,8},{208,16},{216,24},{224,32},{232,40},{240,48},{248,... | collective-permute-start | bytes 393224 | tf_op jit(solution)/shard_map/ppermute | solution.py:368
  35.6 6.4 %collective-permute-start.5 = (f32[256,128]{1,0:T(8,128)S(1)}, f32[256,128]{1,0:T(8,128)S(1)}, u32[]{:S(2)}, u32[]{:S(2)}) collective-permute-start(f32[256,128]{1,0:T(8,128)S(1)} %add_add_fusion), channel_id=1, source_target_pairs={{128,0},{136,8},{144,16},{152,24},{160,32},{168,40},{176,48},{184,... | collective-permute-start | bytes 393224 | tf_op jit(solution)/shard_map/ppermute | solution.py:368
  38.1 4.5 %collective-permute-start.4 = (f32[256,128]{1,0:T(8,128)S(1)}, f32[256,128]{1,0:T(8,128)S(1)}, u32[]{:S(2)}, u32[]{:S(2)}) collective-permute-start(f32[256,128]{1,0:T(8,128)S(1)} %add_add_fusion), channel_id=1, source_target_pairs={{64,0},{72,8},{80,16},{88,24},{96,32},{104,40},{112,48},{120,56},{... | collective-permute-start | bytes 393224 | tf_op jit(solution)/shard_map/ppermute | solution.py:368
  39.2 65.7 %copy-start = (s32[2,1,8,1]{2,3,1,0:T(1,128)S(1)}, s32[2,1,8,1]{2,3,1,0:T(1,128)}, u32[]{:S(2)}) copy-start(s32[2,1,8,1]{2,3,1,0:T(1,128)} %param.3) | copy-start | bytes 196
  47.5 6.7 %collective-permute-start.8 = (f32[72,128]{1,0:T(8,128)S(1)}, f32[72,128]{1,0:T(8,128)S(1)}, u32[]{:S(2)}, u32[]{:S(2)}) collective-permute-start(f32[72,128]{1,0:T(8,128)S(1)} %get-tuple-element.31), channel_id=1, source_target_pairs={{0,64},{8,72},{1,65},{9,73},{2,66},{10,74},{3,67},{11,75},{4,68},{... | collective-permute-start | bytes 110600 | tf_op jit(solution)/shard_map/ppermute | solution.py:406
  50.7 3.5 %collective-permute-start.10 = (f32[72,128]{1,0:T(8,128)S(1)}, f32[72,128]{1,0:T(8,128)S(1)}, u32[]{:S(2)}, u32[]{:S(2)}) collective-permute-start(f32[72,128]{1,0:T(8,128)S(1)} %get-tuple-element.32), channel_id=1, source_target_pairs={{0,128},{8,136},{1,129},{9,137},{2,130},{10,138},{3,131},{11,139},... | collective-permute-start | bytes 110600 | tf_op jit(solution)/shard_map/ppermute | solution.py:406
  52.9 2.3 %collective-permute-start.9 = (f32[72,128]{1,0:T(8,128)S(1)}, f32[72,128]{1,0:T(8,128)S(1)}, u32[]{:S(2)}, u32[]{:S(2)}) collective-permute-start(f32[72,128]{1,0:T(8,128)S(1)} %get-tuple-element.33), channel_id=1, source_target_pairs={{0,192},{8,200},{1,193},{9,201},{2,194},{10,202},{3,195},{11,203},... | collective-permute-start | bytes 110600 | tf_op jit(solution)/shard_map/ppermute | solution.py:406
  55.3 3.9 %collective-permute-start.12 = (f32[72,128]{1,0:T(8,128)S(1)}, f32[72,128]{1,0:T(8,128)S(1)}, u32[]{:S(2)}, u32[]{:S(2)}) collective-permute-start(f32[72,128]{1,0:T(8,128)S(1)} %add_add_fusion.2), channel_id=1, source_target_pairs={{0,48},{8,56},{64,112},{72,120},{128,176},{136,184},{192,240},{200... | collective-permute-start | bytes 110600 | tf_op jit(solution)/shard_map/ppermute | solution.py:368
  56.6 2.6 %collective-permute-start.11 = (f32[72,128]{1,0:T(8,128)S(1)}, f32[72,128]{1,0:T(8,128)S(1)}, u32[]{:S(2)}, u32[]{:S(2)}) collective-permute-start(f32[72,128]{1,0:T(8,128)S(1)} %add_add_fusion.2), channel_id=1, source_target_pairs={{0,24},{8,32},{64,88},{72,96},{128,152},{136,160},{192,216},{200,2... | collective-permute-start | bytes 110600 | tf_op jit(solution)/shard_map/ppermute | solution.py:368
  57.9 11.6 %collective-permute-start.15 = (f32[4,256,128]{2,1,0:T(8,128)S(1)}, f32[4,256,128]{2,1,0:T(8,128)S(1)}, u32[]{:S(2)}, u32[]{:S(2)}) collective-permute-start(f32[4,256,128]{2,1,0:T(8,128)S(1)} %broadcast_select_fusion.1), channel_id=1, source_target_pairs={{0,2},{1,3},{4,6},{5,7},{8,10},{9,11},{12,14},{13,15},{16,18},{17,... | collective-permute-start | bytes 1572872 | tf_op jit(solution)/shard_map/ppermute | solution.py:407
  59.2 3.8 %collective-permute-start.14 = (f32[72,128]{1,0:T(8,128)S(1)}, f32[72,128]{1,0:T(8,128)S(1)}, u32[]{:S(2)}, u32[]{:S(2)}) collective-permute-start(f32[72,128]{1,0:T(8,128)S(1)} %add_add_fusion.1), channel_id=1, source_target_pairs={{24,16},{48,40},{32,24},{56,48},{88,80},{112,104},{96,88},{120,112... | collective-permute-start | bytes 110600 | tf_op jit(solution)/shard_map/ppermute | solution.py:368
  59.9 8.2 %collective-permute-start.13 = (f32[72,128]{1,0:T(8,128)S(1)}, f32[72,128]{1,0:T(8,128)S(1)}, u32[]{:S(2)}, u32[]{:S(2)}) collective-permute-start(f32[72,128]{1,0:T(8,128)S(1)} %add_add_fusion.1), channel_id=1, source_target_pairs={{0,8},{24,32},{48,56},{8,16},{32,40},{56,0},{64,72},{88,96},{112,1... | collective-permute-start | bytes 110600 | tf_op jit(solution)/shard_map/ppermute | solution.py:368
  69.6 13.0 %collective-permute-start.20 = (f32[4,256,128]{2,1,0:T(8,128)S(1)}, f32[4,256,128]{2,1,0:T(8,128)S(1)}, u32[]{:S(2)}, u32[]{:S(2)}) collective-permute-start(f32[4,256,128]{2,1,0:T(8,128)S(1)} %broadcast_select_fusion.slab_ref), channel_id=1, source_target_pairs={{0,1},{1,0},{2,3},{3,2},{4,5},{5,4},{6,7},{7,6},{8,9},{9,8},{10,11... | collective-permute-start | bytes 1572872 | tf_op jit(solution)/shard_map/ppermute | solution.py:427
  71.4 6.1 %collective-permute-start.18 = (f32[2,72,128]{2,1,0:T(8,128)S(1)}, f32[2,72,128]{2,1,0:T(8,128)S(1)}, u32[]{:S(2)}, u32[]{:S(2)}) collective-permute-start(f32[2,72,128]{2,1,0:T(8,128)S(1)} %pad_maximum_fusion.2), channel_id=1, source_target_pairs={{192,0},{200,8},{208,16},{216,24},{224,32},{232,40},{240,48},{248,... | collective-permute-start | bytes 221192 | tf_op jit(solution)/shard_map/ppermute | solution.py:368
  71.4 8.5 %collective-permute-start.17 = (f32[2,72,128]{2,1,0:T(8,128)S(1)}, f32[2,72,128]{2,1,0:T(8,128)S(1)}, u32[]{:S(2)}, u32[]{:S(2)}) collective-permute-start(f32[2,72,128]{2,1,0:T(8,128)S(1)} %pad_maximum_fusion.2), channel_id=1, source_target_pairs={{128,0},{136,8},{144,16},{152,24},{160,32},{168,40},{176,48},{184,... | collective-permute-start | bytes 221192 | tf_op jit(solution)/shard_map/ppermute | solution.py:368
  76.1 3.9 %collective-permute-start.16 = (f32[2,72,128]{2,1,0:T(8,128)S(1)}, f32[2,72,128]{2,1,0:T(8,128)S(1)}, u32[]{:S(2)}, u32[]{:S(2)}) collective-permute-start(f32[2,72,128]{2,1,0:T(8,128)S(1)} %pad_maximum_fusion.2), channel_id=1, source_target_pairs={{64,0},{72,8},{80,16},{88,24},{96,32},{104,40},{112,48},{120,56},{... | collective-permute-start | bytes 221192 | tf_op jit(solution)/shard_map/ppermute | solution.py:368
  80.0 2.5 %collective-permute-start.19 = (f32[4,2,72,128]{3,2,1,0:T(8,128)S(1)}, f32[4,2,72,128]{3,2,1,0:T(8,128)S(1)}, u32[]{:S(2)}, u32[]{:S(2)}) collective-permute-start(f32[4,2,72,128]{3,2,1,0:T(8,128)S(1)} %pad_maximum_fusion.1.mine_ref), channel_id=1, source_target_pairs={{0,1},{1,0},{2,3},{3,2},{4,5},{5,4},{6,7},{7,6},{8,9},{9,8},{10,11... | collective-permute-start | bytes 884744 | tf_op jit(solution)/shard_map/ppermute | solution.py:429
Sparse Core Ops, SparseCore 0:
  9.7 32.1 all-gather.4
  47.6 55.9 all-gather.6

commit v4 on v3

--- a/solution.py
+++ b/solution.py
@@ -161,7 +161,6 @@
     a01 = jnp.concatenate([upper[0:H], low], axis=0)
     v0 = v0_ref[...]
     pt = dot_nn(v0, a01)
-    p10 = jnp.transpose(pt)
     g_ref[...] = unpack(joined(1, False)) - dot_tn(pt, pt)
     first_u = jnp.transpose(u_ref[...])
     for s, ref in enumerate((r0_ref, r1_ref)):
@@ -181,7 +180,7 @@
 
     factor_block(g_ref, u_ref, v1_ref, beside)
     v1 = v1_ref[...]
-    p10v0 = dot_nn(p10, v0)
+    p10v0 = dot_tn(pt, v0)
     second = dot_nt(r1_ref[...], v1)
     back1 = dot_nn(second, v1)
     row_ref[:, 0:W] = r0_ref[...] - dot_nn(back1, p10v0)
@@ -201,7 +200,7 @@
     def _():
         row_ref[0:W, 0:W] = dot_nn(v1, p10v0)
         row_ref[0:W, W : 2 * W] = -v1
-        panel_ref[0:W, :] = jnp.where(c == 0, p10, jnp.transpose(u_ref[...]))
+        panel_ref[0:W, :] = jnp.transpose(jnp.where(c == 0, pt, u_ref[...]))
 
 
 def factor_pair(mine, other, slab, twin):
@@ -381,7 +380,6 @@
     ]
     swap = [(c, c ^ 1) for c in range(8)]
     groups = [[x * 8 + z for z in range(8)] for x in range(4)]
-    z_place = row_place % 8
 
     across = lax.all_gather(packed, "col")
     held = jnp.where(col_place % 2 == 0, across[0], across[1])
@@ -396,32 +394,27 @@
         ]
         share = share + lax.ppermute(pieces[k], BOTH, pairs)
     line = jnp.stack([share] + around(share, "row", x_moves))
-    slab = jnp.where(col_place < 2, slab, lax.ppermute(slab, "col", [(0, 4), (1, 5)]))
-    line, held, slab = lax.optimization_barrier((line, held, slab))
+    moved = lax.ppermute(slab, "col", [(0, 4), (1, 5)])
+    line, moved = lax.optimization_barrier((line, moved))
     gathered = lax.all_gather(line, "row", axis_index_groups=groups)
+    slab = jnp.where(col_place < 2, slab, moved)
 
     quarters = [held[PIECE * x : PIECE * x + PIECE] for x in range(4)]
     held = jnp.where(row_place < 2, quarters[0], 0.0)
     for x in (1, 3, 2):
         held = held + lax.ppermute(quarters[x], "row", [(z, x * 8 + z) for z in range(2)])
+    start = held
     moved = lax.ppermute(slab, "col", [(0, 2), (1, 3), (4, 6), (5, 7)])
 
-    at_first = (z_place == 0) | (z_place == 3) | (z_place == 6)
-    at_second = (z_place == 1) | (z_place == 4) | (z_place == 7)
-    steps = around(held, "row", [
-        [(x * 8 + z, x * 8 + (z + d) % 8) for x in range(4) for z in range(2)]
-        for d in (3, 6)
+    for d in (2, 6, 4):
+        held = held + lax.ppermute(start, "row", [
+            (x * 8 + z, x * 8 + (z + d) % 8) for x in range(4) for z in range(2)
+        ])
+    after = lax.ppermute(held, "row", [
+        (x * 8 + z, x * 8 + (z + 1) % 8) for x in range(4) for z in range(8)
     ])
-    held = held + steps[0] + steps[1]
-    plus, minus = around(held, "row", [
-        [(x * 8 + z, x * 8 + (z + 1) % 8) for x in range(4) for z in (0, 3, 6, 1, 4, 7)],
-        [(x * 8 + z, x * 8 + z - 1) for x in range(4) for z in (3, 6, 4, 7)],
-    ])
-    either = plus + minus
-    diag = jnp.stack([
-        jnp.where(at_first, held, jnp.where(at_second, plus, minus)),
-        jnp.where(at_first, either, jnp.where(at_second, held, plus)),
-    ])
+    even = row_place % 2 == 0
+    diag = jnp.stack([jnp.where(even, held, after), jnp.where(even, after, held)])
     slab = jnp.where(col_place % 4 < 2, slab, moved)
     diag, slab = lax.optimization_barrier((diag, slab))
     twin = lax.ppermute(slab, "col", swap)

time: 125 us -> 123 us (0.984)
  starting transfers between devices: 45.3 us -> 42.5 us
  waiting for transfers between devices: 24.2 us -> 25.7 us
    ppermute x10 -> x6, starting transfers between devices: 15.9 us -> 8.5 us  [around(): return [lax.ppermute(value, axis, pairs) for pairs in moves]]
    ppermute x10 -> x6, waiting for transfers between devices: 12.3 us -> 7.31 us  [around(): return [lax.ppermute(value, axis, pairs) for pairs in moves]]
    ppermute x1 -> x5, starting transfers between devices: 1.32 us -> 5.87 us  [the longest x3 3.88 us: on_device(): lax.ppermute(start, 'row', [(x * 8 + z, x * 8 + (z + d) % 8) for x in ran...]
    ppermute x1, waiting for transfers between devices: 1.4 us -> 4.56 us  [on_device(): moved = lax.ppermute(slab, 'col', [(0, 2), (1, 3), (4, 6), (5, 7)])]
    all_gather x1, waiting for transfers between devices: 0.02 us -> 2.6 us  [on_device(): gathered = lax.all_gather(line, 'row', axis_index_groups=groups)]
    ppermute x1 -> x5, waiting for transfers between devices: 1.82 us -> 3.59 us  [the longest x1 1.86 us: on_device(): moved = lax.ppermute(slab, 'col', [(0, 4), (1, 5)])]
  transfers between devices with their start and end apart: 23 -> 23, of which waited for: 11 -> 11; matrix products, arithmetic and copies ran while one was open for 2% -> 3% of each run, Pallas kernels for 18% -> 18%
where the time goes in v4:
time: 123 us; the launch traced here: 122 us
  starting transfers between devices  42.5 us (35%)
  Pallas kernels  37.4 us (30%)
  waiting for transfers between devices  25.7 us (21%)
  between operations  13.7 us (11%)
  other arithmetic  3.12 us (3%)
    pallas_call x1, Pallas kernels, factor_pair(): pl.pallas_call(factor_kernel, out_shape=[jax.ShapeDtypeStruct((2 * W, W),...  22.4 us
    ppermute x4, starting transfers between devices, on_device(): share = share + lax.ppermute(pieces[k], BOTH, pairs)  16.9 us
    pallas_call x1, Pallas kernels, update(): pl.pallas_call(update_kernel, in_specs=[pl.BlockSpec(memory_space=pltpu.S...  12 us
    ppermute x6, starting transfers between devices, around(): return [lax.ppermute(value, axis, pairs) for pairs in moves]  8.5 us
    ppermute x6, waiting for transfers between devices, around(): return [lax.ppermute(value, axis, pairs) for pairs in moves]  7.31 us
    ppermute x3, starting transfers between devices, on_device(): lax.ppermute(quarters[x], 'row', [(z, x * 8 + z) for z in range(2)])  6.68 us
    ppermute x4, waiting for transfers between devices, on_device(): share = share + lax.ppermute(pieces[k], BOTH, pairs)  6.36 us
    ppermute x1, waiting for transfers between devices, on_device(): moved = lax.ppermute(slab, 'col', [(0, 2), (1, 3), (4, 6), (5, 7)])  4.56 us
  transfers between devices with their start and end apart: 23, of which 11 were waited for; matrix products, arithmetic and copies ran while one was open for 3% of the time, Pallas kernels for 18%

profile of v4, /device:TPU:1, one launch (start us, length us, event | category | flops | bytes accessed | tf_op | source)
XLA Modules:
  0.0 122.4 jit_solution(10516751030621610050)
XLA Ops:
  6.5 0.0 all-gather.7.cloned.1.call-start
  6.5 3.0 %extract.1 = (f32[4,256,128]{2,1,0:T(8,128)}, f32[288,128]{1,0:T(8,128)}, f32[256,128]{1,0:T(8,128)}, f32[256,128]{1,0:T(8,128)}, f32[256,128]{1,0:T(8,128)}, /*index=5*/f32[256,128]{1,0:T(8,128)}) custom-call(s32[2,8]{1,0:T(2,128)} %bitcast.33, f32[512,16,128]{2,1,0:T(8,128)} %bitcast.35), custom_call_target="tpu_custom_call" | custom-call | tf_op jit(solution)/shard_map/extract/pallas_call | solution.py:256
  9.6 0.0 all-gather.7.cloned.1.call-update
  9.6 0.0 all-gather.5.cloned.1.call-start
  9.6 10.2 %collective-permute-start = (f32[256,128]{1,0:T(8,128)}, f32[256,128]{1,0:T(8,128)S(1)}, u32[]{:S(2)}, u32[]{:S(2)}) collective-permute-start(f32[256,128]{1,0:T(8,128)} %get-tuple-element.17), channel_id=1, source_target_pairs={{0,0},{1,32},{8,9},{9,41},{16,18},{17,50},{24,27},{25,59},{32,36},... | collective-permute-start | bytes 393224 | tf_op jit(solution)/shard_map/ppermute | solution.py:395
  19.9 1.3 %collective-permute-start.1 = (f32[256,128]{1,0:T(8,128)}, f32[256,128]{1,0:T(8,128)S(1)}, u32[]{:S(2)}, u32[]{:S(2)}) collective-permute-start(f32[256,128]{1,0:T(8,128)} %get-tuple-element.18), channel_id=1, source_target_pairs={{0,8},{1,24},{8,17},{9,33},{16,26},{17,42},{24,35},{25,51},{32,44}... | collective-permute-start | bytes 393224 | tf_op jit(solution)/shard_map/ppermute | solution.py:395
  21.2 4.1 %collective-permute-start.2 = (f32[256,128]{1,0:T(8,128)}, f32[256,128]{1,0:T(8,128)S(1)}, u32[]{:S(2)}, u32[]{:S(2)}) collective-permute-start(f32[256,128]{1,0:T(8,128)} %get-tuple-element.19), channel_id=1, source_target_pairs={{0,56},{1,40},{8,1},{9,49},{16,10},{17,58},{24,19},{25,3},{32,28},... | collective-permute-start | bytes 393224 | tf_op jit(solution)/shard_map/ppermute | solution.py:395
  25.3 1.3 %collective-permute-start.3 = (f32[256,128]{1,0:T(8,128)}, f32[256,128]{1,0:T(8,128)S(1)}, u32[]{:S(2)}, u32[]{:S(2)}) collective-permute-start(f32[256,128]{1,0:T(8,128)} %get-tuple-element.20), channel_id=1, source_target_pairs={{0,16},{1,48},{8,25},{9,57},{16,34},{17,2},{24,43},{25,11},{32,52}... | collective-permute-start | bytes 393224 | tf_op jit(solution)/shard_map/ppermute | solution.py:395
  26.6 1.3 %collective-permute-start.7 = (f32[4,256,128]{2,1,0:T(8,128)}, f32[4,256,128]{2,1,0:T(8,128)S(1)}, u32[]{:S(2)}, u32[]{:S(2)}) collective-permute-start(f32[4,256,128]{2,1,0:T(8,128)} %get-tuple-element.21), channel_id=1, source_target_pairs={{0,4},{1,5},{8,12},{9,13},{16,20},{17,21},{24,28},{25,29},{32,36},... | collective-permute-start | bytes 1572872 | tf_op jit(solution)/shard_map/ppermute | solution.py:397
  27.9 0.0 collective-permute-done
  27.9 0.0 collective-permute-done.1
  27.9 6.4 %collective-permute-done.2 = f32[256,128]{1,0:T(8,128)S(1)} collective-permute-done((f32[256,128]{1,0:T(8,128)}, f32[256,128]{1,0:T(8,128)S(1)}, u32[]{:S(2)}, u32[]{:S(2)}) %collective-permute-start.2) | collective-permute-done | bytes 131104 | tf_op jit(solution)/shard_map/ppermute | solution.py:395
  34.3 0.0 collective-permute-done.3
  34.3 1.3 %collective-permute-start.6 = (f32[256,128]{1,0:T(8,128)S(1)}, f32[256,128]{1,0:T(8,128)S(1)}, u32[]{:S(2)}, u32[]{:S(2)}) collective-permute-start(f32[256,128]{1,0:T(8,128)S(1)} %add_add_fusion), channel_id=1, source_target_pairs={{192,0},{200,8},{208,16},{216,24},{224,32},{232,40},{240,48},{248,... | collective-permute-start | bytes 393224 | tf_op jit(solution)/shard_map/ppermute | solution.py:367
  35.6 2.5 %collective-permute-start.5 = (f32[256,128]{1,0:T(8,128)S(1)}, f32[256,128]{1,0:T(8,128)S(1)}, u32[]{:S(2)}, u32[]{:S(2)}) collective-permute-start(f32[256,128]{1,0:T(8,128)S(1)} %add_add_fusion), channel_id=1, source_target_pairs={{128,0},{136,8},{144,16},{152,24},{160,32},{168,40},{176,48},{184,... | collective-permute-start | bytes 393224 | tf_op jit(solution)/shard_map/ppermute | solution.py:367
  38.1 1.2 collective-permute-start.4
  39.2 1.4 %collective-permute-done.6 = f32[256,128]{1,0:T(8,128)S(1)} collective-permute-done((f32[256,128]{1,0:T(8,128)S(1)}, f32[256,128]{1,0:T(8,128)S(1)}, u32[]{:S(2)}, u32[]{:S(2)}) %collective-permute-start.6) | collective-permute-done | bytes 131104 | tf_op jit(solution)/shard_map/ppermute | solution.py:367
  40.6 1.4 %collective-permute-done.5 = f32[256,128]{1,0:T(8,128)S(1)} collective-permute-done((f32[256,128]{1,0:T(8,128)S(1)}, f32[256,128]{1,0:T(8,128)S(1)}, u32[]{:S(2)}, u32[]{:S(2)}) %collective-permute-start.5) | collective-permute-done | bytes 131104 | tf_op jit(solution)/shard_map/ppermute | solution.py:367
  42.0 0.6 collective-permute-done.4
  42.6 0.0 copy-start
  42.6 0.8 pad_maximum_fusion
  43.4 1.9 %collective-permute-done.7 = f32[4,256,128]{2,1,0:T(8,128)S(1)} collective-permute-done((f32[4,256,128]{2,1,0:T(8,128)}, f32[4,256,128]{2,1,0:T(8,128)S(1)}, u32[]{:S(2)}, u32[]{:S(2)}) %collective-permute-start.7) | collective-permute-done | bytes 524320 | tf_op jit(solution)/shard_map/ppermute | solution.py:397
  45.3 0.0 all-gather.5.cloned.1.call-update
  45.3 0.0 all-gather.7.cloned.1.call-done
  45.4 1.0 fusion
  46.4 3.2 %collective-permute-start.8 = (f32[72,128]{1,0:T(8,128)S(1)}, f32[72,128]{1,0:T(8,128)S(1)}, u32[]{:S(2)}, u32[]{:S(2)}) collective-permute-start(f32[72,128]{1,0:T(8,128)S(1)} %get-tuple-element.29), channel_id=1, source_target_pairs={{0,64},{8,72},{1,65},{9,73},{2,66},{10,74},{3,67},{11,75},{4,68},{... | collective-permute-start | bytes 110600 | tf_op jit(solution)/shard_map/ppermute | solution.py:405
  49.6 2.2 %collective-permute-start.10 = (f32[72,128]{1,0:T(8,128)S(1)}, f32[72,128]{1,0:T(8,128)S(1)}, u32[]{:S(2)}, u32[]{:S(2)}) collective-permute-start(f32[72,128]{1,0:T(8,128)S(1)} %get-tuple-element.30), channel_id=1, source_target_pairs={{0,128},{8,136},{1,129},{9,137},{2,130},{10,138},{3,131},{11,139},... | collective-permute-start | bytes 110600 | tf_op jit(solution)/shard_map/ppermute | solution.py:405
  51.8 1.3 %collective-permute-start.9 = (f32[72,128]{1,0:T(8,128)S(1)}, f32[72,128]{1,0:T(8,128)S(1)}, u32[]{:S(2)}, u32[]{:S(2)}) collective-permute-start(f32[72,128]{1,0:T(8,128)S(1)} %get-tuple-element.31), channel_id=1, source_target_pairs={{0,192},{8,200},{1,193},{9,201},{2,194},{10,202},{3,195},{11,203},... | collective-permute-start | bytes 110600 | tf_op jit(solution)/shard_map/ppermute | solution.py:405
  53.1 1.1 broadcast_select_fusion
  54.2 1.3 %collective-permute-start.15 = (f32[4,256,128]{2,1,0:T(8,128)S(1)}, f32[4,256,128]{2,1,0:T(8,128)S(1)}, u32[]{:S(2)}, u32[]{:S(2)}) collective-permute-start(f32[4,256,128]{2,1,0:T(8,128)S(1)} %broadcast_select_fusion), channel_id=1, source_target_pairs={{0,2},{1,3},{4,6},{5,7},{8,10},{9,11},{12,14},{13,15},{16,18},{17,... | collective-permute-start | bytes 1572872 | tf_op jit(solution)/shard_map/ppermute | solution.py:407
  55.6 0.0 collective-permute-done.8
  55.6 0.0 collective-permute-done.10
  55.6 0.0 collective-permute-done.9
  55.6 1.3 %collective-permute-start.13 = (f32[72,128]{1,0:T(8,128)S(1)}, f32[72,128]{1,0:T(8,128)S(1)}, u32[]{:S(2)}, u32[]{:S(2)}) collective-permute-start(f32[72,128]{1,0:T(8,128)S(1)} %fusion.4), channel_id=1, source_target_pairs={{0,32},{8,40},{64,96},{72,104},{128,160},{136,168},{192,224},{200,... | collective-permute-start | bytes 110600 | tf_op jit(solution)/shard_map/ppermute | solution.py:410
  56.9 1.3 %collective-permute-start.12 = (f32[72,128]{1,0:T(8,128)S(1)}, f32[72,128]{1,0:T(8,128)S(1)}, u32[]{:S(2)}, u32[]{:S(2)}) collective-permute-start(f32[72,128]{1,0:T(8,128)S(1)} %fusion.4), channel_id=1, source_target_pairs={{0,48},{8,56},{64,112},{72,120},{128,176},{136,184},{192,240},{200... | collective-permute-start | bytes 110600 | tf_op jit(solution)/shard_map/ppermute | solution.py:410
  58.2 1.3 %collective-permute-start.11 = (f32[72,128]{1,0:T(8,128)S(1)}, f32[72,128]{1,0:T(8,128)S(1)}, u32[]{:S(2)}, u32[]{:S(2)}) collective-permute-start(f32[72,128]{1,0:T(8,128)S(1)} %fusion.4), channel_id=1, source_target_pairs={{0,16},{8,24},{64,80},{72,88},{128,144},{136,152},{192,208},{200,2... | collective-permute-start | bytes 110600 | tf_op jit(solution)/shard_map/ppermute | solution.py:410
  59.6 0.0 collective-permute-done.13
  59.6 0.0 collective-permute-done.12
  59.6 1.7 %collective-permute-done.11 = f32[72,128]{1,0:T(8,128)S(1)} collective-permute-done((f32[72,128]{1,0:T(8,128)S(1)}, f32[72,128]{1,0:T(8,128)S(1)}, u32[]{:S(2)}, u32[]{:S(2)}) %collective-permute-start.11) | collective-permute-done | bytes 36896 | tf_op jit(solution)/shard_map/ppermute | solution.py:410
  61.3 0.7 collective-permute-start.14
  62.0 4.6 %collective-permute-done.15 = f32[4,256,128]{2,1,0:T(8,128)S(1)} collective-permute-done((f32[4,256,128]{2,1,0:T(8,128)S(1)}, f32[4,256,128]{2,1,0:T(8,128)S(1)}, u32[]{:S(2)}, u32[]{:S(2)}) %collective-permute-start.15) | collective-permute-done | bytes 524320 | tf_op jit(solution)/shard_map/ppermute | solution.py:407
  66.5 0.1 broadcast_select_fusion.1.slab_ref
  66.6 0.0 collective-permute-done.14
  66.6 1.8 %collective-permute-start.20 = (f32[4,256,128]{2,1,0:T(8,128)S(1)}, f32[4,256,128]{2,1,0:T(8,128)S(1)}, u32[]{:S(2)}, u32[]{:S(2)}) collective-permute-start(f32[4,256,128]{2,1,0:T(8,128)S(1)} %broadcast_select_fusion.1.slab_ref), channel_id=1, source_target_pairs={{0,1},{1,0},{2,3},{3,2},{4,5},{5,4},{6,7},{7,6},{8,9},{9,8},{10,11... | collective-permute-start | bytes 1572872 | tf_op jit(solution)/shard_map/ppermute | solution.py:420
  68.5 0.2 collective-permute-start.18
  68.7 3.4 %collective-permute-start.17 = (f32[2,72,128]{2,1,0:T(8,128)S(1)}, f32[2,72,128]{2,1,0:T(8,128)S(1)}, u32[]{:S(2)}, u32[]{:S(2)}) collective-permute-start(f32[2,72,128]{2,1,0:T(8,128)S(1)} %pad_maximum_fusion.2), channel_id=1, source_target_pairs={{128,0},{136,8},{144,16},{152,24},{160,32},{168,40},{176,48},{184,... | collective-permute-start | bytes 221192 | tf_op jit(solution)/shard_map/ppermute | solution.py:367
  72.1 0.0 collective-permute-start.16
  72.1 1.5 %collective-permute-done.18 = f32[2,72,128]{2,1,0:T(8,128)S(1)} collective-permute-done((f32[2,72,128]{2,1,0:T(8,128)S(1)}, f32[2,72,128]{2,1,0:T(8,128)S(1)}, u32[]{:S(2)}, u32[]{:S(2)}) %collective-permute-start.18) | collective-permute-done | bytes 73760 | tf_op jit(solution)/shard_map/ppermute | solution.py:367
  73.6 2.4 %collective-permute-done.17 = f32[2,72,128]{2,1,0:T(8,128)S(1)} collective-permute-done((f32[2,72,128]{2,1,0:T(8,128)S(1)}, f32[2,72,128]{2,1,0:T(8,128)S(1)}, u32[]{:S(2)}, u32[]{:S(2)}) %collective-permute-start.17) | collective-permute-done | bytes 73760 | tf_op jit(solution)/shard_map/ppermute | solution.py:367
  76.0 0.0 collective-permute-done.16
  76.1 1.3 %collective-permute-start.19 = (f32[4,2,72,128]{3,2,1,0:T(8,128)S(1)}, f32[4,2,72,128]{3,2,1,0:T(8,128)S(1)}, u32[]{:S(2)}, u32[]{:S(2)}) collective-permute-start(f32[4,2,72,128]{3,2,1,0:T(8,128)S(1)} %pad_maximum_fusion.1.mine_ref), channel_id=1, source_target_pairs={{0,1},{1,0},{2,3},{3,2},{4,5},{5,4},{6,7},{7,6},{8,9},{9,8},{10,11... | collective-permute-start | bytes 884744 | tf_op jit(solution)/shard_map/ppermute | solution.py:422
  77.4 1.2 collective-permute-done.19.other_ref
  78.6 0.0 collective-permute-done.20.twin_ref
  78.6 22.4 %factor_pair.1 = (f32[512,256]{1,0:T(8,128)S(1)}, f32[512,512]{1,0:T(8,128)S(1)}) custom-call(f32[4,2,72,128]{3,2,1,0:T(8,128)S(1)} %pad_maximum_fusion.1.mine_ref, f32[4,2,72,128]{3,2,1,0:T(8,128)S(1)} %collective-permute-done.19.other_ref, f32[4,256,128]{2,1,0:T(8,128)S(1)} %broadcast_select_fusion.1.slab_ref, ...), custom_call_target="tpu_custom_call" | custom-call | tf_op jit(solution)/shard_map/factor_pair/pallas_call | solution.py:207
  101.0 2.6 %all-gather.5.cloned.1.call-done = f32[32,256,128]{2,1,0:T(8,128)} async-done(((f32[4,256,128]{2,1,0:T(8,128)}), f32[32,256,128]{2,1,0:T(8,128)}) %all-gather.5.cloned.1.call-update) | async-done | bytes 4194320 | tf_op jit(solution)/shard_map/all_gather | solution.py:399
  103.6 0.0 copy-done
  103.6 12.0 %update.1 = f32[8192,128]{1,0:T(8,128)} custom-call(s32[2,8]{1,0:T(2,128)S(1)} %bitcast.34, f32[8192,128]{1,0:T(8,128)} %bitcast.36, f32[8,4,256,128]{3,2,1,0:T(8,128)} %bitcast.37, f32[512,256]{1,0:T(8,128)S(1)} %get-tuple-element.27.panel_ref, f32[512,512]{1,0:T(8,128)S(1)} %get-tuple-element.28.row_ref), custom_call_target="tpu_custom_call" | custom-call | tf_op jit(solution)/shard_map/update/pallas_call | solution.py:341
  (7 shorter events, 0.1 us)
Async XLA Ops:
  6.5 38.8 %all-gather.7.cloned.1.call-start = ((), (), s32[]{:S(2)}) async-start(), calls=%async_computation.1 | async-start | bytes 1327104 | tf_op jit(solution)/shard_map/all_gather | solution.py:384
  9.6 94.0 %all-gather.5.cloned.1.call-start = ((), (), s32[]{:S(2)}) async-start(), calls=%async_computation | async-start | bytes 4718592 | tf_op jit(solution)/shard_map/all_gather | solution.py:399
  9.6 18.3 %collective-permute-start = (f32[256,128]{1,0:T(8,128)}, f32[256,128]{1,0:T(8,128)S(1)}, u32[]{:S(2)}, u32[]{:S(2)}) collective-permute-start(f32[256,128]{1,0:T(8,128)} %get-tuple-element.17), channel_id=1, source_target_pairs={{0,0},{1,32},{8,9},{9,41},{16,18},{17,50},{24,27},{25,59},{32,36},... | collective-permute-start | bytes 393224 | tf_op jit(solution)/shard_map/ppermute | solution.py:395
  19.9 8.1 %collective-permute-start.1 = (f32[256,128]{1,0:T(8,128)}, f32[256,128]{1,0:T(8,128)S(1)}, u32[]{:S(2)}, u32[]{:S(2)}) collective-permute-start(f32[256,128]{1,0:T(8,128)} %get-tuple-element.18), channel_id=1, source_target_pairs={{0,8},{1,24},{8,17},{9,33},{16,26},{17,42},{24,35},{25,51},{32,44}... | collective-permute-start | bytes 393224 | tf_op jit(solution)/shard_map/ppermute | solution.py:395
  21.2 13.1 %collective-permute-start.2 = (f32[256,128]{1,0:T(8,128)}, f32[256,128]{1,0:T(8,128)S(1)}, u32[]{:S(2)}, u32[]{:S(2)}) collective-permute-start(f32[256,128]{1,0:T(8,128)} %get-tuple-element.19), channel_id=1, source_target_pairs={{0,56},{1,40},{8,1},{9,49},{16,10},{17,58},{24,19},{25,3},{32,28},... | collective-permute-start | bytes 393224 | tf_op jit(solution)/shard_map/ppermute | solution.py:395
  25.3 9.0 %collective-permute-start.3 = (f32[256,128]{1,0:T(8,128)}, f32[256,128]{1,0:T(8,128)S(1)}, u32[]{:S(2)}, u32[]{:S(2)}) collective-permute-start(f32[256,128]{1,0:T(8,128)} %get-tuple-element.20), channel_id=1, source_target_pairs={{0,16},{1,48},{8,25},{9,57},{16,34},{17,2},{24,43},{25,11},{32,52}... | collective-permute-start | bytes 393224 | tf_op jit(solution)/shard_map/ppermute | solution.py:395
  26.6 18.7 %collective-permute-start.7 = (f32[4,256,128]{2,1,0:T(8,128)}, f32[4,256,128]{2,1,0:T(8,128)S(1)}, u32[]{:S(2)}, u32[]{:S(2)}) collective-permute-start(f32[4,256,128]{2,1,0:T(8,128)} %get-tuple-element.21), channel_id=1, source_target_pairs={{0,4},{1,5},{8,12},{9,13},{16,20},{17,21},{24,28},{25,29},{32,36},... | collective-permute-start | bytes 1572872 | tf_op jit(solution)/shard_map/ppermute | solution.py:397
  34.3 6.3 %collective-permute-start.6 = (f32[256,128]{1,0:T(8,128)S(1)}, f32[256,128]{1,0:T(8,128)S(1)}, u32[]{:S(2)}, u32[]{:S(2)}) collective-permute-start(f32[256,128]{1,0:T(8,128)S(1)} %add_add_fusion), channel_id=1, source_target_pairs={{192,0},{200,8},{208,16},{216,24},{224,32},{232,40},{240,48},{248,... | collective-permute-start | bytes 393224 | tf_op jit(solution)/shard_map/ppermute | solution.py:367
  35.6 6.4 %collective-permute-start.5 = (f32[256,128]{1,0:T(8,128)S(1)}, f32[256,128]{1,0:T(8,128)S(1)}, u32[]{:S(2)}, u32[]{:S(2)}) collective-permute-start(f32[256,128]{1,0:T(8,128)S(1)} %add_add_fusion), channel_id=1, source_target_pairs={{128,0},{136,8},{144,16},{152,24},{160,32},{168,40},{176,48},{184,... | collective-permute-start | bytes 393224 | tf_op jit(solution)/shard_map/ppermute | solution.py:367
  38.1 4.5 %collective-permute-start.4 = (f32[256,128]{1,0:T(8,128)S(1)}, f32[256,128]{1,0:T(8,128)S(1)}, u32[]{:S(2)}, u32[]{:S(2)}) collective-permute-start(f32[256,128]{1,0:T(8,128)S(1)} %add_add_fusion), channel_id=1, source_target_pairs={{64,0},{72,8},{80,16},{88,24},{96,32},{104,40},{112,48},{120,56},{... | collective-permute-start | bytes 393224 | tf_op jit(solution)/shard_map/ppermute | solution.py:367
  42.6 61.0 %copy-start = (s32[2,1,8,1]{2,3,1,0:T(1,128)S(1)}, s32[2,1,8,1]{2,3,1,0:T(1,128)}, u32[]{:S(2)}) copy-start(s32[2,1,8,1]{2,3,1,0:T(1,128)} %param.3) | copy-start | bytes 196
  46.4 9.2 %collective-permute-start.8 = (f32[72,128]{1,0:T(8,128)S(1)}, f32[72,128]{1,0:T(8,128)S(1)}, u32[]{:S(2)}, u32[]{:S(2)}) collective-permute-start(f32[72,128]{1,0:T(8,128)S(1)} %get-tuple-element.29), channel_id=1, source_target_pairs={{0,64},{8,72},{1,65},{9,73},{2,66},{10,74},{3,67},{11,75},{4,68},{... | collective-permute-start | bytes 110600 | tf_op jit(solution)/shard_map/ppermute | solution.py:405
  49.6 6.0 %collective-permute-start.10 = (f32[72,128]{1,0:T(8,128)S(1)}, f32[72,128]{1,0:T(8,128)S(1)}, u32[]{:S(2)}, u32[]{:S(2)}) collective-permute-start(f32[72,128]{1,0:T(8,128)S(1)} %get-tuple-element.30), channel_id=1, source_target_pairs={{0,128},{8,136},{1,129},{9,137},{2,130},{10,138},{3,131},{11,139},... | collective-permute-start | bytes 110600 | tf_op jit(solution)/shard_map/ppermute | solution.py:405
  51.8 3.8 %collective-permute-start.9 = (f32[72,128]{1,0:T(8,128)S(1)}, f32[72,128]{1,0:T(8,128)S(1)}, u32[]{:S(2)}, u32[]{:S(2)}) collective-permute-start(f32[72,128]{1,0:T(8,128)S(1)} %get-tuple-element.31), channel_id=1, source_target_pairs={{0,192},{8,200},{1,193},{9,201},{2,194},{10,202},{3,195},{11,203},... | collective-permute-start | bytes 110600 | tf_op jit(solution)/shard_map/ppermute | solution.py:405
  54.2 12.3 %collective-permute-start.15 = (f32[4,256,128]{2,1,0:T(8,128)S(1)}, f32[4,256,128]{2,1,0:T(8,128)S(1)}, u32[]{:S(2)}, u32[]{:S(2)}) collective-permute-start(f32[4,256,128]{2,1,0:T(8,128)S(1)} %broadcast_select_fusion), channel_id=1, source_target_pairs={{0,2},{1,3},{4,6},{5,7},{8,10},{9,11},{12,14},{13,15},{16,18},{17,... | collective-permute-start | bytes 1572872 | tf_op jit(solution)/shard_map/ppermute | solution.py:407
  55.6 3.9 %collective-permute-start.13 = (f32[72,128]{1,0:T(8,128)S(1)}, f32[72,128]{1,0:T(8,128)S(1)}, u32[]{:S(2)}, u32[]{:S(2)}) collective-permute-start(f32[72,128]{1,0:T(8,128)S(1)} %fusion.4), channel_id=1, source_target_pairs={{0,32},{8,40},{64,96},{72,104},{128,160},{136,168},{192,224},{200,... | collective-permute-start | bytes 110600 | tf_op jit(solution)/shard_map/ppermute | solution.py:410
  56.9 2.6 %collective-permute-start.12 = (f32[72,128]{1,0:T(8,128)S(1)}, f32[72,128]{1,0:T(8,128)S(1)}, u32[]{:S(2)}, u32[]{:S(2)}) collective-permute-start(f32[72,128]{1,0:T(8,128)S(1)} %fusion.4), channel_id=1, source_target_pairs={{0,48},{8,56},{64,112},{72,120},{128,176},{136,184},{192,240},{200... | collective-permute-start | bytes 110600 | tf_op jit(solution)/shard_map/ppermute | solution.py:410
  58.2 3.1 %collective-permute-start.11 = (f32[72,128]{1,0:T(8,128)S(1)}, f32[72,128]{1,0:T(8,128)S(1)}, u32[]{:S(2)}, u32[]{:S(2)}) collective-permute-start(f32[72,128]{1,0:T(8,128)S(1)} %fusion.4), channel_id=1, source_target_pairs={{0,16},{8,24},{64,80},{72,88},{128,144},{136,152},{192,208},{200,2... | collective-permute-start | bytes 110600 | tf_op jit(solution)/shard_map/ppermute | solution.py:410
  61.3 5.3 %collective-permute-start.14 = (f32[72,128]{1,0:T(8,128)S(1)}, f32[72,128]{1,0:T(8,128)S(1)}, u32[]{:S(2)}, u32[]{:S(2)}) collective-permute-start(f32[72,128]{1,0:T(8,128)S(1)} %add_add_fusion.1), channel_id=1, source_target_pairs={{0,8},{8,16},{16,24},{24,32},{32,40},{40,48},{48,56},{56,0},{64,72... | collective-permute-start | bytes 110600 | tf_op jit(solution)/shard_map/ppermute | solution.py:413
  66.6 11.9 %collective-permute-start.20 = (f32[4,256,128]{2,1,0:T(8,128)S(1)}, f32[4,256,128]{2,1,0:T(8,128)S(1)}, u32[]{:S(2)}, u32[]{:S(2)}) collective-permute-start(f32[4,256,128]{2,1,0:T(8,128)S(1)} %broadcast_select_fusion.1.slab_ref), channel_id=1, source_target_pairs={{0,1},{1,0},{2,3},{3,2},{4,5},{5,4},{6,7},{7,6},{8,9},{9,8},{10,11... | collective-permute-start | bytes 1572872 | tf_op jit(solution)/shard_map/ppermute | solution.py:420
  68.5 5.1 %collective-permute-start.18 = (f32[2,72,128]{2,1,0:T(8,128)S(1)}, f32[2,72,128]{2,1,0:T(8,128)S(1)}, u32[]{:S(2)}, u32[]{:S(2)}) collective-permute-start(f32[2,72,128]{2,1,0:T(8,128)S(1)} %pad_maximum_fusion.2), channel_id=1, source_target_pairs={{192,0},{200,8},{208,16},{216,24},{224,32},{232,40},{240,48},{248,... | collective-permute-start | bytes 221192 | tf_op jit(solution)/shard_map/ppermute | solution.py:367
  68.7 7.3 %collective-permute-start.17 = (f32[2,72,128]{2,1,0:T(8,128)S(1)}, f32[2,72,128]{2,1,0:T(8,128)S(1)}, u32[]{:S(2)}, u32[]{:S(2)}) collective-permute-start(f32[2,72,128]{2,1,0:T(8,128)S(1)} %pad_maximum_fusion.2), channel_id=1, source_target_pairs={{128,0},{136,8},{144,16},{152,24},{160,32},{168,40},{176,48},{184,... | collective-permute-start | bytes 221192 | tf_op jit(solution)/shard_map/ppermute | solution.py:367
  72.1 3.9 %collective-permute-start.16 = (f32[2,72,128]{2,1,0:T(8,128)S(1)}, f32[2,72,128]{2,1,0:T(8,128)S(1)}, u32[]{:S(2)}, u32[]{:S(2)}) collective-permute-start(f32[2,72,128]{2,1,0:T(8,128)S(1)} %pad_maximum_fusion.2), channel_id=1, source_target_pairs={{64,0},{72,8},{80,16},{88,24},{96,32},{104,40},{112,48},{120,56},{... | collective-permute-start | bytes 221192 | tf_op jit(solution)/shard_map/ppermute | solution.py:367
  76.1 2.5 %collective-permute-start.19 = (f32[4,2,72,128]{3,2,1,0:T(8,128)S(1)}, f32[4,2,72,128]{3,2,1,0:T(8,128)S(1)}, u32[]{:S(2)}, u32[]{:S(2)}) collective-permute-start(f32[4,2,72,128]{3,2,1,0:T(8,128)S(1)} %pad_maximum_fusion.1.mine_ref), channel_id=1, source_target_pairs={{0,1},{1,0},{2,3},{3,2},{4,5},{5,4},{6,7},{7,6},{8,9},{9,8},{10,11... | collective-permute-start | bytes 884744 | tf_op jit(solution)/shard_map/ppermute | solution.py:422
Sparse Core Ops, SparseCore 0:
  9.7 32.1 all-gather.6
  45.4 58.0 all-gather.4

commit v5 on v4

--- a/solution.py
+++ b/solution.py
@@ -394,7 +394,7 @@
         ]
         share = share + lax.ppermute(pieces[k], BOTH, pairs)
     line = jnp.stack([share] + around(share, "row", x_moves))
-    moved = lax.ppermute(slab, "col", [(0, 4), (1, 5)])
+    moved = lax.ppermute(slab, "col", [(0, 6), (1, 7)])
     line, moved = lax.optimization_barrier((line, moved))
     gathered = lax.all_gather(line, "row", axis_index_groups=groups)
     slab = jnp.where(col_place < 2, slab, moved)
@@ -404,7 +404,7 @@
     for x in (1, 3, 2):
         held = held + lax.ppermute(quarters[x], "row", [(z, x * 8 + z) for z in range(2)])
     start = held
-    moved = lax.ppermute(slab, "col", [(0, 2), (1, 3), (4, 6), (5, 7)])
+    moved = lax.ppermute(slab, "col", [(0, 2), (1, 3), (6, 4), (7, 5)])
 
     for d in (2, 6, 4):
         held = held + lax.ppermute(start, "row", [
@@ -415,7 +415,7 @@
     ])
     even = row_place % 2 == 0
     diag = jnp.stack([jnp.where(even, held, after), jnp.where(even, after, held)])
-    slab = jnp.where(col_place % 4 < 2, slab, moved)
+    slab = jnp.where((col_place < 2) | (col_place > 5), slab, moved)
     diag, slab = lax.optimization_barrier((diag, slab))
     twin = lax.ppermute(slab, "col", swap)
     mine = jnp.stack([diag] + around(diag, "row", x_moves))

time: 123 us -> 121 us (0.984)
  waiting for transfers between devices: 25.7 us -> 22.2 us
  starting transfers between devices: 42.5 us -> 43.8 us
    all_gather x1, waiting for transfers between devices: 2.6 us -> 0.02 us  [on_device(): gathered = lax.all_gather(line, 'row', axis_index_groups=groups)]
    ppermute x2, waiting for transfers between devices: 6.42 us -> 4.14 us  [the longest x1 3.02 us: on_device(): moved = lax.ppermute(slab, 'col', [(0, 2), (1, 3), (6, 4), (7, 5)])]
    ppermute x1, starting transfers between devices: 0.67 us -> 2.14 us  [on_device(): lax.ppermute(held, 'row', [(x * 8 + z, x * 8 + (z + 1) % 8) for x in rang...]
    ppermute x1, waiting for transfers between devices: 0.01 us -> 1.41 us  [on_device(): lax.ppermute(held, 'row', [(x * 8 + z, x * 8 + (z + 1) % 8) for x in rang...]
  transfers between devices with their start and end apart: 23 -> 23, of which waited for: 11 -> 12; matrix products, arithmetic and copies ran while one was open for 3% -> 3% of each run, Pallas kernels for 18% -> 19%
where the time goes in v5:
time: 121 us; the launch traced here: 120 us
  starting transfers between devices  43.8 us (36%)
  Pallas kernels  37.4 us (31%)
  waiting for transfers between devices  22.2 us (18%)
  between operations  13.7 us (11%)
  other arithmetic  3.12 us (3%)
    pallas_call x1, Pallas kernels, factor_pair(): pl.pallas_call(factor_kernel, out_shape=[jax.ShapeDtypeStruct((2 * W, W),...  22.4 us
    ppermute x4, starting transfers between devices, on_device(): share = share + lax.ppermute(pieces[k], BOTH, pairs)  16.9 us
    pallas_call x1, Pallas kernels, update(): pl.pallas_call(update_kernel, in_specs=[pl.BlockSpec(memory_space=pltpu.S...  12 us
    ppermute x6, starting transfers between devices, around(): return [lax.ppermute(value, axis, pairs) for pairs in moves]  8.28 us
    ppermute x6, waiting for transfers between devices, around(): return [lax.ppermute(value, axis, pairs) for pairs in moves]  7.22 us
    ppermute x3, starting transfers between devices, on_device(): lax.ppermute(quarters[x], 'row', [(z, x * 8 + z) for z in range(2)])  6.73 us
    ppermute x4, waiting for transfers between devices, on_device(): share = share + lax.ppermute(pieces[k], BOTH, pairs)  6.36 us
    ppermute x3, starting transfers between devices, on_device(): lax.ppermute(start, 'row', [(x * 8 + z, x * 8 + (z + d) % 8) for x in ran...  3.88 us
  transfers between devices with their start and end apart: 23, of which 12 were waited for; matrix products, arithmetic and copies ran while one was open for 3% of the time, Pallas kernels for 19%

profile of v5, /device:TPU:1, one launch (start us, length us, event | category | flops | bytes accessed | tf_op | source)
XLA Modules:
  0.0 120.2 jit_solution(8839301822176245551)
XLA Ops:
  6.5 0.0 all-gather.7.cloned.1.call-start
  6.5 3.0 %extract.1 = (f32[4,256,128]{2,1,0:T(8,128)}, f32[288,128]{1,0:T(8,128)}, f32[256,128]{1,0:T(8,128)}, f32[256,128]{1,0:T(8,128)}, f32[256,128]{1,0:T(8,128)}, /*index=5*/f32[256,128]{1,0:T(8,128)}) custom-call(s32[2,8]{1,0:T(2,128)} %bitcast.33, f32[512,16,128]{2,1,0:T(8,128)} %bitcast.35), custom_call_target="tpu_custom_call" | custom-call | tf_op jit(solution)/shard_map/extract/pallas_call | solution.py:256
  9.6 0.0 all-gather.7.cloned.1.call-update
  9.6 0.0 all-gather.5.cloned.1.call-start
  9.6 10.2 %collective-permute-start = (f32[256,128]{1,0:T(8,128)}, f32[256,128]{1,0:T(8,128)S(1)}, u32[]{:S(2)}, u32[]{:S(2)}) collective-permute-start(f32[256,128]{1,0:T(8,128)} %get-tuple-element.17), channel_id=1, source_target_pairs={{0,0},{1,32},{8,9},{9,41},{16,18},{17,50},{24,27},{25,59},{32,36},... | collective-permute-start | bytes 393224 | tf_op jit(solution)/shard_map/ppermute | solution.py:395
  19.9 1.3 %collective-permute-start.1 = (f32[256,128]{1,0:T(8,128)}, f32[256,128]{1,0:T(8,128)S(1)}, u32[]{:S(2)}, u32[]{:S(2)}) collective-permute-start(f32[256,128]{1,0:T(8,128)} %get-tuple-element.18), channel_id=1, source_target_pairs={{0,8},{1,24},{8,17},{9,33},{16,26},{17,42},{24,35},{25,51},{32,44}... | collective-permute-start | bytes 393224 | tf_op jit(solution)/shard_map/ppermute | solution.py:395
  21.2 4.1 %collective-permute-start.2 = (f32[256,128]{1,0:T(8,128)}, f32[256,128]{1,0:T(8,128)S(1)}, u32[]{:S(2)}, u32[]{:S(2)}) collective-permute-start(f32[256,128]{1,0:T(8,128)} %get-tuple-element.19), channel_id=1, source_target_pairs={{0,56},{1,40},{8,1},{9,49},{16,10},{17,58},{24,19},{25,3},{32,28},... | collective-permute-start | bytes 393224 | tf_op jit(solution)/shard_map/ppermute | solution.py:395
  25.3 1.3 %collective-permute-start.3 = (f32[256,128]{1,0:T(8,128)}, f32[256,128]{1,0:T(8,128)S(1)}, u32[]{:S(2)}, u32[]{:S(2)}) collective-permute-start(f32[256,128]{1,0:T(8,128)} %get-tuple-element.20), channel_id=1, source_target_pairs={{0,16},{1,48},{8,25},{9,57},{16,34},{17,2},{24,43},{25,11},{32,52}... | collective-permute-start | bytes 393224 | tf_op jit(solution)/shard_map/ppermute | solution.py:395
  26.6 1.3 %collective-permute-start.7 = (f32[4,256,128]{2,1,0:T(8,128)}, f32[4,256,128]{2,1,0:T(8,128)S(1)}, u32[]{:S(2)}, u32[]{:S(2)}) collective-permute-start(f32[4,256,128]{2,1,0:T(8,128)} %get-tuple-element.21), channel_id=1, source_target_pairs={{0,6},{1,7},{8,14},{9,15},{16,22},{17,23},{24,30},{25,31},{32,38},... | collective-permute-start | bytes 1572872 | tf_op jit(solution)/shard_map/ppermute | solution.py:397
  27.9 0.0 collective-permute-done
  27.9 0.0 collective-permute-done.1
  27.9 6.4 %collective-permute-done.2 = f32[256,128]{1,0:T(8,128)S(1)} collective-permute-done((f32[256,128]{1,0:T(8,128)}, f32[256,128]{1,0:T(8,128)S(1)}, u32[]{:S(2)}, u32[]{:S(2)}) %collective-permute-start.2) | collective-permute-done | bytes 131104 | tf_op jit(solution)/shard_map/ppermute | solution.py:395
  34.3 0.0 collective-permute-done.3
  34.3 0.0 copy-start
  34.3 1.3 %collective-permute-start.6 = (f32[256,128]{1,0:T(8,128)S(1)}, f32[256,128]{1,0:T(8,128)S(1)}, u32[]{:S(2)}, u32[]{:S(2)}) collective-permute-start(f32[256,128]{1,0:T(8,128)S(1)} %add_add_fusion), channel_id=1, source_target_pairs={{192,0},{200,8},{208,16},{216,24},{224,32},{232,40},{240,48},{248,... | collective-permute-start | bytes 393224 | tf_op jit(solution)/shard_map/ppermute | solution.py:367
  35.6 2.5 %collective-permute-start.5 = (f32[256,128]{1,0:T(8,128)S(1)}, f32[256,128]{1,0:T(8,128)S(1)}, u32[]{:S(2)}, u32[]{:S(2)}) collective-permute-start(f32[256,128]{1,0:T(8,128)S(1)} %add_add_fusion), channel_id=1, source_target_pairs={{128,0},{136,8},{144,16},{152,24},{160,32},{168,40},{176,48},{184,... | collective-permute-start | bytes 393224 | tf_op jit(solution)/shard_map/ppermute | solution.py:367
  38.1 1.2 collective-permute-start.4
  39.2 1.4 %collective-permute-done.6 = f32[256,128]{1,0:T(8,128)S(1)} collective-permute-done((f32[256,128]{1,0:T(8,128)S(1)}, f32[256,128]{1,0:T(8,128)S(1)}, u32[]{:S(2)}, u32[]{:S(2)}) %collective-permute-start.6) | collective-permute-done | bytes 131104 | tf_op jit(solution)/shard_map/ppermute | solution.py:367
  40.6 1.4 %collective-permute-done.5 = f32[256,128]{1,0:T(8,128)S(1)} collective-permute-done((f32[256,128]{1,0:T(8,128)S(1)}, f32[256,128]{1,0:T(8,128)S(1)}, u32[]{:S(2)}, u32[]{:S(2)}) %collective-permute-start.5) | collective-permute-done | bytes 131104 | tf_op jit(solution)/shard_map/ppermute | solution.py:367
  42.0 0.6 collective-permute-done.4
  42.6 0.8 pad_maximum_fusion
  43.4 1.1 collective-permute-done.7
  44.6 0.0 all-gather.5.cloned.1.call-update
  44.6 0.0 all-gather.7.cloned.1.call-done
  44.6 1.0 fusion
  45.7 3.3 %collective-permute-start.8 = (f32[72,128]{1,0:T(8,128)S(1)}, f32[72,128]{1,0:T(8,128)S(1)}, u32[]{:S(2)}, u32[]{:S(2)}) collective-permute-start(f32[72,128]{1,0:T(8,128)S(1)} %get-tuple-element.29), channel_id=1, source_target_pairs={{0,64},{8,72},{1,65},{9,73},{2,66},{10,74},{3,67},{11,75},{4,68},{... | collective-permute-start | bytes 110600 | tf_op jit(solution)/shard_map/ppermute | solution.py:405
  48.9 2.2 %collective-permute-start.10 = (f32[72,128]{1,0:T(8,128)S(1)}, f32[72,128]{1,0:T(8,128)S(1)}, u32[]{:S(2)}, u32[]{:S(2)}) collective-permute-start(f32[72,128]{1,0:T(8,128)S(1)} %get-tuple-element.30), channel_id=1, source_target_pairs={{0,128},{8,136},{1,129},{9,137},{2,130},{10,138},{3,131},{11,139},... | collective-permute-start | bytes 110600 | tf_op jit(solution)/shard_map/ppermute | solution.py:405
  51.1 1.3 %collective-permute-start.9 = (f32[72,128]{1,0:T(8,128)S(1)}, f32[72,128]{1,0:T(8,128)S(1)}, u32[]{:S(2)}, u32[]{:S(2)}) collective-permute-start(f32[72,128]{1,0:T(8,128)S(1)} %get-tuple-element.31), channel_id=1, source_target_pairs={{0,192},{8,200},{1,193},{9,201},{2,194},{10,202},{3,195},{11,203},... | collective-permute-start | bytes 110600 | tf_op jit(solution)/shard_map/ppermute | solution.py:405
  52.4 1.1 broadcast_select_fusion
  53.6 1.3 %collective-permute-start.15 = (f32[4,256,128]{2,1,0:T(8,128)S(1)}, f32[4,256,128]{2,1,0:T(8,128)S(1)}, u32[]{:S(2)}, u32[]{:S(2)}) collective-permute-start(f32[4,256,128]{2,1,0:T(8,128)S(1)} %broadcast_select_fusion), channel_id=1, source_target_pairs={{0,2},{1,3},{6,4},{7,5},{8,10},{9,11},{14,12},{15,13},{16,18},{17,... | collective-permute-start | bytes 1572872 | tf_op jit(solution)/shard_map/ppermute | solution.py:407
  54.9 0.0 collective-permute-done.8
  54.9 0.0 collective-permute-done.10
  54.9 0.0 collective-permute-done.9
  54.9 1.3 %collective-permute-start.13 = (f32[72,128]{1,0:T(8,128)S(1)}, f32[72,128]{1,0:T(8,128)S(1)}, u32[]{:S(2)}, u32[]{:S(2)}) collective-permute-start(f32[72,128]{1,0:T(8,128)S(1)} %fusion.4), channel_id=1, source_target_pairs={{0,32},{8,40},{64,96},{72,104},{128,160},{136,168},{192,224},{200,... | collective-permute-start | bytes 110600 | tf_op jit(solution)/shard_map/ppermute | solution.py:410
  56.2 1.3 %collective-permute-start.12 = (f32[72,128]{1,0:T(8,128)S(1)}, f32[72,128]{1,0:T(8,128)S(1)}, u32[]{:S(2)}, u32[]{:S(2)}) collective-permute-start(f32[72,128]{1,0:T(8,128)S(1)} %fusion.4), channel_id=1, source_target_pairs={{0,48},{8,56},{64,112},{72,120},{128,176},{136,184},{192,240},{200... | collective-permute-start | bytes 110600 | tf_op jit(solution)/shard_map/ppermute | solution.py:410
  57.5 1.3 %collective-permute-start.11 = (f32[72,128]{1,0:T(8,128)S(1)}, f32[72,128]{1,0:T(8,128)S(1)}, u32[]{:S(2)}, u32[]{:S(2)}) collective-permute-start(f32[72,128]{1,0:T(8,128)S(1)} %fusion.4), channel_id=1, source_target_pairs={{0,16},{8,24},{64,80},{72,88},{128,144},{136,152},{192,208},{200,2... | collective-permute-start | bytes 110600 | tf_op jit(solution)/shard_map/ppermute | solution.py:410
  58.9 0.0 collective-permute-done.13
  58.9 0.1 collective-permute-done.12
  59.0 1.6 %collective-permute-done.11 = f32[72,128]{1,0:T(8,128)S(1)} collective-permute-done((f32[72,128]{1,0:T(8,128)S(1)}, f32[72,128]{1,0:T(8,128)S(1)}, u32[]{:S(2)}, u32[]{:S(2)}) %collective-permute-start.11) | collective-permute-done | bytes 36896 | tf_op jit(solution)/shard_map/ppermute | solution.py:410
  60.6 2.1 %collective-permute-start.14 = (f32[72,128]{1,0:T(8,128)S(1)}, f32[72,128]{1,0:T(8,128)S(1)}, u32[]{:S(2)}, u32[]{:S(2)}) collective-permute-start(f32[72,128]{1,0:T(8,128)S(1)} %add_add_fusion.1), channel_id=1, source_target_pairs={{0,8},{8,16},{16,24},{24,32},{32,40},{40,48},{48,56},{56,0},{64,72... | collective-permute-start | bytes 110600 | tf_op jit(solution)/shard_map/ppermute | solution.py:413
  62.8 3.0 %collective-permute-done.15 = f32[4,256,128]{2,1,0:T(8,128)S(1)} collective-permute-done((f32[4,256,128]{2,1,0:T(8,128)S(1)}, f32[4,256,128]{2,1,0:T(8,128)S(1)}, u32[]{:S(2)}, u32[]{:S(2)}) %collective-permute-start.15) | collective-permute-done | bytes 524320 | tf_op jit(solution)/shard_map/ppermute | solution.py:407
  65.8 0.1 broadcast_select_fusion.1.slab_ref
  65.8 1.4 %collective-permute-done.14 = f32[72,128]{1,0:T(8,128)S(1)} collective-permute-done((f32[72,128]{1,0:T(8,128)S(1)}, f32[72,128]{1,0:T(8,128)S(1)}, u32[]{:S(2)}, u32[]{:S(2)}) %collective-permute-start.14) | collective-permute-done | bytes 36896 | tf_op jit(solution)/shard_map/ppermute | solution.py:413
  67.3 1.8 %collective-permute-start.20 = (f32[4,256,128]{2,1,0:T(8,128)S(1)}, f32[4,256,128]{2,1,0:T(8,128)S(1)}, u32[]{:S(2)}, u32[]{:S(2)}) collective-permute-start(f32[4,256,128]{2,1,0:T(8,128)S(1)} %broadcast_select_fusion.1.slab_ref), channel_id=1, source_target_pairs={{0,1},{1,0},{2,3},{3,2},{4,5},{5,4},{6,7},{7,6},{8,9},{9,8},{10,11... | collective-permute-start | bytes 1572872 | tf_op jit(solution)/shard_map/ppermute | solution.py:420
  69.1 0.5 collective-permute-start.18
  69.6 2.8 %collective-permute-start.17 = (f32[2,72,128]{2,1,0:T(8,128)S(1)}, f32[2,72,128]{2,1,0:T(8,128)S(1)}, u32[]{:S(2)}, u32[]{:S(2)}) collective-permute-start(f32[2,72,128]{2,1,0:T(8,128)S(1)} %pad_maximum_fusion.2), channel_id=1, source_target_pairs={{128,0},{136,8},{144,16},{152,24},{160,32},{168,40},{176,48},{184,... | collective-permute-start | bytes 221192 | tf_op jit(solution)/shard_map/ppermute | solution.py:367
  72.4 0.1 collective-permute-start.16
  72.5 1.8 %collective-permute-done.18 = f32[2,72,128]{2,1,0:T(8,128)S(1)} collective-permute-done((f32[2,72,128]{2,1,0:T(8,128)S(1)}, f32[2,72,128]{2,1,0:T(8,128)S(1)}, u32[]{:S(2)}, u32[]{:S(2)}) %collective-permute-start.18) | collective-permute-done | bytes 73760 | tf_op jit(solution)/shard_map/ppermute | solution.py:367
  74.3 2.1 %collective-permute-done.17 = f32[2,72,128]{2,1,0:T(8,128)S(1)} collective-permute-done((f32[2,72,128]{2,1,0:T(8,128)S(1)}, f32[2,72,128]{2,1,0:T(8,128)S(1)}, u32[]{:S(2)}, u32[]{:S(2)}) %collective-permute-start.17) | collective-permute-done | bytes 73760 | tf_op jit(solution)/shard_map/ppermute | solution.py:367
  76.3 0.0 collective-permute-done.16
  76.4 1.3 %collective-permute-start.19 = (f32[4,2,72,128]{3,2,1,0:T(8,128)S(1)}, f32[4,2,72,128]{3,2,1,0:T(8,128)S(1)}, u32[]{:S(2)}, u32[]{:S(2)}) collective-permute-start(f32[4,2,72,128]{3,2,1,0:T(8,128)S(1)} %pad_maximum_fusion.1.mine_ref), channel_id=1, source_target_pairs={{0,1},{1,0},{2,3},{3,2},{4,5},{5,4},{6,7},{7,6},{8,9},{9,8},{10,11... | collective-permute-start | bytes 884744 | tf_op jit(solution)/shard_map/ppermute | solution.py:422
  77.7 1.2 %collective-permute-done.19.other_ref = f32[4,2,72,128]{3,2,1,0:T(8,128)S(1)} collective-permute-done((f32[4,2,72,128]{3,2,1,0:T(8,128)S(1)}, f32[4,2,72,128]{3,2,1,0:T(8,128)S(1)}, u32[]{:S(2)}, u32[]{:S(2)}) %collective-permute-start.19) | collective-permute-done | bytes 294944 | tf_op jit(solution)/shard_map/ppermute | solution.py:422
  78.9 0.0 collective-permute-done.20.twin_ref
  78.9 22.4 %factor_pair.1 = (f32[512,256]{1,0:T(8,128)S(1)}, f32[512,512]{1,0:T(8,128)S(1)}) custom-call(f32[4,2,72,128]{3,2,1,0:T(8,128)S(1)} %pad_maximum_fusion.1.mine_ref, f32[4,2,72,128]{3,2,1,0:T(8,128)S(1)} %collective-permute-done.19.other_ref, f32[4,256,128]{2,1,0:T(8,128)S(1)} %broadcast_select_fusion.1.slab_ref, ...), custom_call_target="tpu_custom_call" | custom-call | tf_op jit(solution)/shard_map/factor_pair/pallas_call | solution.py:207
  101.3 0.0 all-gather.5.cloned.1.call-done
  101.3 0.0 copy-done
  101.3 12.0 %update.1 = f32[8192,128]{1,0:T(8,128)} custom-call(s32[2,8]{1,0:T(2,128)S(1)} %bitcast.34, f32[8192,128]{1,0:T(8,128)} %bitcast.36, f32[8,4,256,128]{3,2,1,0:T(8,128)} %bitcast.37, f32[512,256]{1,0:T(8,128)S(1)} %get-tuple-element.27.panel_ref, f32[512,512]{1,0:T(8,128)S(1)} %get-tuple-element.28.row_ref), custom_call_target="tpu_custom_call" | custom-call | tf_op jit(solution)/shard_map/update/pallas_call | solution.py:341
  (7 shorter events, 0.1 us)
Async XLA Ops:
  6.5 38.1 %all-gather.7.cloned.1.call-start = ((), (), s32[]{:S(2)}) async-start(), calls=%async_computation.1 | async-start | bytes 1327104 | tf_op jit(solution)/shard_map/all_gather | solution.py:384
  9.6 91.7 %all-gather.5.cloned.1.call-start = ((), (), s32[]{:S(2)}) async-start(), calls=%async_computation | async-start | bytes 4718592 | tf_op jit(solution)/shard_map/all_gather | solution.py:399
  9.6 18.3 %collective-permute-start = (f32[256,128]{1,0:T(8,128)}, f32[256,128]{1,0:T(8,128)S(1)}, u32[]{:S(2)}, u32[]{:S(2)}) collective-permute-start(f32[256,128]{1,0:T(8,128)} %get-tuple-element.17), channel_id=1, source_target_pairs={{0,0},{1,32},{8,9},{9,41},{16,18},{17,50},{24,27},{25,59},{32,36},... | collective-permute-start | bytes 393224 | tf_op jit(solution)/shard_map/ppermute | solution.py:395
  19.9 8.1 %collective-permute-start.1 = (f32[256,128]{1,0:T(8,128)}, f32[256,128]{1,0:T(8,128)S(1)}, u32[]{:S(2)}, u32[]{:S(2)}) collective-permute-start(f32[256,128]{1,0:T(8,128)} %get-tuple-element.18), channel_id=1, source_target_pairs={{0,8},{1,24},{8,17},{9,33},{16,26},{17,42},{24,35},{25,51},{32,44}... | collective-permute-start | bytes 393224 | tf_op jit(solution)/shard_map/ppermute | solution.py:395
  21.2 13.1 %collective-permute-start.2 = (f32[256,128]{1,0:T(8,128)}, f32[256,128]{1,0:T(8,128)S(1)}, u32[]{:S(2)}, u32[]{:S(2)}) collective-permute-start(f32[256,128]{1,0:T(8,128)} %get-tuple-element.19), channel_id=1, source_target_pairs={{0,56},{1,40},{8,1},{9,49},{16,10},{17,58},{24,19},{25,3},{32,28},... | collective-permute-start | bytes 393224 | tf_op jit(solution)/shard_map/ppermute | solution.py:395
  25.3 9.0 %collective-permute-start.3 = (f32[256,128]{1,0:T(8,128)}, f32[256,128]{1,0:T(8,128)S(1)}, u32[]{:S(2)}, u32[]{:S(2)}) collective-permute-start(f32[256,128]{1,0:T(8,128)} %get-tuple-element.20), channel_id=1, source_target_pairs={{0,16},{1,48},{8,25},{9,57},{16,34},{17,2},{24,43},{25,11},{32,52}... | collective-permute-start | bytes 393224 | tf_op jit(solution)/shard_map/ppermute | solution.py:395
  26.6 18.0 %collective-permute-start.7 = (f32[4,256,128]{2,1,0:T(8,128)}, f32[4,256,128]{2,1,0:T(8,128)S(1)}, u32[]{:S(2)}, u32[]{:S(2)}) collective-permute-start(f32[4,256,128]{2,1,0:T(8,128)} %get-tuple-element.21), channel_id=1, source_target_pairs={{0,6},{1,7},{8,14},{9,15},{16,22},{17,23},{24,30},{25,31},{32,38},... | collective-permute-start | bytes 1572872 | tf_op jit(solution)/shard_map/ppermute | solution.py:397
  34.3 67.0 %copy-start = (s32[2,1,8,1]{2,3,1,0:T(1,128)S(1)}, s32[2,1,8,1]{2,3,1,0:T(1,128)}, u32[]{:S(2)}) copy-start(s32[2,1,8,1]{2,3,1,0:T(1,128)} %param.3) | copy-start | bytes 196
  34.3 6.3 %collective-permute-start.6 = (f32[256,128]{1,0:T(8,128)S(1)}, f32[256,128]{1,0:T(8,128)S(1)}, u32[]{:S(2)}, u32[]{:S(2)}) collective-permute-start(f32[256,128]{1,0:T(8,128)S(1)} %add_add_fusion), channel_id=1, source_target_pairs={{192,0},{200,8},{208,16},{216,24},{224,32},{232,40},{240,48},{248,... | collective-permute-start | bytes 393224 | tf_op jit(solution)/shard_map/ppermute | solution.py:367
  35.6 6.4 %collective-permute-start.5 = (f32[256,128]{1,0:T(8,128)S(1)}, f32[256,128]{1,0:T(8,128)S(1)}, u32[]{:S(2)}, u32[]{:S(2)}) collective-permute-start(f32[256,128]{1,0:T(8,128)S(1)} %add_add_fusion), channel_id=1, source_target_pairs={{128,0},{136,8},{144,16},{152,24},{160,32},{168,40},{176,48},{184,... | collective-permute-start | bytes 393224 | tf_op jit(solution)/shard_map/ppermute | solution.py:367
  38.1 4.5 %collective-permute-start.4 = (f32[256,128]{1,0:T(8,128)S(1)}, f32[256,128]{1,0:T(8,128)S(1)}, u32[]{:S(2)}, u32[]{:S(2)}) collective-permute-start(f32[256,128]{1,0:T(8,128)S(1)} %add_add_fusion), channel_id=1, source_target_pairs={{64,0},{72,8},{80,16},{88,24},{96,32},{104,40},{112,48},{120,56},{... | collective-permute-start | bytes 393224 | tf_op jit(solution)/shard_map/ppermute | solution.py:367
  45.7 9.2 %collective-permute-start.8 = (f32[72,128]{1,0:T(8,128)S(1)}, f32[72,128]{1,0:T(8,128)S(1)}, u32[]{:S(2)}, u32[]{:S(2)}) collective-permute-start(f32[72,128]{1,0:T(8,128)S(1)} %get-tuple-element.29), channel_id=1, source_target_pairs={{0,64},{8,72},{1,65},{9,73},{2,66},{10,74},{3,67},{11,75},{4,68},{... | collective-permute-start | bytes 110600 | tf_op jit(solution)/shard_map/ppermute | solution.py:405
  48.9 6.0 %collective-permute-start.10 = (f32[72,128]{1,0:T(8,128)S(1)}, f32[72,128]{1,0:T(8,128)S(1)}, u32[]{:S(2)}, u32[]{:S(2)}) collective-permute-start(f32[72,128]{1,0:T(8,128)S(1)} %get-tuple-element.30), channel_id=1, source_target_pairs={{0,128},{8,136},{1,129},{9,137},{2,130},{10,138},{3,131},{11,139},... | collective-permute-start | bytes 110600 | tf_op jit(solution)/shard_map/ppermute | solution.py:405
  51.1 3.8 %collective-permute-start.9 = (f32[72,128]{1,0:T(8,128)S(1)}, f32[72,128]{1,0:T(8,128)S(1)}, u32[]{:S(2)}, u32[]{:S(2)}) collective-permute-start(f32[72,128]{1,0:T(8,128)S(1)} %get-tuple-element.31), channel_id=1, source_target_pairs={{0,192},{8,200},{1,193},{9,201},{2,194},{10,202},{3,195},{11,203},... | collective-permute-start | bytes 110600 | tf_op jit(solution)/shard_map/ppermute | solution.py:405
  53.6 12.2 %collective-permute-start.15 = (f32[4,256,128]{2,1,0:T(8,128)S(1)}, f32[4,256,128]{2,1,0:T(8,128)S(1)}, u32[]{:S(2)}, u32[]{:S(2)}) collective-permute-start(f32[4,256,128]{2,1,0:T(8,128)S(1)} %broadcast_select_fusion), channel_id=1, source_target_pairs={{0,2},{1,3},{6,4},{7,5},{8,10},{9,11},{14,12},{15,13},{16,18},{17,... | collective-permute-start | bytes 1572872 | tf_op jit(solution)/shard_map/ppermute | solution.py:407
  54.9 3.9 %collective-permute-start.13 = (f32[72,128]{1,0:T(8,128)S(1)}, f32[72,128]{1,0:T(8,128)S(1)}, u32[]{:S(2)}, u32[]{:S(2)}) collective-permute-start(f32[72,128]{1,0:T(8,128)S(1)} %fusion.4), channel_id=1, source_target_pairs={{0,32},{8,40},{64,96},{72,104},{128,160},{136,168},{192,224},{200,... | collective-permute-start | bytes 110600 | tf_op jit(solution)/shard_map/ppermute | solution.py:410
  56.2 2.8 %collective-permute-start.12 = (f32[72,128]{1,0:T(8,128)S(1)}, f32[72,128]{1,0:T(8,128)S(1)}, u32[]{:S(2)}, u32[]{:S(2)}) collective-permute-start(f32[72,128]{1,0:T(8,128)S(1)} %fusion.4), channel_id=1, source_target_pairs={{0,48},{8,56},{64,112},{72,120},{128,176},{136,184},{192,240},{200... | collective-permute-start | bytes 110600 | tf_op jit(solution)/shard_map/ppermute | solution.py:410
  57.5 3.1 %collective-permute-start.11 = (f32[72,128]{1,0:T(8,128)S(1)}, f32[72,128]{1,0:T(8,128)S(1)}, u32[]{:S(2)}, u32[]{:S(2)}) collective-permute-start(f32[72,128]{1,0:T(8,128)S(1)} %fusion.4), channel_id=1, source_target_pairs={{0,16},{8,24},{64,80},{72,88},{128,144},{136,152},{192,208},{200,2... | collective-permute-start | bytes 110600 | tf_op jit(solution)/shard_map/ppermute | solution.py:410
  60.6 6.6 %collective-permute-start.14 = (f32[72,128]{1,0:T(8,128)S(1)}, f32[72,128]{1,0:T(8,128)S(1)}, u32[]{:S(2)}, u32[]{:S(2)}) collective-permute-start(f32[72,128]{1,0:T(8,128)S(1)} %add_add_fusion.1), channel_id=1, source_target_pairs={{0,8},{8,16},{16,24},{24,32},{32,40},{40,48},{48,56},{56,0},{64,72... | collective-permute-start | bytes 110600 | tf_op jit(solution)/shard_map/ppermute | solution.py:413
  67.3 11.6 %collective-permute-start.20 = (f32[4,256,128]{2,1,0:T(8,128)S(1)}, f32[4,256,128]{2,1,0:T(8,128)S(1)}, u32[]{:S(2)}, u32[]{:S(2)}) collective-permute-start(f32[4,256,128]{2,1,0:T(8,128)S(1)} %broadcast_select_fusion.1.slab_ref), channel_id=1, source_target_pairs={{0,1},{1,0},{2,3},{3,2},{4,5},{5,4},{6,7},{7,6},{8,9},{9,8},{10,11... | collective-permute-start | bytes 1572872 | tf_op jit(solution)/shard_map/ppermute | solution.py:420
  69.1 5.1 %collective-permute-start.18 = (f32[2,72,128]{2,1,0:T(8,128)S(1)}, f32[2,72,128]{2,1,0:T(8,128)S(1)}, u32[]{:S(2)}, u32[]{:S(2)}) collective-permute-start(f32[2,72,128]{2,1,0:T(8,128)S(1)} %pad_maximum_fusion.2), channel_id=1, source_target_pairs={{192,0},{200,8},{208,16},{216,24},{224,32},{232,40},{240,48},{248,... | collective-permute-start | bytes 221192 | tf_op jit(solution)/shard_map/ppermute | solution.py:367
  69.6 6.7 %collective-permute-start.17 = (f32[2,72,128]{2,1,0:T(8,128)S(1)}, f32[2,72,128]{2,1,0:T(8,128)S(1)}, u32[]{:S(2)}, u32[]{:S(2)}) collective-permute-start(f32[2,72,128]{2,1,0:T(8,128)S(1)} %pad_maximum_fusion.2), channel_id=1, source_target_pairs={{128,0},{136,8},{144,16},{152,24},{160,32},{168,40},{176,48},{184,... | collective-permute-start | bytes 221192 | tf_op jit(solution)/shard_map/ppermute | solution.py:367
  72.4 3.9 %collective-permute-start.16 = (f32[2,72,128]{2,1,0:T(8,128)S(1)}, f32[2,72,128]{2,1,0:T(8,128)S(1)}, u32[]{:S(2)}, u32[]{:S(2)}) collective-permute-start(f32[2,72,128]{2,1,0:T(8,128)S(1)} %pad_maximum_fusion.2), channel_id=1, source_target_pairs={{64,0},{72,8},{80,16},{88,24},{96,32},{104,40},{112,48},{120,56},{... | collective-permute-start | bytes 221192 | tf_op jit(solution)/shard_map/ppermute | solution.py:367
  76.4 2.5 %collective-permute-start.19 = (f32[4,2,72,128]{3,2,1,0:T(8,128)S(1)}, f32[4,2,72,128]{3,2,1,0:T(8,128)S(1)}, u32[]{:S(2)}, u32[]{:S(2)}) collective-permute-start(f32[4,2,72,128]{3,2,1,0:T(8,128)S(1)} %pad_maximum_fusion.1.mine_ref), channel_id=1, source_target_pairs={{0,1},{1,0},{2,3},{3,2},{4,5},{5,4},{6,7},{7,6},{8,9},{9,8},{10,11... | collective-permute-start | bytes 884744 | tf_op jit(solution)/shard_map/ppermute | solution.py:422
Sparse Core Ops, SparseCore 0:
  9.7 31.8 all-gather.6
  44.7 54.4 all-gather.4
